TPU v7x, 32 devices: a whole 2x2x4 slice. The times are simulated.
32 devices in a mesh: space: 4 (over z), tm: 4 (over y, x), param: 2 (over core).
Axes of the slice: x: 2, y: 2, z: 4, core: 2. Of those that a mesh axis runs over, the one named last changes fastest.
Arguments:
- snapshots: float32 [512, 64, 3072], P('tm', 'param', 'space'), may hold values from -6 to 6
- time_basis: float32 [512, 64], replicated, may hold values from -0.25 to 0.25
Outputs:
- gram_time: float32 [512, 512], P('tm')
- core: float32 [64, 64, 3072], P('tm', 'param', 'space')
- gram_param: float32 [64, 64], P('param')
All inputs are finite; a program needn't handle non-finite values.
Results may differ from a plain program's by a relative error of at most 0.000071.
Values sent between devices are 32-bit elements; how exact they have to be, the bound alone decides.
No kernel may reach another device: no remote copies, remote signals or barrier semaphores. Data moves between devices by JAX's collectives and lax.ppermute only.
A program may use at most 128 MiB of HBM per device.

v0:
```python
import jax
import jax.numpy as jnp
from jax import lax
from jax.sharding import PartitionSpec as P

precise_mode = lax.Precision.HIGHEST


def body(snapshots, time_basis):
    time_local, load_local, point_local = snapshots.shape
    total_points = point_local * lax.axis_size("space")
    all_loads = load_local * lax.axis_size("param")
    rank_all = time_basis.shape[1]
    traded = lax.all_to_all(snapshots, "tm", split_axis=2, concat_axis=0, tiled=True)
    rows_part = lax.psum_scatter(
        jnp.einsum("tps,ups->tu", traded, traded, precision=precise_mode),
        "tm",
        scatter_dimension=0,
        tiled=True,
    )
    gram_time = lax.psum(rows_part, ("space", "param")) / (all_loads * total_points)
    basis_rows = lax.dynamic_slice_in_dim(
        time_basis, lax.axis_index("tm") * time_local, time_local, 0
    )
    core = lax.psum_scatter(
        jnp.einsum("tr,tps->rps", basis_rows, snapshots, precision=precise_mode),
        "tm",
        scatter_dimension=0,
        tiled=True,
    )
    param_part = jnp.einsum(
        "rps,rqs->pq",
        core,
        lax.all_gather(core, "param", axis=1, tiled=True),
        precision=precise_mode,
    )
    gram_param = lax.psum(param_part, ("space", "tm")) / (rank_all * total_points)
    return (gram_time, core, gram_param)


def solution(mesh):
    placed = (P("tm", "param", "space"), P())
    return jax.shard_map(
        body,
        mesh=mesh,
        in_specs=placed,
        out_specs=(P("tm", None), P("tm", "param", "space"), P("param", None)),
        check_vma=False,
    )
```

profile of v0, /device:TPU:0, one launch (start us, length us, event | category | flops | bytes accessed | tf_op | source)
XLA Modules:
  0.0 481.5 jit_solution(1896236236314588488)
XLA Ops:
  7.2 0.0 copy-start
  7.2 0.0 reduce-scatter.3.cloned.1.call-start
  7.2 12.8 %copy.16 = f32[128,32,768]{0,1,2:T(8,128)} copy(f32[128,32,768]{2,1,0:T(8,128)} %param.2) | data formatting | bytes 25165824 | tf_op args[0]
  20.0 143.7 %all_to_all.18 = f32[128,32,768]{0,1,2:T(8,128)S(1)} all-to-all(f32[128,32,768]{0,1,2:T(8,128)} %copy.16), channel_id=1, replica_groups=mesh['space'=4,'tm'=4,'param'=2] {'tm'}, dimensions={2} | all-to-all | bytes 25165824 | tf_op jit(solution)/shard_map/all_to_all | solution.py:14
  163.7 16.7 %copy.18 = f32[4,128,32,192]{1,0,3,2:T(4,128)} copy(f32[4,128,32,192]{1,2,3,0:T(8,128)S(1)} %bitcast.15) | data formatting | bytes 25165824 | tf_op jit(solution)/shard_map/all_to_all | solution.py:14
  180.4 15.1 %all_to_all.16 = f32[512,32,192]{0,2,1:T(8,128)} reshape(f32[4,128,32,192]{1,0,3,2:T(4,128)} %copy.18) | data formatting | bytes 25165824 | tf_op jit(solution)/shard_map/all_to_all | solution.py:14
  195.5 24.5 %convolution_bitcast_fusion = f32[512,512]{1,0:T(8,128)} fusion(f32[512,32,192]{0,2,1:T(8,128)} %all_to_all.16), kind=kOutput, calls=%fused_computation.4 | convolution fusion | flops 19327352832 | bytes 13631488 | tf_op jit(solution)/shard_map/tps,ups->tu/dot_general | solution.py:16
  219.9 0.0 reduce-scatter.3.cloned.1.call-update
  220.0 0.2 reduce-scatter.5.cloned.1.call-start
  220.2 0.0 copy-done
  220.2 20.3 %fusion = f32[64,32,768]{2,0,1:T(8,128)} fusion(f32[128,32,768]{2,1,0:T(8,128)} %param.2, f32[512,64]{0,1:T(8,128)S(1)} %copy-done, s32[]{:T(128)S(6)} %select_n.3), kind=kOutput, calls=%fused_computation | convolution fusion | flops 2415919104 | bytes 18907140 | tf_op jit(solution)/shard_map/tr,tps->rps/dot_general | solution.py:26
  240.6 0.0 reduce-scatter.5.cloned.1.call-update
  240.6 0.0 all-reduce.2.cloned.1.call-start
  240.6 7.1 %reduce-scatter.3.cloned.1.call-done = f32[128,512]{1,0:T(8,128)} async-done(((f32[512,512]{1,0:T(8,128)}), f32[128,512]{1,0:T(8,128)}) %reduce-scatter.3.cloned.1.call-update) | async-done | bytes 262160 | tf_op jit(solution)/shard_map/reduce_scatter | solution.py:15
  247.8 0.0 all-reduce.2.cloned.1.call-update
  247.8 0.3 all-gather.2.cloned.1.call-start
  248.1 73.2 %reduce-scatter.5.cloned.1.call-done = f32[16,32,768]{2,0,1:T(8,128)} async-done(((f32[64,32,768]{2,0,1:T(8,128)}), f32[16,32,768]{2,0,1:T(8,128)}) %reduce-scatter.5.cloned.1.call-update) | async-done | bytes 1572880 | tf_op jit(solution)/shard_map/reduce_scatter | solution.py:25
  321.3 0.0 all-gather.2.cloned.1.call-update
  321.3 57.4 %all-reduce.2.cloned.1.call-done = f32[128,512]{1,0:T(8,128)} async-done(((f32[128,512]{1,0:T(8,128)}), f32[128,512]{1,0:T(8,128)}) %all-reduce.2.cloned.1.call-update) | async-done | bytes 262160 | tf_op jit(solution)/shard_map/psum | solution.py:21
  378.6 1.7 broadcast_multiply_fusion
  380.3 2.3 copy.22
  382.6 0.0 copy-start.1
  382.7 8.5 %all-gather.2.cloned.1.call-done = f32[16,64,768]{2,0,1:T(8,128)} async-done(((f32[16,32,768]{2,0,1:T(8,128)}), f32[16,64,768]{2,0,1:T(8,128)}) %all-gather.2.cloned.1.call-update) | async-done | bytes 3145744 | tf_op jit(solution)/shard_map/all_gather | solution.py:34
  391.2 6.1 %fusion.4 = f32[32,64]{1,0:T(8,128)S(1)} fusion(f32[16,32,768]{2,1,0:T(8,128)S(1)} %copy.22, f32[16,64,768]{2,0,1:T(8,128)} %all-gather.2.cloned.1.call-done), kind=kOutput, calls=%fused_computation.5 | convolution fusion | flops 301989888 | bytes 4726784 | tf_op jit(solution)/shard_map/rps,rqs->pq/dot_general | solution.py:31
  397.3 77.0 %psum.15 = f32[32,64]{1,0:T(8,128)S(1)} all-reduce(f32[32,64]{1,0:T(8,128)S(1)} %fusion.4), channel_id=1, replica_groups=mesh['space'=4,'tm'=4,'param'=2] {'space','tm'}, use_global_device_ids=true, to_apply=%region_3.0 | all-reduce | flops 2048 | bytes 16384 | tf_op jit(solution)/shard_map/psum | solution.py:37
  474.3 0.6 broadcast_multiply_fusion.1
  474.9 0.0 copy-done.1
Async XLA Ops:
  7.2 213.0 %copy-start = (f32[512,64]{0,1:T(8,128)S(1)}, f32[512,64]{0,1:T(8,128)}, u32[]{:S(2)}) copy-start(f32[512,64]{0,1:T(8,128)} %param.3) | copy-start | bytes 393220
  7.2 240.6 %reduce-scatter.3.cloned.1.call-start = ((), (), s32[]{:S(2)}) async-start(), calls=%async_computation.3 | async-start | bytes 1310720 | tf_op jit(solution)/shard_map/reduce_scatter | solution.py:15
  220.0 101.3 %reduce-scatter.5.cloned.1.call-start = ((), (), s32[]{:S(2)}) async-start(), calls=%async_computation.5 | async-start | bytes 7864320 | tf_op jit(solution)/shard_map/reduce_scatter | solution.py:25
  240.6 138.1 %all-reduce.2.cloned.1.call-start = ((), (), s32[]{:S(2)}) async-start(), calls=%async_computation.4 | async-start | bytes 524288 | tf_op jit(solution)/shard_map/psum | solution.py:21
  247.8 143.4 %all-gather.2.cloned.1.call-start = ((), (), s32[]{:S(2)}) async-start(), calls=%async_computation.6 | async-start | bytes 4718592 | tf_op jit(solution)/shard_map/all_gather | solution.py:34
  382.6 92.3 %copy-start.1 = (f32[16,32,768]{2,1,0:T(8,128)}, f32[16,32,768]{2,1,0:T(8,128)S(1)}, u32[]{:S(2)}) copy-start(f32[16,32,768]{2,1,0:T(8,128)S(1)} %copy.22) | copy-start | bytes 4718596
Sparse Core Ops, SparseCore 0:
  220.1 27.6 reduce-scatter.2
  251.0 70.1 reduce-scatter.4
  323.7 54.9 all-reduce.1
  380.0 11.0 all-gather.1
where the time goes:
time: 482 us; the launch traced here: 481 us
  blocking collectives  221 us (46%)
  waiting for transfers between devices  146 us (30%)
  matrix products  50.9 us (11%)
  local copies, waits for them, and re-layouts  46.9 us (10%)
  between operations  13.8 us (3%)
    all_to_all x1, blocking collectives, body(): lax.all_to_all(snapshots, 'tm', split_axis=2, concat_axis=0, tiled=True)  144 us
    psum x1, blocking collectives, body(): lax.psum(param_part, ('space', 'tm')) / (rank_all * total_points)  77 us
    reduce_scatter x1, waiting for transfers between devices, body(): lax.psum_scatter(jnp.einsum('tr,tps->rps', basis_rows, snapshots, precisi...  73.2 us
    psum x1, waiting for transfers between devices, body(): lax.psum(rows_part, ('space', 'param')) / (all_loads * total_points)  57.4 us
    all_to_all x2, local copies, waits for them, and re-layouts, body(): lax.all_to_all(snapshots, 'tm', split_axis=2, concat_axis=0, tiled=True)  31.8 us
    dot_general x1, matrix products, body(): jnp.einsum('tps,ups->tu', traded, traded, precision=precise_mode)  24.5 us
    dot_general x1, matrix products, body(): jnp.einsum('tr,tps->rps', basis_rows, snapshots, precision=precise_mode)  20.3 us
    unnamed x6, local copies, waits for them, and re-layouts  15.2 us
  transfers between devices with their start and end apart: 4, of which 4 were waited for; matrix products, arithmetic and copies ran while one was open for 5% of the time, Pallas kernels for 0%

commit v1 on v0

v1 whole, which is shorter than its diff:
```python
import functools

import jax
import jax.numpy as jnp
from jax import lax
from jax.experimental import pallas as pl
from jax.experimental.pallas import tpu as pltpu
from jax.sharding import PartitionSpec as P

LANES = 128
precise_mode = lax.Precision.HIGHEST


def xor_pairs(k, n):
    return [(i, i ^ k) for i in range(n)]


def swap(v, axis, k):
    return lax.ppermute(v, axis, xor_pairs(k, lax.axis_size(axis)))


def all_sum(v, axis):
    k = 1
    while k < lax.axis_size(axis):
        v = v + swap(v, axis, k)
        k *= 2
    return v


def all_sum_direct(v, axis):
    parts = [swap(v, axis, k) for k in range(1, lax.axis_size(axis))]
    for part in parts:
        v = v + part
    return v


def split(v):
    high = v.astype(jnp.bfloat16)
    return high, (v - high.astype(jnp.float32)).astype(jnp.bfloat16)


def dot_t(a, b):
    return lax.dot_general(
        a, b, (((1,), (1,)), ((), ())), preferred_element_type=jnp.float32
    )


def pack_kernel(n, place, *refs):
    for share, packed in zip(refs[:n], refs[n:]):
        for p in range(share.shape[1]):
            packed[p] = share[:, p, :]


def pack(place, snapshots, chunk, n, cut, group):
    rows = snapshots.shape[0]
    width = cut if chunk[0] == "load" else group
    part = 32 if rows % 32 == 0 else rows

    def spec(k):
        if chunk[0] == "load":
            where = lambda i, place: (i, place[0] ^ k, chunk[1])
        else:
            where = lambda i, place: (i, chunk[2], chunk[1] * n + (place[0] ^ k))
        return pl.BlockSpec((part, width, LANES), where)

    return pl.pallas_call(
        functools.partial(pack_kernel, n),
        out_shape=[jax.ShapeDtypeStruct((width, rows, LANES), jnp.float32)] * n,
        grid_spec=pltpu.PrefetchScalarGridSpec(
            num_scalar_prefetch=1,
            grid=(rows // part,),
            in_specs=[spec(k) for k in range(n)],
            out_specs=[pl.BlockSpec((width, part, LANES), lambda i, place: (0, i, 0))]
            * n,
        ),
        cost_estimate=pl.CostEstimate(
            flops=0, bytes_accessed=8 * n * width * rows * LANES, transcendentals=0
        ),
    )(place, *[snapshots] * n)


def chunk_kernel(n, first, last, pair, place, basis, *refs):
    blocks, refs = refs[:n], refs[n:]
    if not first:
        before, refs = refs[0], refs[1:]
    core, pieces, refs = refs[0], refs[1:n], refs[n:]
    if last:
        keep, send, total, high, low = refs
    else:
        total, high, low = refs
    step = pl.program_id(0)
    steps = high.shape[0]
    me, half = place[0], place[1]
    rows = blocks[0].shape[1]
    rank = core.shape[0]
    for e in range(pair):
        for k in range(n):
            h, l = split(blocks[k][e])
            at = pl.ds(pl.multiple_of((me ^ k) * rows, rows), rows)
            high[step, at, e * LANES : (e + 1) * LANES] = h
            low[step, at, e * LANES : (e + 1) * LANES] = l

    @pl.when(step == steps - 1)
    def _():
        h = jnp.concatenate([high[s] for s in range(steps)], axis=1)
        l = jnp.concatenate([low[s] for s in range(steps)], axis=1)
        product = dot_t(
            jnp.concatenate([h, h, l], axis=1), jnp.concatenate([h, l, h], axis=1)
        )
        if first:
            total[...] = product
        else:
            total[...] = before[...] + product
        if last:
            cut = keep.shape[1]
            for j in range(n):
                mine = pl.multiple_of(j * rows + half * cut, cut)
                other = pl.multiple_of(j * rows + (1 - half) * cut, cut)
                keep[j] = total[pl.ds(mine, cut), :]
                send[j] = total[pl.ds(other, cut), :]
        b = jnp.concatenate(split(basis[...]), axis=0)
        wide = jnp.dot(b, h, preferred_element_type=jnp.float32)
        wide = wide + jnp.dot(b, l, preferred_element_type=jnp.float32)
        values = wide[:rank] + wide[rank:]
        own = rank // n
        for p in range(core.shape[1]):
            part = values[:, p * LANES : (p + 1) * LANES]
            core[:, p, :] = part
            for k in range(1, n):
                pieces[k - 1][:, p, :] = part[k * own : (k + 1) * own]


def run_chunk(place, basis, blocks, before, last):
    n = len(blocks)
    loads, rows, lanes = blocks[0].shape
    steps = n * rows
    rank = basis.shape[0]
    pair = 2 if loads % 2 == 0 else 1
    first = before is None
    whole = lambda *dims: pl.BlockSpec(dims, lambda i, place: (0,) * len(dims))
    in_specs = [whole(*basis.shape)]
    in_specs += [pl.BlockSpec((pair, rows, lanes), lambda i, place: (i, 0, 0))] * n
    args = [place, basis, *blocks]
    if not first:
        in_specs.append(whole(steps, steps))
        args.append(before)
    f32 = lambda *dims: jax.ShapeDtypeStruct(dims, jnp.float32)
    shapes = [f32(rank, loads, lanes)] + [f32(rank // n, loads, lanes)] * (n - 1)
    scratch = [pltpu.VMEM((loads // pair, steps, pair * lanes), jnp.bfloat16)] * 2
    if last:
        shapes += [f32(n, rows // 2, steps)] * 2
        scratch = [pltpu.VMEM((steps, steps), jnp.float32)] + scratch
    else:
        shapes += [f32(steps, steps)]
    points = loads * lanes
    return pl.pallas_call(
        functools.partial(chunk_kernel, n, first, last, pair),
        out_shape=shapes,
        grid_spec=pltpu.PrefetchScalarGridSpec(
            num_scalar_prefetch=1,
            grid=(loads // pair,),
            in_specs=in_specs,
            out_specs=[whole(*s.shape) for s in shapes],
            scratch_shapes=scratch,
        ),
        compiler_params=pltpu.CompilerParams(vmem_limit_bytes=40 * 2**20),
        cost_estimate=pl.CostEstimate(
            flops=2 * steps * points * (3 * steps + 4 * rank),
            bytes_accessed=4 * steps * (points + 2 * steps),
            transcendentals=0,
        ),
    )(*args)


def body(snapshots, time_basis):
    rows, loads, points = snapshots.shape
    n = lax.axis_size("tm")
    me, half = lax.axis_index("tm"), lax.axis_index("param")
    rank = time_basis.shape[1]
    own_rank = rank // n
    total_points = points * lax.axis_size("space")
    total_loads = loads * lax.axis_size("param")
    tiles = points // LANES
    cut = loads // n
    mains = tiles // n
    group = 8 if loads % 8 == 0 else loads

    chunks = [("load", t) for t in range(mains * n, tiles)]
    chunks += [("tile", m, g) for m in range(mains) for g in range(loads // group)]

    place = jnp.stack([me, half]).astype(jnp.int32)
    order = me ^ jnp.arange(n)
    basis = time_basis.reshape(-1, n, own_rank)[:, order].reshape(-1, rank).T

    def shares(x, chunk):
        if (cut if chunk[0] == "load" else group) % 8 == 0:
            return pack(place, x, chunk, n, cut, group)
        out = []
        for k in range(n):
            j = me ^ k
            if chunk[0] == "load":
                start, size = (0, j * cut, chunk[1] * LANES), (rows, cut, LANES)
            else:
                start = (0, chunk[2] * group, (chunk[1] * n + j) * LANES)
                size = (rows, group, LANES)
            out.append(lax.dynamic_slice(x, start, size).transpose(1, 0, 2))
        return out

    held = []
    for i, chunk in enumerate(chunks):
        x = snapshots
        if i >= 2:
            x = lax.optimization_barrier((x, held[i - 2][1:]))[0]
        parts = shares(x, chunk)
        held.append([parts[0]] + [swap(parts[k], "tm", k) for k in range(1, n)])

    total = None
    cores, pieces = [], []
    for i, chunk in enumerate(chunks):
        last = i == len(chunks) - 1
        out = run_chunk(place, basis, held[i], total, last)
        cores.append(out[0])
        pieces.append(out[1:n])
        total = out[n]
        if last:
            keep, send = out[n], out[n + 1]

    rows_part = keep + swap(send, "param", 1)
    pick = lambda v, k: lax.dynamic_index_in_dim(v, me ^ k, 0, False)
    arrived = [swap(pick(rows_part, k), "tm", k) for k in range(1, n)]
    mine = pick(rows_part, 0)
    for part in arrived:
        mine = mine + part
    mine = all_sum(mine, "space") / (total_loads * total_points)
    other = swap(mine, "param", 1)
    gram_time = jnp.where(
        half == 0,
        jnp.concatenate([mine, other]),
        jnp.concatenate([other, mine]),
    )

    core = jnp.zeros((own_rank, loads, points), jnp.float32)
    for i, chunk in enumerate(chunks):
        parts = [cores[i][:own_rank]]
        parts += [swap(pieces[i][k - 1], "tm", k) for k in range(1, n)]
        for k, part in enumerate(parts):
            j = me ^ k
            if chunk[0] == "load":
                at = (0, j * cut, chunk[1] * LANES)
            else:
                at = (0, chunk[2] * group, (chunk[1] * n + j) * LANES)
            core = lax.dynamic_update_slice(core, part, at)

    def load_gram(v):
        far = swap(v, "param", 1)
        both = jnp.where(
            half == 0,
            jnp.concatenate([v, far], axis=1),
            jnp.concatenate([far, v], axis=1),
        )
        return jnp.einsum("rps,rqs->pq", v, both, precision=precise_mode)

    param_part = jnp.zeros((loads, total_loads), jnp.float32)
    if mains * n < tiles:
        param_part = param_part + load_gram(core[:, :, mains * n * LANES :])
    for m in range(mains):
        tile = [c for c, chunk in zip(cores, chunks) if chunk[:2] == ("tile", m)]
        param_part = param_part + load_gram(jnp.concatenate(tile, axis=1))
    param_part = all_sum(all_sum_direct(param_part, "tm"), "space")
    gram_param = param_part / (rank * total_points)
    return (gram_time, core, gram_param)


def solution(mesh):
    placed = (P("tm", "param", "space"), P())
    return jax.shard_map(
        body,
        mesh=mesh,
        in_specs=placed,
        out_specs=(P("tm", None), P("tm", "param", "space"), P("param", None)),
        check_vma=False,
    )
```

time: 482 us -> 215 us (0.45)
  blocking collectives: 221 us -> 0 us
  waiting for transfers between devices: 146 us -> 57.9 us
  starting transfers between devices: 0.56 us -> 66 us
  Pallas kernels: 0 us -> 54.7 us
  matrix products: 50.9 us -> 2.75 us
  local copies, waits for them, and re-layouts: 46.9 us -> 29 us
  between operations: 13.8 us -> 0.98 us
    all_to_all x1 -> x0, blocking collectives: 144 us -> none  [body(): lax.all_to_all(snapshots, 'tm', split_axis=2, concat_axis=0, tiled=True)]
    reduce_scatter x2 -> x0, waiting for transfers between devices: 80.3 us -> none  [the longest x1 73.2 us: body(): lax.psum_scatter(jnp.einsum('tr,tps->rps', basis_rows, snapshots, precisi...]
    psum x1 -> x0, blocking collectives: 77 us -> none  [body(): lax.psum(param_part, ('space', 'tm')) / (rank_all * total_points)]
    ppermute x0 -> x50, starting transfers between devices: none -> 66 us  [swap(): return lax.ppermute(v, axis, xor_pairs(k, lax.axis_size(axis)))]
    ppermute x0 -> x50, waiting for transfers between devices: none -> 57.9 us  [swap(): return lax.ppermute(v, axis, xor_pairs(k, lax.axis_size(axis)))]
    psum x1 -> x0, waiting for transfers between devices: 57.4 us -> none  [body(): lax.psum(rows_part, ('space', 'param')) / (all_loads * total_points)]
    pallas_call x0 -> x12, Pallas kernels: none -> 54.7 us  [the longest x6 30.8 us: pack(): pl.pallas_call(functools.partial(pack_kernel, n), out_shape=[jax.ShapeDty...]
    dot_general x3 -> x2, matrix products: 50.9 us -> 2.75 us  [load_gram(): return jnp.einsum('rps,rqs->pq', v, both, precision=precise_mode)]
  transfers between devices with their start and end apart: 4 -> 50, of which waited for: 4 -> 17; matrix products, arithmetic and copies ran while one was open for 5% -> 12% of each run, Pallas kernels for 0% -> 23%
where the time goes in v1:
time: 215 us; the launch traced here: 214 us
  starting transfers between devices  66 us (31%)
  waiting for transfers between devices  57.9 us (27%)
  Pallas kernels  54.7 us (25%)
  local copies, waits for them, and re-layouts  29 us (13%)
  matrix products  2.75 us (1%)
    ppermute x50, starting transfers between devices, swap(): return lax.ppermute(v, axis, xor_pairs(k, lax.axis_size(axis)))  66 us
    ppermute x50, waiting for transfers between devices, swap(): return lax.ppermute(v, axis, xor_pairs(k, lax.axis_size(axis)))  57.9 us
    pallas_call x6, Pallas kernels, pack(): pl.pallas_call(functools.partial(pack_kernel, n), out_shape=[jax.ShapeDty...  30.8 us
    pallas_call x6, Pallas kernels, run_chunk(): pl.pallas_call(functools.partial(chunk_kernel, n, first, last, pair), out...  23.9 us
    dynamic_update_slice x24, local copies, waits for them, and re-layouts, body(): core = lax.dynamic_update_slice(core, part, at)  17.7 us
    unnamed x52, local copies, waits for them, and re-layouts  8.31 us
  transfers between devices with their start and end apart: 50, of which 17 were waited for; matrix products, arithmetic and copies ran while one was open for 12% of the time, Pallas kernels for 23%

profile of v1, /device:TPU:0, one launch (start us, length us, event | category | flops | bytes accessed | tf_op | source)
XLA Modules:
  0.0 213.6 jit_solution(519578318395929400)
XLA Ops:
  1.2 5.0 %shard_map.52 = (f32[8,128,128]{2,1,0:T(8,128)}, f32[8,128,128]{2,1,0:T(8,128)}, f32[8,128,128]{2,1,0:T(8,128)}, f32[8,128,128]{2,1,0:T(8,128)}) custom-call(s32[2]{0:T(128)} %pad_add_fusion.place, f32[128,32,768]{2,1,0:T(8,128)} %refs_3_.7, f32[128,32,768]{2,1,0:T(8,128)} %refs_3_.7, f32[128,32,768]{2,1,0:T(8,128)} %refs_3_.7, f32[128,32,768]{2,1,0:T(8,128)} %refs_3_.7), custom_call_target="tpu_custom_call" | custom-call | bytes 4194304 | tf_op jit(solution)/shard_map/pallas_call | solution.py:66
  6.3 2.9 %collective-permute-start.9 = (f32[8,128,128]{2,1,0:T(8,128)}, f32[8,128,128]{2,1,0:T(8,128)S(1)}, u32[]{:S(2)}, u32[]{:S(2)}) collective-permute-start(f32[8,128,128]{2,1,0:T(8,128)} %get-tuple-element.74), channel_id=1, source_target_pairs={{0,2},{2,0},{4,6},{6,4},{1,3},{3,1},{5,7},{7,5},{8,10},{10,8},{12,... | collective-permute-start | bytes 1572872 | tf_op jit(solution)/shard_map/ppermute | solution.py:19
  9.2 1.5 collective-permute-start.10
  10.7 5.1 %shard_map.49 = (f32[8,128,128]{2,1,0:T(8,128)}, f32[8,128,128]{2,1,0:T(8,128)}, f32[8,128,128]{2,1,0:T(8,128)}, f32[8,128,128]{2,1,0:T(8,128)}) custom-call(s32[2]{0:T(128)} %pad_add_fusion.place, f32[128,32,768]{2,1,0:T(8,128)} %refs_3_.7, f32[128,32,768]{2,1,0:T(8,128)} %refs_3_.7, f32[128,32,768]{2,1,0:T(8,128)} %refs_3_.7, f32[128,32,768]{2,1,0:T(8,128)} %refs_3_.7), custom_call_target="tpu_custom_call" | custom-call | bytes 4194304 | tf_op jit(solution)/shard_map/pallas_call | solution.py:66
  15.8 2.0 collective-permute-start
  17.9 1.5 collective-permute-start.1
  19.4 2.8 %collective-permute-done.9.refs_1_ = f32[8,128,128]{2,1,0:T(8,128)S(1)} collective-permute-done((f32[8,128,128]{2,1,0:T(8,128)}, f32[8,128,128]{2,1,0:T(8,128)S(1)}, u32[]{:S(2)}, u32[]{:S(2)}) %collective-permute-start.9) | collective-permute-done | bytes 524320 | tf_op jit(solution)/shard_map/ppermute | solution.py:19
  22.2 3.0 %collective-permute-start.2 = (f32[8,128,128]{2,1,0:T(8,128)}, f32[8,128,128]{2,1,0:T(8,128)S(1)}, u32[]{:S(2)}, u32[]{:S(2)}) collective-permute-start(f32[8,128,128]{2,1,0:T(8,128)} %get-tuple-element.64), channel_id=1, source_target_pairs={{0,6},{2,4},{4,2},{6,0},{1,7},{3,5},{5,3},{7,1},{8,14},{10,12},{12... | collective-permute-start | bytes 1572872 | tf_op jit(solution)/shard_map/ppermute | solution.py:19
  25.8 9.7 %collective-permute-done.10.refs_2_ = f32[8,128,128]{2,1,0:T(8,128)S(1)} collective-permute-done((f32[8,128,128]{2,1,0:T(8,128)}, f32[8,128,128]{2,1,0:T(8,128)S(1)}, u32[]{:S(2)}, u32[]{:S(2)}) %collective-permute-start.10) | collective-permute-done | bytes 524320 | tf_op jit(solution)/shard_map/ppermute | solution.py:19
  37.4 4.9 %shard_map.55 = (f32[64,8,128]{2,1,0:T(8,128)S(1)}, f32[16,8,128]{2,1,0:T(8,128)S(1)}, f32[16,8,128]{2,1,0:T(8,128)S(1)}, f32[16,8,128]{2,1,0:T(8,128)S(1)}, f32[512,512]{1,0:T(8,128)S(1)}) custom-call(s32[2]{0:T(128)S(1)} %copy-done.1, f32[64,512]{1,0:T(8,128)S(1)} %bitcast.31, f32[8,128,128]{2,1,0:T(8,128)S(1)} %copy-done.9, ...), custom_call_target="tpu_custom_call" | custom-call | flops 1879048192 | bytes 4194304 | tf_op jit(solution)/shard_map/pallas_call | solution.py:156
  43.5 1.8 collective-permute-start.26
  45.3 5.1 %shard_map.53 = (f32[8,128,128]{2,1,0:T(8,128)}, f32[8,128,128]{2,1,0:T(8,128)}, f32[8,128,128]{2,1,0:T(8,128)}, f32[8,128,128]{2,1,0:T(8,128)}) custom-call(s32[2]{0:T(128)} %pad_add_fusion.place, f32[128,32,768]{2,1,0:T(8,128)} %refs_3_.7, f32[128,32,768]{2,1,0:T(8,128)} %refs_3_.7, f32[128,32,768]{2,1,0:T(8,128)} %refs_3_.7, f32[128,32,768]{2,1,0:T(8,128)} %refs_3_.7), custom_call_target="tpu_custom_call" | custom-call | bytes 4194304 | tf_op jit(solution)/shard_map/pallas_call | solution.py:66
  53.8 4.5 %collective-permute-done.1.refs_2_ = f32[8,128,128]{2,1,0:T(8,128)S(1)} collective-permute-done((f32[8,128,128]{2,1,0:T(8,128)}, f32[8,128,128]{2,1,0:T(8,128)S(1)}, u32[]{:S(2)}, u32[]{:S(2)}) %collective-permute-start.1) | collective-permute-done | bytes 524320 | tf_op jit(solution)/shard_map/ppermute | solution.py:19
  58.3 2.5 %collective-permute-start.13 = (f32[8,128,128]{2,1,0:T(8,128)}, f32[8,128,128]{2,1,0:T(8,128)S(1)}, u32[]{:S(2)}, u32[]{:S(2)}) collective-permute-start(f32[8,128,128]{2,1,0:T(8,128)} %get-tuple-element.79), channel_id=1, source_target_pairs={{0,4},{2,6},{4,0},{6,2},{1,5},{3,7},{5,1},{7,3},{8,12},{10,14},{12... | collective-permute-start | bytes 1572872 | tf_op jit(solution)/shard_map/ppermute | solution.py:19
  60.8 3.2 %shard_map.56 = (f32[64,8,128]{2,1,0:T(8,128)S(1)}, f32[16,8,128]{2,1,0:T(8,128)S(1)}, f32[16,8,128]{2,1,0:T(8,128)S(1)}, f32[16,8,128]{2,1,0:T(8,128)S(1)}, f32[512,512]{1,0:T(8,128)S(1)}) custom-call(s32[2]{0:T(128)S(1)} %copy-done.2, f32[64,512]{1,0:T(8,128)S(1)} %bitcast.32, f32[8,128,128]{2,1,0:T(8,128)S(1)} %copy-done.5, ...), custom_call_target="tpu_custom_call" | custom-call | flops 1879048192 | bytes 4194304 | tf_op jit(solution)/shard_map/pallas_call | solution.py:156
  65.0 5.2 %shard_map.50 = (f32[8,128,128]{2,1,0:T(8,128)}, f32[8,128,128]{2,1,0:T(8,128)}, f32[8,128,128]{2,1,0:T(8,128)}, f32[8,128,128]{2,1,0:T(8,128)}) custom-call(s32[2]{0:T(128)} %pad_add_fusion.place, f32[128,32,768]{2,1,0:T(8,128)} %refs_3_.7, f32[128,32,768]{2,1,0:T(8,128)} %refs_3_.7, f32[128,32,768]{2,1,0:T(8,128)} %refs_3_.7, f32[128,32,768]{2,1,0:T(8,128)} %refs_3_.7), custom_call_target="tpu_custom_call" | custom-call | bytes 4194304 | tf_op jit(solution)/shard_map/pallas_call | solution.py:66
  70.2 1.5 collective-permute-start.14
  78.9 3.4 %collective-permute-done.28 = f32[16,8,128]{2,1,0:T(8,128)S(1)} collective-permute-done((f32[16,8,128]{2,1,0:T(8,128)S(1)}, f32[16,8,128]{2,1,0:T(8,128)S(1)}, u32[]{:S(2)}, u32[]{:S(2)}) %collective-permute-start.28) | collective-permute-done | bytes 65568 | tf_op jit(solution)/shard_map/ppermute | solution.py:19
  82.3 3.0 %collective-permute-start.30 = (f32[16,8,128]{2,1,0:T(8,128)S(1)}, f32[16,8,128]{2,1,0:T(8,128)S(1)}, u32[]{:S(2)}, u32[]{:S(2)}) collective-permute-start(f32[16,8,128]{2,1,0:T(8,128)S(1)} %get-tuple-element.104), channel_id=1, source_target_pairs={{0,6},{2,4},{4,2},{6,0},{1,7},{3,5},{5,3},{7,1},{8,14},{10,12},{12... | collective-permute-start | bytes 196616 | tf_op jit(solution)/shard_map/ppermute | solution.py:19
  86.4 1.8 collective-permute-done.30
  88.2 2.0 collective-permute-start.4
  92.9 5.2 %shard_map.54 = (f32[8,128,128]{2,1,0:T(8,128)}, f32[8,128,128]{2,1,0:T(8,128)}, f32[8,128,128]{2,1,0:T(8,128)}, f32[8,128,128]{2,1,0:T(8,128)}) custom-call(s32[2]{0:T(128)} %pad_add_fusion.place, f32[128,32,768]{2,1,0:T(8,128)} %refs_3_.7, f32[128,32,768]{2,1,0:T(8,128)} %refs_3_.7, f32[128,32,768]{2,1,0:T(8,128)} %refs_3_.7, f32[128,32,768]{2,1,0:T(8,128)} %refs_3_.7), custom_call_target="tpu_custom_call" | custom-call | bytes 4194304 | tf_op jit(solution)/shard_map/pallas_call | solution.py:66
  98.4 2.0 collective-permute-start.16
  102.6 3.8 %shard_map.57 = (f32[64,8,128]{2,1,0:T(8,128)S(1)}, f32[16,8,128]{2,1,0:T(8,128)}, f32[16,8,128]{2,1,0:T(8,128)S(1)}, f32[16,8,128]{2,1,0:T(8,128)S(1)}, f32[512,512]{1,0:T(8,128)S(1)}) custom-call(s32[2]{0:T(128)S(1)} %copy-done.3, f32[64,512]{1,0:T(8,128)S(1)} %bitcast.33, f32[8,128,128]{2,1,0:T(8,128)S(1)} %copy-done.7, ...), custom_call_target="tpu_custom_call" | custom-call | flops 1879048192 | bytes 4194304 | tf_op jit(solution)/shard_map/pallas_call | solution.py:156
  107.1 1.5 collective-permute-start.31
  108.6 3.1 %collective-permute-done.4.refs_2_ = f32[8,128,128]{2,1,0:T(8,128)} collective-permute-done((f32[8,128,128]{2,1,0:T(8,128)}, f32[8,128,128]{2,1,0:T(8,128)}, u32[]{:S(2)}, u32[]{:S(2)}) %collective-permute-start.4) | collective-permute-done | bytes 524320 | tf_op jit(solution)/shard_map/ppermute | solution.py:19
  111.7 2.4 %collective-permute-start.32 = (f32[16,8,128]{2,1,0:T(8,128)S(1)}, f32[16,8,128]{2,1,0:T(8,128)S(1)}, u32[]{:S(2)}, u32[]{:S(2)}) collective-permute-start(f32[16,8,128]{2,1,0:T(8,128)S(1)} %get-tuple-element.107), channel_id=1, source_target_pairs={{0,4},{2,6},{4,0},{6,2},{1,5},{3,7},{5,1},{7,3},{8,12},{10,14},{12... | collective-permute-start | bytes 196616 | tf_op jit(solution)/shard_map/ppermute | solution.py:19
  114.1 1.5 collective-permute-start.33
  115.7 5.3 %shard_map.58 = (f32[64,8,128]{2,1,0:T(8,128)S(1)}, f32[16,8,128]{2,1,0:T(8,128)S(1)}, f32[16,8,128]{2,1,0:T(8,128)S(1)}, f32[16,8,128]{2,1,0:T(8,128)S(1)}, f32[512,512]{1,0:T(8,128)S(1)}) custom-call(s32[2]{0:T(128)S(1)} %copy-done.3, f32[64,512]{1,0:T(8,128)S(1)} %bitcast.34, f32[8,128,128]{2,1,0:T(8,128)S(1)} %copy-done.8, ...), custom_call_target="tpu_custom_call" | custom-call | flops 1879048192 | bytes 4194304 | tf_op jit(solution)/shard_map/pallas_call | solution.py:156
  121.8 5.1 %shard_map.51 = (f32[8,128,128]{2,1,0:T(8,128)}, f32[8,128,128]{2,1,0:T(8,128)}, f32[8,128,128]{2,1,0:T(8,128)}, f32[8,128,128]{2,1,0:T(8,128)}) custom-call(s32[2]{0:T(128)} %pad_add_fusion.place, f32[128,32,768]{2,1,0:T(8,128)} %refs_3_.7, f32[128,32,768]{2,1,0:T(8,128)} %refs_3_.7, f32[128,32,768]{2,1,0:T(8,128)} %refs_3_.7, f32[128,32,768]{2,1,0:T(8,128)} %refs_3_.7), custom_call_target="tpu_custom_call" | custom-call | bytes 4194304 | tf_op jit(solution)/shard_map/pallas_call | solution.py:66
  134.7 2.2 %collective-permute-done.35 = f32[16,8,128]{2,1,0:T(8,128)S(1)} collective-permute-done((f32[16,8,128]{2,1,0:T(8,128)S(1)}, f32[16,8,128]{2,1,0:T(8,128)S(1)}, u32[]{:S(2)}, u32[]{:S(2)}) %collective-permute-start.35) | collective-permute-done | bytes 65568 | tf_op jit(solution)/shard_map/ppermute | solution.py:19
  137.5 2.3 %collective-permute-start.7 = (f32[8,128,128]{2,1,0:T(8,128)}, f32[8,128,128]{2,1,0:T(8,128)S(1)}, u32[]{:S(2)}, u32[]{:S(2)}) collective-permute-start(f32[8,128,128]{2,1,0:T(8,128)} %get-tuple-element.72), channel_id=1, source_target_pairs={{0,4},{2,6},{4,0},{6,2},{1,5},{3,7},{5,1},{7,3},{8,12},{10,14},{12... | collective-permute-start | bytes 1572872 | tf_op jit(solution)/shard_map/ppermute | solution.py:19
  143.4 6.0 %collective-permute-done.17.refs_3_ = f32[8,128,128]{2,1,0:T(8,128)S(1)} collective-permute-done((f32[8,128,128]{2,1,0:T(8,128)}, f32[8,128,128]{2,1,0:T(8,128)S(1)}, u32[]{:S(2)}, u32[]{:S(2)}) %collective-permute-start.17) | collective-permute-done | bytes 524320 | tf_op jit(solution)/shard_map/ppermute | solution.py:19
  149.4 3.4 %shard_map.59 = (f32[64,8,128]{2,1,0:T(8,128)S(1)}, f32[16,8,128]{2,1,0:T(8,128)S(1)}, f32[16,8,128]{2,1,0:T(8,128)S(1)}, f32[16,8,128]{2,1,0:T(8,128)S(1)}, f32[512,512]{1,0:T(8,128)S(1)}) custom-call(s32[2]{0:T(128)S(1)} %copy-done.4, f32[64,512]{1,0:T(8,128)S(1)} %bitcast.35, f32[8,128,128]{2,1,0:T(8,128)S(1)} %copy-done.6, ...), custom_call_target="tpu_custom_call" | custom-call | flops 1879048192 | bytes 4194304 | tf_op jit(solution)/shard_map/pallas_call | solution.py:156
  154.9 5.5 %collective-permute-done.6.refs_1_ = f32[8,128,128]{2,1,0:T(8,128)S(1)} collective-permute-done((f32[8,128,128]{2,1,0:T(8,128)}, f32[8,128,128]{2,1,0:T(8,128)S(1)}, u32[]{:S(2)}, u32[]{:S(2)}) %collective-permute-start.6) | collective-permute-done | bytes 524320 | tf_op jit(solution)/shard_map/ppermute | solution.py:19
  160.8 5.8 %collective-permute-done.8.refs_3_ = f32[8,128,128]{2,1,0:T(8,128)S(1)} collective-permute-done((f32[8,128,128]{2,1,0:T(8,128)}, f32[8,128,128]{2,1,0:T(8,128)S(1)}, u32[]{:S(2)}, u32[]{:S(2)}) %collective-permute-start.8) | collective-permute-done | bytes 524320 | tf_op jit(solution)/shard_map/ppermute | solution.py:19
  166.5 3.3 %shard_map.60 = (f32[64,8,128]{2,1,0:T(8,128)S(1)}, f32[16,8,128]{2,1,0:T(8,128)S(1)}, f32[16,8,128]{2,1,0:T(8,128)S(1)}, f32[16,8,128]{2,1,0:T(8,128)S(1)}, f32...) custom-call(s32[2]{0:T(128)S(1)} %copy-done.4, f32[64,512]{1,0:T(8,128)S(1)} %bitcast.36, ...), custom_call_target="tpu_custom_call" | custom-call | flops 1879048192 | bytes 4194304 | tf_op jit(solution)/shard_map/pallas_call | solution.py:156
  173.9 1.5 collective-permute-start.19
  180.1 2.8 %collective-permute-start.42 = (f32[16,8,128]{2,1,0:T(8,128)S(1)}, f32[16,8,128]{2,1,0:T(8,128)S(1)}, u32[]{:S(2)}, u32[]{:S(2)}) collective-permute-start(f32[16,8,128]{2,1,0:T(8,128)S(1)} %get-tuple-element.120), channel_id=1, source_target_pairs={{0,6},{2,4},{4,2},{6,0},{1,7},{3,5},{5,3},{7,1},{8,14},{10,12},{12... | collective-permute-start | bytes 196616 | tf_op jit(solution)/shard_map/ppermute | solution.py:19
  183.6 3.1 %collective-permute-done.20 = f32[64,512]{1,0:T(8,128)S(1)} collective-permute-done((f32[64,512]{1,0:T(8,128)S(1)}, f32[64,512]{1,0:T(8,128)S(1)}, u32[]{:S(2)}, u32[]{:S(2)}) %collective-permute-start.20) | collective-permute-done | bytes 131104 | tf_op jit(solution)/shard_map/ppermute | solution.py:19
  186.8 2.0 collective-permute-start.22
  191.8 3.0 %collective-permute-start.23 = (f32[64,512]{1,0:T(8,128)S(1)}, f32[64,512]{1,0:T(8,128)S(1)}, u32[]{:S(2)}, u32[]{:S(2)}) collective-permute-start(f32[64,512]{1,0:T(8,128)S(1)} %add.108), channel_id=1, source_target_pairs={{0,16},{8,24},{16,0},{24,8},{1,17},{9,25},{17,1},{25,9},{2,18},{10... | collective-permute-start | bytes 393224 | tf_op jit(solution)/shard_map/ppermute | solution.py:19
  195.2 1.8 fusion.3
  198.4 2.4 %collective-permute-start.46 = (f32[32,64]{1,0:T(8,128)S(1)}, f32[32,64]{1,0:T(8,128)S(1)}, u32[]{:S(2)}, u32[]{:S(2)}) collective-permute-start(f32[32,64]{1,0:T(8,128)S(1)} %fusion.2), channel_id=1, source_target_pairs={{0,4},{2,6},{4,0},{6,2},{1,5},{3,7},{5,1},{7,3},{8,12},{10,14},{12... | collective-permute-start | bytes 24584 | tf_op jit(solution)/shard_map/ppermute | solution.py:19
  202.7 1.8 collective-permute-done.45
  204.6 1.6 collective-permute-start.48
  206.2 2.2 %collective-permute-done.48 = f32[32,64]{1,0:T(8,128)S(1)} collective-permute-done((f32[32,64]{1,0:T(8,128)S(1)}, f32[32,64]{1,0:T(8,128)S(1)}, u32[]{:S(2)}, u32[]{:S(2)}) %collective-permute-start.48) | collective-permute-done | bytes 8224 | tf_op jit(solution)/shard_map/ppermute | solution.py:19
  209.4 3.6 %collective-permute-done.49 = f32[32,64]{1,0:T(8,128)S(1)} collective-permute-done((f32[32,64]{1,0:T(8,128)S(1)}, f32[32,64]{1,0:T(8,128)S(1)}, u32[]{:S(2)}, u32[]{:S(2)}) %collective-permute-start.49) | collective-permute-done | bytes 8224 | tf_op jit(solution)/shard_map/ppermute | solution.py:19
  (158 shorter events, 55.8 us)
Async XLA Ops:
  6.3 15.9 %collective-permute-start.9 = (f32[8,128,128]{2,1,0:T(8,128)}, f32[8,128,128]{2,1,0:T(8,128)S(1)}, u32[]{:S(2)}, u32[]{:S(2)}) collective-permute-start(f32[8,128,128]{2,1,0:T(8,128)} %get-tuple-element.74), channel_id=1, source_target_pairs={{0,2},{2,0},{4,6},{6,4},{1,3},{3,1},{5,7},{7,5},{8,10},{10,8},{12,... | collective-permute-start | bytes 1572872 | tf_op jit(solution)/shard_map/ppermute | solution.py:19
  9.2 26.3 %collective-permute-start.10 = (f32[8,128,128]{2,1,0:T(8,128)}, f32[8,128,128]{2,1,0:T(8,128)S(1)}, u32[]{:S(2)}, u32[]{:S(2)}) collective-permute-start(f32[8,128,128]{2,1,0:T(8,128)} %get-tuple-element.75), channel_id=1, source_target_pairs={{0,4},{2,6},{4,0},{6,2},{1,5},{3,7},{5,1},{7,3},{8,12},{10,14},{12... | collective-permute-start | bytes 1572872 | tf_op jit(solution)/shard_map/ppermute | solution.py:19
  10.7 25.6 %collective-permute-start.11 = (f32[8,128,128]{2,1,0:T(8,128)}, f32[8,128,128]{2,1,0:T(8,128)}, u32[]{:S(2)}, u32[]{:S(2)}) collective-permute-start(f32[8,128,128]{2,1,0:T(8,128)} %get-tuple-element.76), channel_id=1, source_target_pairs={{0,6},{2,4},{4,2},{6,0},{1,7},{3,5},{5,3},{7,1},{8,14},{10,12},{12... | collective-permute-start | bytes 1572872 | tf_op jit(solution)/shard_map/ppermute | solution.py:19
  15.8 36.5 %collective-permute-start = (f32[8,128,128]{2,1,0:T(8,128)}, f32[8,128,128]{2,1,0:T(8,128)S(1)}, u32[]{:S(2)}, u32[]{:S(2)}) collective-permute-start(f32[8,128,128]{2,1,0:T(8,128)} %get-tuple-element.62), channel_id=1, source_target_pairs={{0,2},{2,0},{4,6},{6,4},{1,3},{3,1},{5,7},{7,5},{8,10},{10,8},{12,... | collective-permute-start | bytes 1572872 | tf_op jit(solution)/shard_map/ppermute | solution.py:19
  17.9 40.4 %collective-permute-start.1 = (f32[8,128,128]{2,1,0:T(8,128)}, f32[8,128,128]{2,1,0:T(8,128)S(1)}, u32[]{:S(2)}, u32[]{:S(2)}) collective-permute-start(f32[8,128,128]{2,1,0:T(8,128)} %get-tuple-element.63), channel_id=1, source_target_pairs={{0,4},{2,6},{4,0},{6,2},{1,5},{3,7},{5,1},{7,3},{8,12},{10,14},{12... | collective-permute-start | bytes 1572872 | tf_op jit(solution)/shard_map/ppermute | solution.py:19
  22.2 36.1 %collective-permute-start.2 = (f32[8,128,128]{2,1,0:T(8,128)}, f32[8,128,128]{2,1,0:T(8,128)S(1)}, u32[]{:S(2)}, u32[]{:S(2)}) collective-permute-start(f32[8,128,128]{2,1,0:T(8,128)} %get-tuple-element.64), channel_id=1, source_target_pairs={{0,6},{2,4},{4,2},{6,0},{1,7},{3,5},{5,3},{7,1},{8,14},{10,12},{12... | collective-permute-start | bytes 1572872 | tf_op jit(solution)/shard_map/ppermute | solution.py:19
  43.2 27.0 %collective-permute-start.25 = (f32[16,8,128]{2,1,0:T(8,128)S(1)}, f32[16,8,128]{2,1,0:T(8,128)}, u32[]{:S(2)}, u32[]{:S(2)}) collective-permute-start(f32[16,8,128]{2,1,0:T(8,128)S(1)} %get-tuple-element.98), channel_id=1, source_target_pairs={{0,2},{2,0},{4,6},{6,4},{1,3},{3,1},{5,7},{7,5},{8,10},{10,8},{12,... | collective-permute-start | bytes 196616 | tf_op jit(solution)/shard_map/ppermute | solution.py:19
  43.5 29.8 %collective-permute-start.26 = (f32[16,8,128]{2,1,0:T(8,128)S(1)}, f32[16,8,128]{2,1,0:T(8,128)}, u32[]{:S(2)}, u32[]{:S(2)}) collective-permute-start(f32[16,8,128]{2,1,0:T(8,128)S(1)} %get-tuple-element.99), channel_id=1, source_target_pairs={{0,4},{2,6},{4,0},{6,2},{1,5},{3,7},{5,1},{7,3},{8,12},{10,14},{12... | collective-permute-start | bytes 196616 | tf_op jit(solution)/shard_map/ppermute | solution.py:19
  52.3 23.0 %collective-permute-start.27 = (f32[16,8,128]{2,1,0:T(8,128)S(1)}, f32[16,8,128]{2,1,0:T(8,128)}, u32[]{:S(2)}, u32[]{:S(2)}) collective-permute-start(f32[16,8,128]{2,1,0:T(8,128)S(1)} %get-tuple-element.100), channel_id=1, source_target_pairs={{0,6},{2,4},{4,2},{6,0},{1,7},{3,5},{5,3},{7,1},{8,14},{10,12},{12... | collective-permute-start | bytes 196616 | tf_op jit(solution)/shard_map/ppermute | solution.py:19
  58.3 31.9 %collective-permute-start.12 = (f32[8,128,128]{2,1,0:T(8,128)}, f32[8,128,128]{2,1,0:T(8,128)S(1)}, u32[]{:S(2)}, u32[]{:S(2)}) collective-permute-start(f32[8,128,128]{2,1,0:T(8,128)} %get-tuple-element.78), channel_id=1, source_target_pairs={{0,2},{2,0},{4,6},{6,4},{1,3},{3,1},{5,7},{7,5},{8,10},{10,8},{12,... | collective-permute-start | bytes 1572872 | tf_op jit(solution)/shard_map/ppermute | solution.py:19
  58.3 34.6 %collective-permute-start.13 = (f32[8,128,128]{2,1,0:T(8,128)}, f32[8,128,128]{2,1,0:T(8,128)S(1)}, u32[]{:S(2)}, u32[]{:S(2)}) collective-permute-start(f32[8,128,128]{2,1,0:T(8,128)} %get-tuple-element.79), channel_id=1, source_target_pairs={{0,4},{2,6},{4,0},{6,2},{1,5},{3,7},{5,1},{7,3},{8,12},{10,14},{12... | collective-permute-start | bytes 1572872 | tf_op jit(solution)/shard_map/ppermute | solution.py:19
  70.2 22.7 %collective-permute-start.14 = (f32[8,128,128]{2,1,0:T(8,128)S(1)}, f32[8,128,128]{2,1,0:T(8,128)S(1)}, u32[]{:S(2)}, u32[]{:S(2)}) collective-permute-start(f32[8,128,128]{2,1,0:T(8,128)S(1)} %copy-done.21), channel_id=1, source_target_pairs={{0,6},{2,4},{4,2},{6,0},{1,7},{3,5},{5,3},{7,1},{8,14},{10,12},{12... | collective-permute-start | bytes 1572872 | tf_op jit(solution)/shard_map/ppermute | solution.py:19
  73.3 9.0 %collective-permute-start.28 = (f32[16,8,128]{2,1,0:T(8,128)S(1)}, f32[16,8,128]{2,1,0:T(8,128)S(1)}, u32[]{:S(2)}, u32[]{:S(2)}) collective-permute-start(f32[16,8,128]{2,1,0:T(8,128)S(1)} %get-tuple-element.102), channel_id=1, source_target_pairs={{0,2},{2,0},{4,6},{6,4},{1,3},{3,1},{5,7},{7,5},{8,10},{10,8},{12,... | collective-permute-start | bytes 196616 | tf_op jit(solution)/shard_map/ppermute | solution.py:19
  75.3 10.6 %collective-permute-start.29 = (f32[16,8,128]{2,1,0:T(8,128)S(1)}, f32[16,8,128]{2,1,0:T(8,128)S(1)}, u32[]{:S(2)}, u32[]{:S(2)}) collective-permute-start(f32[16,8,128]{2,1,0:T(8,128)S(1)} %get-tuple-element.103), channel_id=1, source_target_pairs={{0,4},{2,6},{4,0},{6,2},{1,5},{3,7},{5,1},{7,3},{8,12},{10,14},{12... | collective-permute-start | bytes 196616 | tf_op jit(solution)/shard_map/ppermute | solution.py:19
  82.3 5.9 %collective-permute-start.30 = (f32[16,8,128]{2,1,0:T(8,128)S(1)}, f32[16,8,128]{2,1,0:T(8,128)S(1)}, u32[]{:S(2)}, u32[]{:S(2)}) collective-permute-start(f32[16,8,128]{2,1,0:T(8,128)S(1)} %get-tuple-element.104), channel_id=1, source_target_pairs={{0,6},{2,4},{4,2},{6,0},{1,7},{3,5},{5,3},{7,1},{8,14},{10,12},{12... | collective-permute-start | bytes 196616 | tf_op jit(solution)/shard_map/ppermute | solution.py:19
  85.9 21.2 %collective-permute-start.3 = (f32[8,128,128]{2,1,0:T(8,128)}, f32[8,128,128]{2,1,0:T(8,128)}, u32[]{:S(2)}, u32[]{:S(2)}) collective-permute-start(f32[8,128,128]{2,1,0:T(8,128)} %get-tuple-element.66), channel_id=1, source_target_pairs={{0,2},{2,0},{4,6},{6,4},{1,3},{3,1},{5,7},{7,5},{8,10},{10,8},{12,... | collective-permute-start | bytes 1572872 | tf_op jit(solution)/shard_map/ppermute | solution.py:19
  88.2 23.5 %collective-permute-start.4 = (f32[8,128,128]{2,1,0:T(8,128)}, f32[8,128,128]{2,1,0:T(8,128)}, u32[]{:S(2)}, u32[]{:S(2)}) collective-permute-start(f32[8,128,128]{2,1,0:T(8,128)} %get-tuple-element.67), channel_id=1, source_target_pairs={{0,4},{2,6},{4,0},{6,2},{1,5},{3,7},{5,1},{7,3},{8,12},{10,14},{12... | collective-permute-start | bytes 1572872 | tf_op jit(solution)/shard_map/ppermute | solution.py:19
  90.2 23.9 %collective-permute-start.5 = (f32[8,128,128]{2,1,0:T(8,128)}, f32[8,128,128]{2,1,0:T(8,128)}, u32[]{:S(2)}, u32[]{:S(2)}) collective-permute-start(f32[8,128,128]{2,1,0:T(8,128)} %get-tuple-element.68), channel_id=1, source_target_pairs={{0,6},{2,4},{4,2},{6,0},{1,7},{3,5},{5,3},{7,1},{8,14},{10,12},{12... | collective-permute-start | bytes 1572872 | tf_op jit(solution)/shard_map/ppermute | solution.py:19
  98.2 41.6 %collective-permute-start.15 = (f32[8,128,128]{2,1,0:T(8,128)}, f32[8,128,128]{2,1,0:T(8,128)S(1)}, u32[]{:S(2)}, u32[]{:S(2)}) collective-permute-start(f32[8,128,128]{2,1,0:T(8,128)} %get-tuple-element.83), channel_id=1, source_target_pairs={{0,2},{2,0},{4,6},{6,4},{1,3},{3,1},{5,7},{7,5},{8,10},{10,8},{12,... | collective-permute-start | bytes 1572872 | tf_op jit(solution)/shard_map/ppermute | solution.py:19
  98.4 45.0 %collective-permute-start.16 = (f32[8,128,128]{2,1,0:T(8,128)}, f32[8,128,128]{2,1,0:T(8,128)S(1)}, u32[]{:S(2)}, u32[]{:S(2)}) collective-permute-start(f32[8,128,128]{2,1,0:T(8,128)} %get-tuple-element.84), channel_id=1, source_target_pairs={{0,4},{2,6},{4,0},{6,2},{1,5},{3,7},{5,1},{7,3},{8,12},{10,14},{12... | collective-permute-start | bytes 1572872 | tf_op jit(solution)/shard_map/ppermute | solution.py:19
  107.1 20.8 %collective-permute-start.31 = (f32[16,8,128]{2,1,0:T(8,128)}, f32[16,8,128]{2,1,0:T(8,128)S(1)}, u32[]{:S(2)}, u32[]{:S(2)}) collective-permute-start(f32[16,8,128]{2,1,0:T(8,128)} %get-tuple-element.106), channel_id=1, source_target_pairs={{0,2},{2,0},{4,6},{6,4},{1,3},{3,1},{5,7},{7,5},{8,10},{10,8},{12,... | collective-permute-start | bytes 196616 | tf_op jit(solution)/shard_map/ppermute | solution.py:19
  111.7 17.3 %collective-permute-start.32 = (f32[16,8,128]{2,1,0:T(8,128)S(1)}, f32[16,8,128]{2,1,0:T(8,128)S(1)}, u32[]{:S(2)}, u32[]{:S(2)}) collective-permute-start(f32[16,8,128]{2,1,0:T(8,128)S(1)} %get-tuple-element.107), channel_id=1, source_target_pairs={{0,4},{2,6},{4,0},{6,2},{1,5},{3,7},{5,1},{7,3},{8,12},{10,14},{12... | collective-permute-start | bytes 196616 | tf_op jit(solution)/shard_map/ppermute | solution.py:19
  114.1 17.1 %collective-permute-start.33 = (f32[16,8,128]{2,1,0:T(8,128)S(1)}, f32[16,8,128]{2,1,0:T(8,128)S(1)}, u32[]{:S(2)}, u32[]{:S(2)}) collective-permute-start(f32[16,8,128]{2,1,0:T(8,128)S(1)} %get-tuple-element.108), channel_id=1, source_target_pairs={{0,6},{2,4},{4,2},{6,0},{1,7},{3,5},{5,3},{7,1},{8,14},{10,12},{12... | collective-permute-start | bytes 196616 | tf_op jit(solution)/shard_map/ppermute | solution.py:19
  127.9 5.4 %collective-permute-start.34 = (f32[16,8,128]{2,1,0:T(8,128)S(1)}, f32[16,8,128]{2,1,0:T(8,128)S(1)}, u32[]{:S(2)}, u32[]{:S(2)}) collective-permute-start(f32[16,8,128]{2,1,0:T(8,128)S(1)} %get-tuple-element.110), channel_id=1, source_target_pairs={{0,2},{2,0},{4,6},{6,4},{1,3},{3,1},{5,7},{7,5},{8,10},{10,8},{12,... | collective-permute-start | bytes 196616 | tf_op jit(solution)/shard_map/ppermute | solution.py:19
  129.1 7.8 %collective-permute-start.35 = (f32[16,8,128]{2,1,0:T(8,128)S(1)}, f32[16,8,128]{2,1,0:T(8,128)S(1)}, u32[]{:S(2)}, u32[]{:S(2)}) collective-permute-start(f32[16,8,128]{2,1,0:T(8,128)S(1)} %get-tuple-element.111), channel_id=1, source_target_pairs={{0,4},{2,6},{4,0},{6,2},{1,5},{3,7},{5,1},{7,3},{8,12},{10,14},{12... | collective-permute-start | bytes 196616 | tf_op jit(solution)/shard_map/ppermute | solution.py:19
  131.2 6.3 %collective-permute-start.36 = (f32[16,8,128]{2,1,0:T(8,128)S(1)}, f32[16,8,128]{2,1,0:T(8,128)S(1)}, u32[]{:S(2)}, u32[]{:S(2)}) collective-permute-start(f32[16,8,128]{2,1,0:T(8,128)S(1)} %get-tuple-element.112), channel_id=1, source_target_pairs={{0,6},{2,4},{4,2},{6,0},{1,7},{3,5},{5,3},{7,1},{8,14},{10,12},{12... | collective-permute-start | bytes 196616 | tf_op jit(solution)/shard_map/ppermute | solution.py:19
  133.3 16.1 %collective-permute-start.17 = (f32[8,128,128]{2,1,0:T(8,128)}, f32[8,128,128]{2,1,0:T(8,128)S(1)}, u32[]{:S(2)}, u32[]{:S(2)}) collective-permute-start(f32[8,128,128]{2,1,0:T(8,128)} %get-tuple-element.85), channel_id=1, source_target_pairs={{0,6},{2,4},{4,2},{6,0},{1,7},{3,5},{5,3},{7,1},{8,14},{10,12},{12... | collective-permute-start | bytes 1572872 | tf_op jit(solution)/shard_map/ppermute | solution.py:19
  136.9 23.5 %collective-permute-start.6 = (f32[8,128,128]{2,1,0:T(8,128)}, f32[8,128,128]{2,1,0:T(8,128)S(1)}, u32[]{:S(2)}, u32[]{:S(2)}) collective-permute-start(f32[8,128,128]{2,1,0:T(8,128)} %get-tuple-element.71), channel_id=1, source_target_pairs={{0,2},{2,0},{4,6},{6,4},{1,3},{3,1},{5,7},{7,5},{8,10},{10,8},{12,... | collective-permute-start | bytes 1572872 | tf_op jit(solution)/shard_map/ppermute | solution.py:19
  137.5 23.3 %collective-permute-start.7 = (f32[8,128,128]{2,1,0:T(8,128)}, f32[8,128,128]{2,1,0:T(8,128)S(1)}, u32[]{:S(2)}, u32[]{:S(2)}) collective-permute-start(f32[8,128,128]{2,1,0:T(8,128)} %get-tuple-element.72), channel_id=1, source_target_pairs={{0,4},{2,6},{4,0},{6,2},{1,5},{3,7},{5,1},{7,3},{8,12},{10,14},{12... | collective-permute-start | bytes 1572872 | tf_op jit(solution)/shard_map/ppermute | solution.py:19
  139.8 26.8 %collective-permute-start.8 = (f32[8,128,128]{2,1,0:T(8,128)}, f32[8,128,128]{2,1,0:T(8,128)S(1)}, u32[]{:S(2)}, u32[]{:S(2)}) collective-permute-start(f32[8,128,128]{2,1,0:T(8,128)} %get-tuple-element.73), channel_id=1, source_target_pairs={{0,6},{2,4},{4,2},{6,0},{1,7},{3,5},{5,3},{7,1},{8,14},{10,12},{12... | collective-permute-start | bytes 1572872 | tf_op jit(solution)/shard_map/ppermute | solution.py:19
  152.8 18.5 %collective-permute-start.37 = (f32[16,8,128]{2,1,0:T(8,128)S(1)}, f32[16,8,128]{2,1,0:T(8,128)S(1)}, u32[]{:S(2)}, u32[]{:S(2)}) collective-permute-start(f32[16,8,128]{2,1,0:T(8,128)S(1)} %get-tuple-element.114), channel_id=1, source_target_pairs={{0,2},{2,0},{4,6},{6,4},{1,3},{3,1},{5,7},{7,5},{8,10},{10,8},{12,... | collective-permute-start | bytes 196616 | tf_op jit(solution)/shard_map/ppermute | solution.py:19
  154.0 18.6 %collective-permute-start.38 = (f32[16,8,128]{2,1,0:T(8,128)S(1)}, f32[16,8,128]{2,1,0:T(8,128)S(1)}, u32[]{:S(2)}, u32[]{:S(2)}) collective-permute-start(f32[16,8,128]{2,1,0:T(8,128)S(1)} %get-tuple-element.115), channel_id=1, source_target_pairs={{0,4},{2,6},{4,0},{6,2},{1,5},{3,7},{5,1},{7,3},{8,12},{10,14},{12... | collective-permute-start | bytes 196616 | tf_op jit(solution)/shard_map/ppermute | solution.py:19
  160.4 12.7 %collective-permute-start.39 = (f32[16,8,128]{2,1,0:T(8,128)S(1)}, f32[16,8,128]{2,1,0:T(8,128)S(1)}, u32[]{:S(2)}, u32[]{:S(2)}) collective-permute-start(f32[16,8,128]{2,1,0:T(8,128)S(1)} %get-tuple-element.116), channel_id=1, source_target_pairs={{0,6},{2,4},{4,2},{6,0},{1,7},{3,5},{5,3},{7,1},{8,14},{10,12},{12... | collective-permute-start | bytes 196616 | tf_op jit(solution)/shard_map/ppermute | solution.py:19
  169.9 8.2 %collective-permute-start.40 = (f32[16,8,128]{2,1,0:T(8,128)S(1)}, f32[16,8,128]{2,1,0:T(8,128)S(1)}, u32[]{:S(2)}, u32[]{:S(2)}) collective-permute-start(f32[16,8,128]{2,1,0:T(8,128)S(1)} %get-tuple-element.118), channel_id=1, source_target_pairs={{0,2},{2,0},{4,6},{6,4},{1,3},{3,1},{5,7},{7,5},{8,10},{10,8},{12,... | collective-permute-start | bytes 196616 | tf_op jit(solution)/shard_map/ppermute | solution.py:19
  171.3 23.5 %collective-permute-start.44 = (f32[64,32,128]{2,1,0:T(8,128)S(1)}, f32[64,32,128]{2,1,0:T(8,128)S(1)}, u32[]{:S(2)}, u32[]{:S(2)}) collective-permute-start(f32[64,32,128]{2,1,0:T(8,128)S(1)} %get-tuple-element.127), channel_id=1, source_target_pairs={{0,1},{1,0},{2,3},{3,2},{4,5},{5,4},{6,7},{7,6},{8,9},{9,8},{10,11... | collective-permute-start | bytes 3145736 | tf_op jit(solution)/shard_map/ppermute | solution.py:19
  173.9 6.2 %collective-permute-start.19 = (f32[64,512]{1,0:T(8,128)S(1)}, f32[64,512]{1,0:T(8,128)S(1)}, u32[]{:S(2)}, u32[]{:S(2)}) collective-permute-start(f32[64,512]{1,0:T(8,128)S(1)} %get-tuple-element.123), channel_id=1, source_target_pairs={{0,2},{2,0},{4,6},{6,4},{1,3},{3,1},{5,7},{7,5},{8,10},{10,8},{12,... | collective-permute-start | bytes 393224 | tf_op jit(solution)/shard_map/ppermute | solution.py:19
  175.4 8.2 %collective-permute-start.21 = (f32[64,512]{1,0:T(8,128)S(1)}, f32[64,512]{1,0:T(8,128)S(1)}, u32[]{:S(2)}, u32[]{:S(2)}) collective-permute-start(f32[64,512]{1,0:T(8,128)S(1)} %get-tuple-element.124), channel_id=1, source_target_pairs={{0,6},{2,4},{4,2},{6,0},{1,7},{3,5},{5,3},{7,1},{8,14},{10,12},{12... | collective-permute-start | bytes 393224 | tf_op jit(solution)/shard_map/ppermute | solution.py:19
  176.8 9.9 %collective-permute-start.20 = (f32[64,512]{1,0:T(8,128)S(1)}, f32[64,512]{1,0:T(8,128)S(1)}, u32[]{:S(2)}, u32[]{:S(2)}) collective-permute-start(f32[64,512]{1,0:T(8,128)S(1)} %get-tuple-element.125), channel_id=1, source_target_pairs={{0,4},{2,6},{4,0},{6,2},{1,5},{3,7},{5,1},{7,3},{8,12},{10,14},{12... | collective-permute-start | bytes 393224 | tf_op jit(solution)/shard_map/ppermute | solution.py:19
  178.1 10.6 %collective-permute-start.41 = (f32[16,8,128]{2,1,0:T(8,128)S(1)}, f32[16,8,128]{2,1,0:T(8,128)S(1)}, u32[]{:S(2)}, u32[]{:S(2)}) collective-permute-start(f32[16,8,128]{2,1,0:T(8,128)S(1)} %get-tuple-element.119), channel_id=1, source_target_pairs={{0,4},{2,6},{4,0},{6,2},{1,5},{3,7},{5,1},{7,3},{8,12},{10,14},{12... | collective-permute-start | bytes 196616 | tf_op jit(solution)/shard_map/ppermute | solution.py:19
  180.1 9.2 %collective-permute-start.42 = (f32[16,8,128]{2,1,0:T(8,128)S(1)}, f32[16,8,128]{2,1,0:T(8,128)S(1)}, u32[]{:S(2)}, u32[]{:S(2)}) collective-permute-start(f32[16,8,128]{2,1,0:T(8,128)S(1)} %get-tuple-element.120), channel_id=1, source_target_pairs={{0,6},{2,4},{4,2},{6,0},{1,7},{3,5},{5,3},{7,1},{8,14},{10,12},{12... | collective-permute-start | bytes 196616 | tf_op jit(solution)/shard_map/ppermute | solution.py:19
  186.8 5.0 %collective-permute-start.22 = (f32[64,512]{1,0:T(8,128)S(1)}, f32[64,512]{1,0:T(8,128)S(1)}, u32[]{:S(2)}, u32[]{:S(2)}) collective-permute-start(f32[64,512]{1,0:T(8,128)S(1)} %fusion.14), channel_id=1, source_target_pairs={{0,8},{8,0},{16,24},{24,16},{1,9},{9,1},{17,25},{25,17},{2,10},{10... | collective-permute-start | bytes 393224 | tf_op jit(solution)/shard_map/ppermute | solution.py:19
  191.1 5.9 %collective-permute-start.43 = (f32[16,32,256]{2,1,0:T(8,128)S(1)}, f32[16,32,256]{2,1,0:T(8,128)S(1)}, u32[]{:S(2)}, u32[]{:S(2)}) collective-permute-start(f32[16,32,256]{2,1,0:T(8,128)S(1)} %slice.30), channel_id=1, source_target_pairs={{0,1},{1,0},{2,3},{3,2},{4,5},{5,4},{6,7},{7,6},{8,9},{9,8},{10,11... | collective-permute-start | bytes 1572872 | tf_op jit(solution)/shard_map/ppermute | solution.py:19
  191.8 9.7 %collective-permute-start.23 = (f32[64,512]{1,0:T(8,128)S(1)}, f32[64,512]{1,0:T(8,128)S(1)}, u32[]{:S(2)}, u32[]{:S(2)}) collective-permute-start(f32[64,512]{1,0:T(8,128)S(1)} %add.108), channel_id=1, source_target_pairs={{0,16},{8,24},{16,0},{24,8},{1,17},{9,25},{17,1},{25,9},{2,18},{10... | collective-permute-start | bytes 393224 | tf_op jit(solution)/shard_map/ppermute | solution.py:19
  198.0 4.8 %collective-permute-start.47 = (f32[32,64]{1,0:T(8,128)S(1)}, f32[32,64]{1,0:T(8,128)S(1)}, u32[]{:S(2)}, u32[]{:S(2)}) collective-permute-start(f32[32,64]{1,0:T(8,128)S(1)} %fusion.2), channel_id=1, source_target_pairs={{0,6},{2,4},{4,2},{6,0},{1,7},{3,5},{5,3},{7,1},{8,14},{10,12},{12... | collective-permute-start | bytes 24584 | tf_op jit(solution)/shard_map/ppermute | solution.py:19
  198.4 4.3 %collective-permute-start.46 = (f32[32,64]{1,0:T(8,128)S(1)}, f32[32,64]{1,0:T(8,128)S(1)}, u32[]{:S(2)}, u32[]{:S(2)}) collective-permute-start(f32[32,64]{1,0:T(8,128)S(1)} %fusion.2), channel_id=1, source_target_pairs={{0,4},{2,6},{4,0},{6,2},{1,5},{3,7},{5,1},{7,3},{8,12},{10,14},{12... | collective-permute-start | bytes 24584 | tf_op jit(solution)/shard_map/ppermute | solution.py:19
  200.8 3.7 %collective-permute-start.45 = (f32[32,64]{1,0:T(8,128)S(1)}, f32[32,64]{1,0:T(8,128)S(1)}, u32[]{:S(2)}, u32[]{:S(2)}) collective-permute-start(f32[32,64]{1,0:T(8,128)S(1)} %fusion.2), channel_id=1, source_target_pairs={{0,2},{2,0},{4,6},{6,4},{1,3},{3,1},{5,7},{7,5},{8,10},{10,8},{12,... | collective-permute-start | bytes 24584 | tf_op jit(solution)/shard_map/ppermute | solution.py:19
  201.6 7.1 %collective-permute-start.24 = (f32[64,512]{1,0:T(8,128)S(1)}, f32[64,512]{1,0:T(8,128)S(1)}, u32[]{:S(2)}, u32[]{:S(2)}) collective-permute-start(f32[64,512]{1,0:T(8,128)S(1)} %add_multiply_fusion), channel_id=1, source_target_pairs={{0,1},{1,0},{2,3},{3,2},{4,5},{5,4},{6,7},{7,6},{8,9},{9,8},{10,11... | collective-permute-start | bytes 393224 | tf_op jit(solution)/shard_map/ppermute | solution.py:19
  208.3 4.6 %collective-permute-start.49 = (f32[32,64]{1,0:T(8,128)S(1)}, f32[32,64]{1,0:T(8,128)S(1)}, u32[]{:S(2)}, u32[]{:S(2)}) collective-permute-start(f32[32,64]{1,0:T(8,128)S(1)} %add.122), channel_id=1, source_target_pairs={{0,16},{8,24},{16,0},{24,8},{1,17},{9,25},{17,1},{25,9},{2,18},{10... | collective-permute-start | bytes 24584 | tf_op jit(solution)/shard_map/ppermute | solution.py:19
  (24 other events, 219.5 us)

commit v2 on v0

v2 whole, which is shorter than its diff:
```python
import functools

import jax
import jax.numpy as jnp
from jax import lax
from jax.experimental import pallas as pl
from jax.experimental.pallas import tpu as pltpu
from jax.sharding import PartitionSpec as P

LANES = 128
precise_mode = lax.Precision.HIGHEST


def xor_pairs(k, n):
    return [(i, i ^ k) for i in range(n)]


def swap(v, axis, k):
    return lax.ppermute(v, axis, xor_pairs(k, lax.axis_size(axis)))


def all_sum(v, axis):
    k = 1
    while k < lax.axis_size(axis):
        v = v + swap(v, axis, k)
        k *= 2
    return v


def split(v):
    high = v.astype(jnp.bfloat16)
    return high, (v - high.astype(jnp.float32)).astype(jnp.bfloat16)


def dot_t(a, b):
    return lax.dot_general(
        a, b, (((1,), (1,)), ((), ())), preferred_element_type=jnp.float32
    )


def pack_kernel(shifts, corner, snapshots, *refs):
    count = len(shifts)
    packed, (taken, taken_sem) = refs[:count], refs[count:]
    width = taken.shape[2]
    me = lax.axis_index("tm")
    loads = []
    for i, k in enumerate(shifts):
        load, lane = corner(me ^ k)
        source = snapshots.at[
            :,
            pl.ds(pl.multiple_of(load, 8), width),
            pl.ds(pl.multiple_of(lane, LANES), LANES),
        ]
        loads.append(pltpu.make_async_copy(source, taken.at[i], taken_sem.at[i]))
        loads[-1].start()
    for i in range(count):
        loads[i].wait()
        for p in range(width):
            packed[i][p] = taken[i, :, p, :]


def pack(snapshots, shifts, corner, width):
    rows = snapshots.shape[0]
    count = len(shifts)
    f32 = jnp.float32
    return pl.pallas_call(
        functools.partial(pack_kernel, shifts, corner),
        out_shape=[jax.ShapeDtypeStruct((width, rows, LANES), f32)] * count,
        in_specs=[pl.BlockSpec(memory_space=pl.ANY)],
        out_specs=[pl.BlockSpec(memory_space=pltpu.VMEM)] * count,
        scratch_shapes=[
            pltpu.VMEM((count, rows, width, LANES), f32),
            pltpu.SemaphoreType.DMA((count,)),
        ],
        compiler_params=pltpu.CompilerParams(vmem_limit_bytes=53 * 2**20),
        cost_estimate=pl.CostEstimate(
            flops=0, bytes_accessed=8 * count * width * rows * LANES, transcendentals=0
        ),
    )(snapshots)


def chunk_kernel(n, first, last, basis, *refs):
    blocks, refs = refs[:n], refs[n:]
    if not first:
        before, refs = refs[0], refs[1:]
    core, pieces, refs = refs[0], refs[1 : n + 1], refs[n + 1 :]
    if last:
        keep, send, total, high, low = refs
    else:
        total, high, low = refs
    me, half = lax.axis_index("tm"), lax.axis_index("param")
    loads, rows = blocks[0].shape[:2]
    rank = core.shape[0]
    for k in range(n):
        at = pl.ds(pl.multiple_of((me ^ k) * rows, rows), rows)
        for p in range(loads):
            h, l = split(blocks[k][p])
            high[at, p * LANES : (p + 1) * LANES] = h
            low[at, p * LANES : (p + 1) * LANES] = l
    h, l = high[...], low[...]
    product = dot_t(
        jnp.concatenate([h, h, l], axis=1), jnp.concatenate([h, l, h], axis=1)
    )
    if first:
        total[...] = product
    else:
        total[...] = before[...] + product
    if last:
        cut = keep.shape[1]
        for j in range(n):
            mine = pl.multiple_of(j * rows + half * cut, cut)
            other = pl.multiple_of(j * rows + (1 - half) * cut, cut)
            keep[j] = total[pl.ds(mine, cut), :]
            send[j] = total[pl.ds(other, cut), :]
    b = jnp.concatenate(split(basis[...]), axis=0)
    wide = jnp.dot(b, h, preferred_element_type=jnp.float32)
    wide = wide + jnp.dot(b, l, preferred_element_type=jnp.float32)
    values = wide[:rank] + wide[rank:]
    own = rank // n
    for p in range(loads):
        part = values[:, p * LANES : (p + 1) * LANES]
        core[:, p, :] = part
        for k in range(n):
            pieces[k][:, p, :] = part[k * own : (k + 1) * own]


def run_chunk(basis, blocks, before, last):
    n = len(blocks)
    loads, rows, lanes = blocks[0].shape
    steps = n * rows
    rank = basis.shape[0]
    first = before is None
    args = [basis, *blocks] + ([] if first else [before])
    f32 = lambda *dims: jax.ShapeDtypeStruct(dims, jnp.float32)
    shapes = [f32(rank, loads, lanes)] + [f32(rank // n, loads, lanes)] * n
    scratch = [pltpu.VMEM((steps, loads * lanes), jnp.bfloat16)] * 2
    if last:
        shapes += [f32(n, rows // 2, steps)] * 2
        scratch = [pltpu.VMEM((steps, steps), jnp.float32)] + scratch
    else:
        shapes += [f32(steps, steps)]
    points = loads * lanes
    return pl.pallas_call(
        functools.partial(chunk_kernel, n, first, last),
        out_shape=shapes,
        scratch_shapes=scratch,
        compiler_params=pltpu.CompilerParams(vmem_limit_bytes=40 * 2**20),
        cost_estimate=pl.CostEstimate(
            flops=2 * steps * points * (3 * steps + 4 * rank),
            bytes_accessed=4 * steps * (points + 2 * steps),
            transcendentals=0,
        ),
    )(*args)


def load_products(left, right):
    rank = left[0].shape[0]
    many = 16 if rank % 16 == 0 else rank

    def tiles(refs, first):
        rows = [
            jnp.concatenate([ref[r] for ref in refs])
            for r in range(first, first + many)
        ]
        return jnp.concatenate(split(jnp.concatenate(rows, axis=1)), axis=0)

    acc = 0.0
    for r in range(0, rank, many):
        acc = acc + dot_t(tiles(left, r), tiles(right, r))
    rows, columns = acc.shape[0] // 2, acc.shape[1] // 2
    acc = acc[:rows] + acc[rows:]
    return acc[:, :columns] + acc[:, columns:]


def load_gram_kernel(groups, *refs):
    own, far, out = refs[:groups], refs[groups:-1], refs[-1]
    out[...] = load_products(own, own + far)


def load_gram(own, far):
    loads = sum(v.shape[1] for v in own)
    both = loads + sum(v.shape[1] for v in far)
    return pl.pallas_call(
        functools.partial(load_gram_kernel, len(own)),
        out_shape=jax.ShapeDtypeStruct((loads, both), jnp.float32),
    )(*own, *far)


def fold_kernel(n, groups, keep, got, far, part, rest, *refs):
    own, outs = refs[:groups], refs[groups:]
    me, half = lax.axis_index("tm"), lax.axis_index("param")
    loads = part.shape[0]
    total = jnp.concatenate([part[...], load_products(own, [far])], axis=1)
    swapped = jnp.concatenate([total[:, loads:], total[:, :loads]], axis=1)
    total = jnp.where(half == 0, total, swapped) + rest[...]
    total = jnp.concatenate(
        [total, jnp.zeros((loads, LANES - 2 * loads), jnp.float32)], axis=1
    )
    cut = keep.shape[1]
    for k in range(n):
        outs[k][:cut] = keep[me ^ k] + got[me ^ k]
        for b in range(loads // 8):
            outs[k][cut:, b * LANES : (b + 1) * LANES] = total[b * 8 : (b + 1) * 8]


def fold(keep, got, far, part, rest, own):
    n, cut, steps = keep.shape
    shape = jax.ShapeDtypeStruct((cut + 8, steps), jnp.float32)
    return pl.pallas_call(
        functools.partial(fold_kernel, n, len(own)),
        out_shape=[shape] * n,
    )(keep, got, far, part, rest, *own)


def place_kernel(n, places, *refs):
    out = refs[-1]
    me = lax.axis_index("tm")
    for where, piece in zip(places, refs):
        load, lane = where(me)
        count = piece.shape[1]
        at = pl.ds(pl.multiple_of(load, 8), count)
        out[:, at, pl.ds(pl.multiple_of(lane, LANES), LANES)] = piece[...]


def place_pieces(n, places, pieces, shape):
    specs = []
    for piece in pieces:
        block = (shape[0],) + piece.shape[1:]
        specs.append(pl.BlockSpec(block, lambda i: (0, 0, 0)))
    return pl.pallas_call(
        functools.partial(place_kernel, n, places),
        out_shape=jax.ShapeDtypeStruct(shape, jnp.float32),
        grid=(1,),
        in_specs=specs,
        out_specs=pl.BlockSpec(shape, lambda i: (0, 0, 0)),
        compiler_params=pltpu.CompilerParams(vmem_limit_bytes=16 * 2**20),
    )(*pieces)


def after(v, *others):
    return lax.optimization_barrier((v, others))[0]


def body(snapshots, time_basis):
    rows, loads, points = snapshots.shape
    n = lax.axis_size("tm")
    me, half = lax.axis_index("tm"), lax.axis_index("param")
    rank = time_basis.shape[1]
    own_rank = rank // n
    total_points = points * lax.axis_size("space")
    total_loads = loads * lax.axis_size("param")
    tiles = points // LANES
    cut = loads // n
    mains = tiles // n
    group = 8 if loads % 8 == 0 else loads
    groups = loads // group
    others = tuple(range(1, n))

    chunks = [("load", t) for t in range(mains * n, tiles)]
    chunks += [("tile", m, g) for m in range(mains) for g in range(groups)]
    n_load = tiles - mains * n

    order = me ^ jnp.arange(n)
    basis = time_basis.reshape(-1, n, own_rank)[:, order].reshape(-1, rank).T

    def corner(chunk, j):
        if chunk[0] == "load":
            return j * cut, chunk[1] * LANES
        return chunk[2] * group, (chunk[1] * n + j) * LANES

    def shares(x, chunk, shifts):
        width = cut if chunk[0] == "load" else group
        if width % 8 == 0:
            return pack(x, shifts, functools.partial(corner, chunk), width)
        out = []
        for k in shifts:
            load, lane = corner(chunk, me ^ k)
            v = lax.dynamic_slice(x, (0, load, lane), (rows, width, LANES))
            out.append(v.transpose(1, 0, 2))
        return out

    sent = []

    def send(v, k, depth=4):
        if len(sent) >= depth:
            v = after(v, sent[-depth])
        sent.append(swap(v, "tm", k))
        return sent[-1]

    pick = lambda v, k: lax.dynamic_index_in_dim(v, me ^ k, 0, False)
    place_of = lambda i, k: lambda me: corner(chunks[i], me ^ k)
    held, cores, pieces, far = [], [], [], []
    places, placed = [], []
    total = param_part = None

    def send_pieces(first, last, depth=4):
        for k in others:
            parts = [pieces[i][k] for i in range(first, last)]
            part = parts[0] if len(parts) == 1 else jnp.concatenate(parts, axis=1)
            part = send(part, k, depth)
            if chunks[first][0] == "load":
                width = part.shape[1] // (last - first)
                for i in range(first, last):
                    places.append(place_of(i, k))
                    placed.append(part[:, (i - first) * width : (i - first + 1) * width])
            else:
                places.append(place_of(first, k))
                placed.append(part)

    def chunk_done(i):
        nonlocal total
        x = after(snapshots, held[i - 1][0]) if i else snapshots
        own = shares(x, chunks[i], (0,))[0]
        before, partners = total, held[i]
        last = i == len(chunks) - 1
        if last and i:
            before, partners = after((before, partners), param_part, far)
        out = run_chunk(basis, [own, *partners], before, last)
        cores.append(out[0])
        pieces.append(out[1 : n + 1])
        total = out[n + 1 :] if last else out[n + 1]
        if chunks[i][0] == "tile" and not last:
            far.append(swap(cores[i], "param", 1))
        for_own = pieces[i][0]
        places.append(place_of(i, 0))
        placed.append(for_own)

    def put(core, part, at):
        return lax.dynamic_update_slice(core, part, at)

    def load_part():
        rest = []
        for i in range(n_load):
            tile = jnp.zeros((own_rank, loads, LANES), jnp.float32)
            for where, part in zip(places, placed):
                load, lane = where(me)
                if where(0)[1] == chunks[i][1] * LANES:
                    tile = put(tile, part, (0, load, 0))
            rest.append(tile)
        rest = jnp.concatenate(rest, axis=2)
        other = swap(rest, "param", 1)
        both = jnp.where(
            half == 0,
            jnp.concatenate([rest, other], axis=1),
            jnp.concatenate([other, rest], axis=1),
        )
        return jnp.einsum("rps,rqs->pq", rest, both, precision=precise_mode)

    ahead = 2
    load_sent = n_load == 0
    packs = ()
    for i, chunk in enumerate(chunks):
        x = after(snapshots, packs, held[i - 3] if i >= 3 else ())
        packs = parts = shares(x, chunk, others)
        held.append([send(v, k) for v, k in zip(parts, others)])
        if i >= ahead:
            chunk_done(i - ahead)
        if len(cores) == n_load and not load_sent and mains:
            send_pieces(0, n_load)
            load_sent = True
            param_part = load_part()
    for i in range(len(chunks) - ahead, len(chunks)):
        chunk_done(i)
    if not load_sent:
        send_pieces(0, n_load)
        param_part = load_part()
    keep, other_half = total
    wide = -(-total_loads // LANES) * LANES
    steps = n * rows
    across = steps // wide
    fused = mains == 1 and group == 8 and loads * LANES == 8 * steps and n_load
    got = swap(other_half, "param", 1)
    if fused:
        far_last = swap(cores[-1], "param", 1)
        part = load_gram(cores[n_load:], far)
        mixed = fold(keep, got, far_last, part, param_part, cores[n_load:])
    else:
        if mains:
            far.append(swap(cores[-1], "param", 1))
        for m in range(mains):
            these = slice(m * groups, (m + 1) * groups)
            part = load_gram(cores[n_load:][these], far[these])
            swapped = jnp.concatenate([part[:, loads:], part[:, :loads]], axis=1)
            part = jnp.where(half == 0, part, swapped)
            param_part = part if param_part is None else param_part + part
        padded = jnp.pad(param_part, ((0, 0), (0, wide - total_loads)))
        extra = padded.reshape(across, loads // across, wide).swapaxes(0, 1)
        extra = extra.reshape(loads // across, steps)
        rows_part = keep + got
        mixed = [jnp.concatenate([pick(rows_part, k), extra]) for k in range(n)]
    arrived = [send(mixed[k], k) for k in others]
    mine = mixed[0]
    for part in arrived:
        mine = mine + part
    mine = all_sum(mine, "space")

    for m in range(mains):
        at = n_load + m * groups
        send_pieces(at, at + groups)
    if cut % 8 == 0 and group % 8 == 0:
        core = place_pieces(n, places, placed, (own_rank, loads, points))
    else:
        core = jnp.zeros((own_rank, loads, points), jnp.float32)
        for where, part in zip(places, placed):
            core = put(core, part, (0, *where(me)))

    extra = mine[rows // 2 :].reshape(loads // across, across, wide).swapaxes(0, 1)
    gram_param = extra.reshape(loads, wide)[:, :total_loads] / (rank * total_points)
    other = swap(mine, "param", 1)[: rows // 2]
    mine = mine[: rows // 2]
    gram_time = jnp.where(
        half == 0,
        jnp.concatenate([mine, other]),
        jnp.concatenate([other, mine]),
    )
    gram_time = gram_time / (total_loads * total_points)
    return (gram_time, core, gram_param)


def solution(mesh):
    placed = (P("tm", "param", "space"), P())
    return jax.shard_map(
        body,
        mesh=mesh,
        in_specs=placed,
        out_specs=(P("tm", None), P("tm", "param", "space"), P("param", None)),
        check_vma=False,
    )
```

time: 482 us -> 195 us (0.40)
  blocking collectives: 221 us -> 0 us
  waiting for transfers between devices: 146 us -> 79.9 us
  Pallas kernels: 0 us -> 54.1 us
  matrix products: 50.9 us -> 3.24 us
  starting transfers between devices: 0.56 us -> 46.1 us
  local copies, waits for them, and re-layouts: 46.9 us -> 6.39 us
  between operations: 13.8 us -> 1.14 us
    all_to_all x1 -> x0, blocking collectives: 144 us -> none  [body(): lax.all_to_all(snapshots, 'tm', split_axis=2, concat_axis=0, tiled=True)]
    reduce_scatter x2 -> x0, waiting for transfers between devices: 80.3 us -> none  [the longest x1 73.2 us: body(): lax.psum_scatter(jnp.einsum('tr,tps->rps', basis_rows, snapshots, precisi...]
    ppermute x0 -> x36, waiting for transfers between devices: none -> 79.9 us  [swap(): return lax.ppermute(v, axis, xor_pairs(k, lax.axis_size(axis)))]
    psum x1 -> x0, blocking collectives: 77 us -> none  [body(): lax.psum(param_part, ('space', 'tm')) / (rank_all * total_points)]
    psum x1 -> x0, waiting for transfers between devices: 57.4 us -> none  [body(): lax.psum(rows_part, ('space', 'param')) / (all_loads * total_points)]
    pallas_call x0 -> x21, Pallas kernels: none -> 54.1 us  [the longest x12 26.2 us: pack(): pl.pallas_call(functools.partial(pack_kernel, shifts, corner), out_shape=...]
    dot_general x3 -> x1, matrix products: 50.9 us -> 3.24 us  [load_part(): return jnp.einsum('rps,rqs->pq', rest, both, precision=precise_mode)]
    ppermute x0 -> x36, starting transfers between devices: none -> 46.1 us  [swap(): return lax.ppermute(v, axis, xor_pairs(k, lax.axis_size(axis)))]
  transfers between devices with their start and end apart: 4 -> 36, of which waited for: 4 -> 18; matrix products, arithmetic and copies ran while one was open for 5% -> 3% of each run, Pallas kernels for 0% -> 23%
where the time goes in v2:
time: 195 us; the launch traced here: 194 us
  waiting for transfers between devices  79.9 us (41%)
  Pallas kernels  54.1 us (28%)
  starting transfers between devices  46.1 us (24%)
  local copies, waits for them, and re-layouts  6.39 us (3%)
  other arithmetic  3.33 us (2%)
  matrix products  3.24 us (2%)
    ppermute x36, waiting for transfers between devices, swap(): return lax.ppermute(v, axis, xor_pairs(k, lax.axis_size(axis)))  79.9 us
    ppermute x36, starting transfers between devices, swap(): return lax.ppermute(v, axis, xor_pairs(k, lax.axis_size(axis)))  46.1 us
    pallas_call x12, Pallas kernels, pack(): pl.pallas_call(functools.partial(pack_kernel, shifts, corner), out_shape=...  26.2 us
    pallas_call x6, Pallas kernels, run_chunk(): pl.pallas_call(functools.partial(chunk_kernel, n, first, last), out_shape...  20.6 us
    unnamed x44, local copies, waits for them, and re-layouts  5.69 us
  transfers between devices with their start and end apart: 36, of which 18 were waited for; matrix products, arithmetic and copies ran while one was open for 3% of the time, Pallas kernels for 23%

profile of v2, /device:TPU:0, one launch (start us, length us, event | category | flops | bytes accessed | tf_op | source)
XLA Modules:
  0.0 194.3 jit_solution(3665115247217449586)
XLA Ops:
  0.6 2.9 %shard_map.49 = (f32[8,128,128]{2,1,0:T(8,128)S(1)}, f32[8,128,128]{2,1,0:T(8,128)}, f32[8,128,128]{2,1,0:T(8,128)}) custom-call(f32[128,32,768]{2,1,0:T(8,128)} %snapshots.12), custom_call_target="tpu_custom_call" | custom-call | bytes 3145728 | tf_op jit(solution)/shard_map/pallas_call | solution.py:66
  3.6 3.0 %collective-permute-start = (f32[8,128,128]{2,1,0:T(8,128)S(1)}, f32[8,128,128]{2,1,0:T(8,128)S(1)}, u32[]{:S(2)}, u32[]{:S(2)}) collective-permute-start(f32[8,128,128]{2,1,0:T(8,128)S(1)} %get-tuple-element.97), channel_id=1, source_target_pairs={{0,2},{2,0},{4,6},{6,4},{1,3},{3,1},{5,7},{7,5},{8,10},{10,8},{12,... | collective-permute-start | bytes 1572872 | tf_op jit(solution)/shard_map/ppermute | solution.py:19
  6.6 1.5 collective-permute-start.1
  8.1 2.9 %shard_map.50 = (f32[8,128,128]{2,1,0:T(8,128)S(1)}, f32[8,128,128]{2,1,0:T(8,128)}, f32[8,128,128]{2,1,0:T(8,128)}) custom-call(f32[128,32,768]{2,1,0:T(8,128)} %snapshots.12), custom_call_target="tpu_custom_call" | custom-call | bytes 3145728 | tf_op jit(solution)/shard_map/pallas_call | solution.py:66
  11.0 2.0 %collective-permute-start.3 = (f32[8,128,128]{2,1,0:T(8,128)S(1)}, f32[8,128,128]{2,1,0:T(8,128)S(1)}, u32[]{:S(2)}, u32[]{:S(2)}) collective-permute-start(f32[8,128,128]{2,1,0:T(8,128)S(1)} %get-tuple-element.101), channel_id=1, source_target_pairs={{0,2},{2,0},{4,6},{6,4},{1,3},{3,1},{5,7},{7,5},{8,10},{10,8},{12,... | collective-permute-start | bytes 1572872 | tf_op jit(solution)/shard_map/ppermute | solution.py:19
  13.0 6.3 %collective-permute-done.refs_1_ = f32[8,128,128]{2,1,0:T(8,128)S(1)} collective-permute-done((f32[8,128,128]{2,1,0:T(8,128)S(1)}, f32[8,128,128]{2,1,0:T(8,128)S(1)}, u32[]{:S(2)}, u32[]{:S(2)}) %collective-permute-start) | collective-permute-done | bytes 524320 | tf_op jit(solution)/shard_map/ppermute | solution.py:19
  19.3 2.1 %collective-permute-start.4 = (f32[8,128,128]{2,1,0:T(8,128)}, f32[8,128,128]{2,1,0:T(8,128)S(1)}, u32[]{:S(2)}, u32[]{:S(2)}) collective-permute-start(f32[8,128,128]{2,1,0:T(8,128)} %get-tuple-element.112), channel_id=1, source_target_pairs={{0,4},{2,6},{4,0},{6,2},{1,5},{3,7},{5,1},{7,3},{8,12},{10,14},{12... | collective-permute-start | bytes 1572872 | tf_op jit(solution)/shard_map/ppermute | solution.py:19
  21.4 10.6 %collective-permute-done.1.refs_2_ = f32[8,128,128]{2,1,0:T(8,128)S(1)} collective-permute-done((f32[8,128,128]{2,1,0:T(8,128)}, f32[8,128,128]{2,1,0:T(8,128)S(1)}, u32[]{:S(2)}, u32[]{:S(2)}) %collective-permute-start.1) | collective-permute-done | bytes 524320 | tf_op jit(solution)/shard_map/ppermute | solution.py:19
  32.9 3.0 %shard_map.51 = (f32[8,128,128]{2,1,0:T(8,128)}, f32[8,128,128]{2,1,0:T(8,128)}, f32[8,128,128]{2,1,0:T(8,128)}) custom-call(f32[128,32,768]{2,1,0:T(8,128)} %snapshots.12), custom_call_target="tpu_custom_call" | custom-call | bytes 3145728 | tf_op jit(solution)/shard_map/pallas_call | solution.py:66
  36.8 2.9 %collective-permute-start.15 = (f32[8,128,128]{2,1,0:T(8,128)}, f32[8,128,128]{2,1,0:T(8,128)S(1)}, u32[]{:S(2)}, u32[]{:S(2)}) collective-permute-start(f32[8,128,128]{2,1,0:T(8,128)} %get-tuple-element.135), channel_id=1, source_target_pairs={{0,2},{2,0},{4,6},{6,4},{1,3},{3,1},{5,7},{7,5},{8,10},{10,8},{12,... | collective-permute-start | bytes 1572872 | tf_op jit(solution)/shard_map/ppermute | solution.py:19
  39.7 2.2 %collective-permute-done.3.refs_1_ = f32[8,128,128]{2,1,0:T(8,128)S(1)} collective-permute-done((f32[8,128,128]{2,1,0:T(8,128)S(1)}, f32[8,128,128]{2,1,0:T(8,128)S(1)}, u32[]{:S(2)}, u32[]{:S(2)}) %collective-permute-start.3) | collective-permute-done | bytes 524320 | tf_op jit(solution)/shard_map/ppermute | solution.py:19
  41.8 2.1 %collective-permute-start.6 = (f32[8,128,128]{2,1,0:T(8,128)}, f32[8,128,128]{2,1,0:T(8,128)S(1)}, u32[]{:S(2)}, u32[]{:S(2)}) collective-permute-start(f32[8,128,128]{2,1,0:T(8,128)} %get-tuple-element.116), channel_id=1, source_target_pairs={{0,4},{2,6},{4,0},{6,2},{1,5},{3,7},{5,1},{7,3},{8,12},{10,14},{12... | collective-permute-start | bytes 1572872 | tf_op jit(solution)/shard_map/ppermute | solution.py:19
  45.9 3.0 %shard_map.52 = (f32[8,128,128]{2,1,0:T(8,128)S(1)}, f32[8,128,128]{2,1,0:T(8,128)}, f32[8,128,128]{2,1,0:T(8,128)}) custom-call(f32[128,32,768]{2,1,0:T(8,128)} %snapshots.12), custom_call_target="tpu_custom_call" | custom-call | bytes 3145728 | tf_op jit(solution)/shard_map/pallas_call | solution.py:66
  48.9 5.6 %collective-permute-done.4.refs_2_ = f32[8,128,128]{2,1,0:T(8,128)S(1)} collective-permute-done((f32[8,128,128]{2,1,0:T(8,128)}, f32[8,128,128]{2,1,0:T(8,128)S(1)}, u32[]{:S(2)}, u32[]{:S(2)}) %collective-permute-start.4) | collective-permute-done | bytes 524320 | tf_op jit(solution)/shard_map/ppermute | solution.py:19
  55.4 3.0 %collective-permute-start.9 = (f32[8,128,128]{2,1,0:T(8,128)S(1)}, f32[8,128,128]{2,1,0:T(8,128)S(1)}, u32[]{:S(2)}, u32[]{:S(2)}) collective-permute-start(f32[8,128,128]{2,1,0:T(8,128)S(1)} %get-tuple-element.120), channel_id=1, source_target_pairs={{0,2},{2,0},{4,6},{6,4},{1,3},{3,1},{5,7},{7,5},{8,10},{10,8},{12,... | collective-permute-start | bytes 1572872 | tf_op jit(solution)/shard_map/ppermute | solution.py:19
  58.3 3.4 %shard_map.57 = (f32[64,8,128]{2,1,0:T(8,128)}, f32[16,8,128]{2,1,0:T(8,128)S(1)}, f32[16,8,128]{2,1,0:T(8,128)S(1)}, f32[16,8,128]{2,1,0:T(8,128)S(1)}, f32[16,...) custom-call(f32[64,512]{1,0:T(8,128)S(1)} %bitcast.17, f32[8,128,128]{2,1,0:T(8,128)S(1)} %shard_map.56.refs_0_, ...), custom_call_target="tpu_custom_call" | custom-call | flops 1879048192 | bytes 4194304 | tf_op jit(solution)/shard_map/pallas_call | solution.py:143
  64.6 11.0 %collective-permute-done.6.refs_2_ = f32[8,128,128]{2,1,0:T(8,128)S(1)} collective-permute-done((f32[8,128,128]{2,1,0:T(8,128)}, f32[8,128,128]{2,1,0:T(8,128)S(1)}, u32[]{:S(2)}, u32[]{:S(2)}) %collective-permute-start.6) | collective-permute-done | bytes 524320 | tf_op jit(solution)/shard_map/ppermute | solution.py:19
  75.5 1.5 collective-permute-start.7
  77.9 4.5 %shard_map.59 = (f32[64,8,128]{2,1,0:T(8,128)}, f32[16,8,128]{2,1,0:T(8,128)S(1)}, f32[16,8,128]{2,1,0:T(8,128)S(1)}, f32[16,8,128]{2,1,0:T(8,128)S(1)}, f32[16,...) custom-call(f32[64,512]{1,0:T(8,128)S(1)} %bitcast.18, f32[8,128,128]{2,1,0:T(8,128)S(1)} %shard_map.58.refs_0_, ...), custom_call_target="tpu_custom_call" | custom-call | flops 1879048192 | bytes 4194304 | tf_op jit(solution)/shard_map/pallas_call | solution.py:143
  82.4 1.5 collective-permute-start.11
  83.9 3.0 %collective-permute-done.9.refs_1_ = f32[8,128,128]{2,1,0:T(8,128)S(1)} collective-permute-done((f32[8,128,128]{2,1,0:T(8,128)S(1)}, f32[8,128,128]{2,1,0:T(8,128)S(1)}, u32[]{:S(2)}, u32[]{:S(2)}) %collective-permute-start.9) | collective-permute-done | bytes 524320 | tf_op jit(solution)/shard_map/ppermute | solution.py:19
  86.9 2.1 %collective-permute-start.13 = (f32[16,16,128]{2,1,0:T(8,128)S(1)}, f32[16,16,128]{2,1,0:T(8,128)S(1)}, u32[]{:S(2)}, u32[]{:S(2)}) collective-permute-start(f32[16,16,128]{2,1,0:T(8,128)S(1)} %pad_maximum_fusion.6), channel_id=1, source_target_pairs={{0,4},{2,6},{4,0},{6,2},{1,5},{3,7},{5,1},{7,3},{8,12},{10,14},{12... | collective-permute-start | bytes 393224 | tf_op jit(solution)/shard_map/ppermute | solution.py:19
  90.3 2.9 %shard_map.53 = (f32[8,128,128]{2,1,0:T(8,128)S(1)}, f32[8,128,128]{2,1,0:T(8,128)}, f32[8,128,128]{2,1,0:T(8,128)}) custom-call(f32[128,32,768]{2,1,0:T(8,128)} %snapshots.12), custom_call_target="tpu_custom_call" | custom-call | bytes 3145728 | tf_op jit(solution)/shard_map/pallas_call | solution.py:66
  93.2 8.3 %collective-permute-done.16.refs_2_ = f32[8,128,128]{2,1,0:T(8,128)S(1)} collective-permute-done((f32[8,128,128]{2,1,0:T(8,128)}, f32[8,128,128]{2,1,0:T(8,128)S(1)}, u32[]{:S(2)}, u32[]{:S(2)}) %collective-permute-start.16) | collective-permute-done | bytes 524320 | tf_op jit(solution)/shard_map/ppermute | solution.py:19
  101.5 3.3 %collective-permute-start.17 = (f32[16,16,128]{2,1,0:T(8,128)S(1)}, f32[16,16,128]{2,1,0:T(8,128)S(1)}, u32[]{:S(2)}, u32[]{:S(2)}) collective-permute-start(f32[16,16,128]{2,1,0:T(8,128)S(1)} %pad_maximum_fusion.7), channel_id=1, source_target_pairs={{0,6},{2,4},{4,2},{6,0},{1,7},{3,5},{5,3},{7,1},{8,14},{10,12},{12... | collective-permute-start | bytes 393224 | tf_op jit(solution)/shard_map/ppermute | solution.py:19
  105.4 2.6 %collective-permute-start.14 = (f32[8,128,128]{2,1,0:T(8,128)}, f32[8,128,128]{2,1,0:T(8,128)S(1)}, u32[]{:S(2)}, u32[]{:S(2)}) collective-permute-start(f32[8,128,128]{2,1,0:T(8,128)} %get-tuple-element.134), channel_id=1, source_target_pairs={{0,6},{2,4},{4,2},{6,0},{1,7},{3,5},{5,3},{7,1},{8,14},{10,12},{12... | collective-permute-start | bytes 1572872 | tf_op jit(solution)/shard_map/ppermute | solution.py:19
  110.2 2.9 %shard_map.62 = (f32[64,8,128]{2,1,0:T(8,128)S(1)}, f32[16,8,128]{2,1,0:T(8,128)S(1)}, f32[16,8,128]{2,1,0:T(8,128)S(1)}, f32[16,8,128]{2,1,0:T(8,128)S(1)}, f32...) custom-call(f32[64,512]{1,0:T(8,128)S(1)} %bitcast.19, f32[8,128,128]{2,1,0:T(8,128)S(1)} %shard_map.61.refs_0_, ...), custom_call_target="tpu_custom_call" | custom-call | flops 1879048192 | bytes 4194304 | tf_op jit(solution)/shard_map/pallas_call | solution.py:143
  113.6 3.0 %shard_map.65 = (f32[8,128,128]{2,1,0:T(8,128)}, f32[8,128,128]{2,1,0:T(8,128)}, f32[8,128,128]{2,1,0:T(8,128)}) custom-call(f32[128,32,768]{2,1,0:T(8,128)} %snapshots.12), custom_call_target="tpu_custom_call" | custom-call | bytes 3145728 | tf_op jit(solution)/shard_map/pallas_call | solution.py:66
  116.7 3.2 %collective-permute-done.8.refs_1_ = f32[8,128,128]{2,1,0:T(8,128)S(1)} collective-permute-done((f32[8,128,128]{2,1,0:T(8,128)S(1)}, f32[8,128,128]{2,1,0:T(8,128)S(1)}, u32[]{:S(2)}, u32[]{:S(2)}) %collective-permute-start.8) | collective-permute-done | bytes 524320 | tf_op jit(solution)/shard_map/ppermute | solution.py:19
  119.8 1.7 collective-permute-start.18
  121.6 7.5 %collective-permute-done.12.refs_2_ = f32[8,128,128]{2,1,0:T(8,128)S(1)} collective-permute-done((f32[8,128,128]{2,1,0:T(8,128)}, f32[8,128,128]{2,1,0:T(8,128)S(1)}, u32[]{:S(2)}, u32[]{:S(2)}) %collective-permute-start.12) | collective-permute-done | bytes 524320 | tf_op jit(solution)/shard_map/ppermute | solution.py:19
  129.1 2.3 %collective-permute-start.19 = (f32[8,128,128]{2,1,0:T(8,128)}, f32[8,128,128]{2,1,0:T(8,128)S(1)}, u32[]{:S(2)}, u32[]{:S(2)}) collective-permute-start(f32[8,128,128]{2,1,0:T(8,128)} %get-tuple-element.150), channel_id=1, source_target_pairs={{0,4},{2,6},{4,0},{6,2},{1,5},{3,7},{5,1},{7,3},{8,12},{10,14},{12... | collective-permute-start | bytes 1572872 | tf_op jit(solution)/shard_map/ppermute | solution.py:19
  132.4 2.7 %shard_map.63 = (f32[64,8,128]{2,1,0:T(8,128)S(1)}, f32[16,8,128]{2,1,0:T(8,128)S(1)}, f32[16,8,128]{2,1,0:T(8,128)S(1)}, f32[16,8,128]{2,1,0:T(8,128)S(1)}, f32...) custom-call(f32[64,512]{1,0:T(8,128)S(1)} %bitcast.20, f32[8,128,128]{2,1,0:T(8,128)S(1)} %shard_map.60.refs_0_, ...), custom_call_target="tpu_custom_call" | custom-call | flops 1879048192 | bytes 4194304 | tf_op jit(solution)/shard_map/pallas_call | solution.py:143
  135.1 1.8 shard_map.55.refs_0_
  138.1 2.7 %shard_map.64 = (f32[64,8,128]{2,1,0:T(8,128)S(1)}, f32[16,8,128]{2,1,0:T(8,128)S(1)}, f32[16,8,128]{2,1,0:T(8,128)S(1)}, f32[16,8,128]{2,1,0:T(8,128)S(1)}, f32...) custom-call(f32[64,512]{1,0:T(8,128)S(1)} %bitcast.21, f32[8,128,128]{2,1,0:T(8,128)S(1)} %shard_map.55.refs_0_, ...), custom_call_target="tpu_custom_call" | custom-call | flops 1879048192 | bytes 4194304 | tf_op jit(solution)/shard_map/pallas_call | solution.py:143
  142.6 1.4 shard_map.54.refs_0_
  144.0 3.2 %convolution_bitcast_fusion.rest = f32[32,64]{1,0:T(8,128)} fusion(f32[16,32,256]{2,1,0:T(8,128)} %collective-permute-done.21, f32[16,32,128]{2,1,0:T(8,128)} %copy-done.16, f32[16,32,128]{2,1,0:T(8,128)} %copy-done.17, pred[]{:T(512)S(6)} %eq.4), kind=kOutput, calls=%fused_computation.1 | convolution fusion | flops 102105088 | bytes 1056769 | tf_op jit(solution)/shard_map/rps,rqs->pq/dot_general | solution.py:347
  147.3 6.0 %collective-permute-done.19.refs_2_ = f32[8,128,128]{2,1,0:T(8,128)S(1)} collective-permute-done((f32[8,128,128]{2,1,0:T(8,128)}, f32[8,128,128]{2,1,0:T(8,128)S(1)}, u32[]{:S(2)}, u32[]{:S(2)}) %collective-permute-start.19) | collective-permute-done | bytes 524320 | tf_op jit(solution)/shard_map/ppermute | solution.py:19
  153.3 4.4 %shard_map.66 = (f32[64,8,128]{2,1,0:T(8,128)S(1)}, f32[16,8,128]{2,1,0:T(8,128)S(1)}, f32[16,8,128]{2,1,0:T(8,128)S(1)}, f32[16,8,128]{2,1,0:T(8,128)S(1)}, f32...) custom-call(f32[64,512]{1,0:T(8,128)S(1)} %bitcast.22, ...), custom_call_target="tpu_custom_call" | custom-call | flops 1879048192 | bytes 4194304 | tf_op jit(solution)/shard_map/pallas_call | solution.py:143
  159.2 2.9 %shard_map.67.part = f32[32,56]{1,0:T(8,128)} custom-call(f32[64,8,128]{2,1,0:T(8,128)} %copy-done.1, f32[64,8,128]{2,1,0:T(8,128)} %copy-done.2, f32[64,8,128]{2,1,0:T(8,128)} %copy-done.3, f32[64,8,128]{2,1,0:T(8,128)} %copy-done.4, f32[64,8,128]{2,1,0:T(8,128)} %copy-done.19, f32[64,8,128]{2,1,0:T(8,128)} %collective-permute-done.23.refs_5_, ...), custom_call_target="tpu_custom_call" | custom-call | tf_op jit(solution)/shard_map/pallas_call | solution.py:183
  163.0 3.1 %shard_map.68 = (f32[72,512]{1,0:T(8,128)}, f32[72,512]{1,0:T(8,128)}, f32[72,512]{1,0:T(8,128)}, f32[72,512]{1,0:T(8,128)}) custom-call(f32[4,64,512]{2,1,0:T(8,128)} %copy-done.5, f32[4,64,512]{2,1,0:T(8,128)} %copy-done.18, f32[64,8,128]{2,1,0:T(8,128)} %copy-done.20, f32[32,56]{1,0:T(8,128)} %shard_map.67.part, f32[32,64]{1,0:T(8,128)} %convolution_bitcast_fusion.rest, ...), custom_call_target="tpu_custom_call" | custom-call | tf_op jit(solution)/shard_map/pallas_call | solution.py:209
  167.8 1.8 collective-permute-start.27
  169.9 4.0 %collective-permute-done.29 = f32[72,512]{1,0:T(8,128)S(1)} collective-permute-done((f32[72,512]{1,0:T(8,128)}, f32[72,512]{1,0:T(8,128)S(1)}, u32[]{:S(2)}, u32[]{:S(2)}) %collective-permute-start.29) | collective-permute-done | bytes 147488 | tf_op jit(solution)/shard_map/ppermute | solution.py:19
  173.9 1.5 collective-permute-done.28
  178.9 1.7 collective-permute-start.35
  180.6 1.8 collective-permute-done.30
  182.4 2.3 %collective-permute-start.31 = (f32[72,512]{1,0:T(8,128)S(1)}, f32[72,512]{1,0:T(8,128)S(1)}, u32[]{:S(2)}, u32[]{:S(2)}) collective-permute-start(f32[72,512]{1,0:T(8,128)S(1)} %add.49), channel_id=1, source_target_pairs={{0,16},{8,24},{16,0},{24,8},{1,17},{9,25},{17,1},{25,9},{2,18},{10... | collective-permute-start | bytes 442376 | tf_op jit(solution)/shard_map/ppermute | solution.py:19
  184.7 6.0 %collective-permute-done.34.refs_13_ = f32[16,32,128]{2,1,0:T(8,128)S(1)} collective-permute-done((f32[16,32,128]{2,1,0:T(8,128)S(1)}, f32[16,32,128]{2,1,0:T(8,128)S(1)}, u32[]{:S(2)}, u32[]{:S(2)}) %collective-permute-start.34) | collective-permute-done | bytes 262176 | tf_op jit(solution)/shard_map/ppermute | solution.py:19
  (115 shorter events, 28.1 us)
Async XLA Ops:
  0.6 44.7 %copy-start = (f32[512,64]{0,1:T(8,128)S(1)}, f32[512,64]{0,1:T(8,128)}, u32[]{:S(2)}) copy-start(f32[512,64]{0,1:T(8,128)} %param.3) | copy-start | bytes 393220
  3.6 15.8 %collective-permute-start = (f32[8,128,128]{2,1,0:T(8,128)S(1)}, f32[8,128,128]{2,1,0:T(8,128)S(1)}, u32[]{:S(2)}, u32[]{:S(2)}) collective-permute-start(f32[8,128,128]{2,1,0:T(8,128)S(1)} %get-tuple-element.97), channel_id=1, source_target_pairs={{0,2},{2,0},{4,6},{6,4},{1,3},{3,1},{5,7},{7,5},{8,10},{10,8},{12,... | collective-permute-start | bytes 1572872 | tf_op jit(solution)/shard_map/ppermute | solution.py:19
  6.6 25.4 %collective-permute-start.1 = (f32[8,128,128]{2,1,0:T(8,128)}, f32[8,128,128]{2,1,0:T(8,128)S(1)}, u32[]{:S(2)}, u32[]{:S(2)}) collective-permute-start(f32[8,128,128]{2,1,0:T(8,128)} %get-tuple-element.98), channel_id=1, source_target_pairs={{0,4},{2,6},{4,0},{6,2},{1,5},{3,7},{5,1},{7,3},{8,12},{10,14},{12... | collective-permute-start | bytes 1572872 | tf_op jit(solution)/shard_map/ppermute | solution.py:19
  8.1 27.9 %collective-permute-start.2 = (f32[8,128,128]{2,1,0:T(8,128)}, f32[8,128,128]{2,1,0:T(8,128)S(1)}, u32[]{:S(2)}, u32[]{:S(2)}) collective-permute-start(f32[8,128,128]{2,1,0:T(8,128)} %get-tuple-element.99), channel_id=1, source_target_pairs={{0,6},{2,4},{4,2},{6,0},{1,7},{3,5},{5,3},{7,1},{8,14},{10,12},{12... | collective-permute-start | bytes 1572872 | tf_op jit(solution)/shard_map/ppermute | solution.py:19
  11.0 30.8 %collective-permute-start.3 = (f32[8,128,128]{2,1,0:T(8,128)S(1)}, f32[8,128,128]{2,1,0:T(8,128)S(1)}, u32[]{:S(2)}, u32[]{:S(2)}) collective-permute-start(f32[8,128,128]{2,1,0:T(8,128)S(1)} %get-tuple-element.101), channel_id=1, source_target_pairs={{0,2},{2,0},{4,6},{6,4},{1,3},{3,1},{5,7},{7,5},{8,10},{10,8},{12,... | collective-permute-start | bytes 1572872 | tf_op jit(solution)/shard_map/ppermute | solution.py:19
  19.3 24.6 %copy-start.6 = (f32[8,128,128]{2,1,0:T(8,128)}, f32[8,128,128]{2,1,0:T(8,128)S(1)}, u32[]{:S(2)}) copy-start(f32[8,128,128]{2,1,0:T(8,128)S(1)} %collective-permute-done.refs_1_) | copy-start | bytes 1572868
  19.3 35.2 %collective-permute-start.4 = (f32[8,128,128]{2,1,0:T(8,128)}, f32[8,128,128]{2,1,0:T(8,128)S(1)}, u32[]{:S(2)}, u32[]{:S(2)}) collective-permute-start(f32[8,128,128]{2,1,0:T(8,128)} %get-tuple-element.112), channel_id=1, source_target_pairs={{0,4},{2,6},{4,0},{6,2},{1,5},{3,7},{5,1},{7,3},{8,12},{10,14},{12... | collective-permute-start | bytes 1572872 | tf_op jit(solution)/shard_map/ppermute | solution.py:19
  32.0 11.9 %copy-start.8 = (f32[8,128,128]{2,1,0:T(8,128)}, f32[8,128,128]{2,1,0:T(8,128)S(1)}, u32[]{:S(2)}) copy-start(f32[8,128,128]{2,1,0:T(8,128)S(1)} %collective-permute-done.1.refs_2_) | copy-start | bytes 1572868
  32.0 23.3 %collective-permute-start.5 = (f32[8,128,128]{2,1,0:T(8,128)}, f32[8,128,128]{2,1,0:T(8,128)}, u32[]{:S(2)}, u32[]{:S(2)}) collective-permute-start(f32[8,128,128]{2,1,0:T(8,128)} %get-tuple-element.113), channel_id=1, source_target_pairs={{0,6},{2,4},{4,2},{6,0},{1,7},{3,5},{5,3},{7,1},{8,14},{10,12},{12... | collective-permute-start | bytes 1572872 | tf_op jit(solution)/shard_map/ppermute | solution.py:19
  36.8 27.8 %collective-permute-start.15 = (f32[8,128,128]{2,1,0:T(8,128)}, f32[8,128,128]{2,1,0:T(8,128)S(1)}, u32[]{:S(2)}, u32[]{:S(2)}) collective-permute-start(f32[8,128,128]{2,1,0:T(8,128)} %get-tuple-element.135), channel_id=1, source_target_pairs={{0,2},{2,0},{4,6},{6,4},{1,3},{3,1},{5,7},{7,5},{8,10},{10,8},{12,... | collective-permute-start | bytes 1572872 | tf_op jit(solution)/shard_map/ppermute | solution.py:19
  41.8 33.7 %collective-permute-start.6 = (f32[8,128,128]{2,1,0:T(8,128)}, f32[8,128,128]{2,1,0:T(8,128)S(1)}, u32[]{:S(2)}, u32[]{:S(2)}) collective-permute-start(f32[8,128,128]{2,1,0:T(8,128)} %get-tuple-element.116), channel_id=1, source_target_pairs={{0,4},{2,6},{4,0},{6,2},{1,5},{3,7},{5,1},{7,3},{8,12},{10,14},{12... | collective-permute-start | bytes 1572872 | tf_op jit(solution)/shard_map/ppermute | solution.py:19
  45.9 12.4 %copy-start.7 = (f32[8,128,128]{2,1,0:T(8,128)S(1)}, f32[8,128,128]{2,1,0:T(8,128)}, u32[]{:S(2)}) copy-start(f32[8,128,128]{2,1,0:T(8,128)} %copy-done.6) | copy-start | bytes 1572868
  45.9 12.4 %copy-start.9 = (f32[8,128,128]{2,1,0:T(8,128)S(1)}, f32[8,128,128]{2,1,0:T(8,128)}, u32[]{:S(2)}) copy-start(f32[8,128,128]{2,1,0:T(8,128)} %copy-done.8) | copy-start | bytes 1572868
  45.9 12.4 %copy-start.11 = (f32[8,128,128]{2,1,0:T(8,128)S(1)}, f32[8,128,128]{2,1,0:T(8,128)}, u32[]{:S(2)}) copy-start(f32[8,128,128]{2,1,0:T(8,128)} %copy-done.10) | copy-start | bytes 1572868
  54.5 27.9 %collective-permute-start.10 = (f32[8,128,128]{2,1,0:T(8,128)}, f32[8,128,128]{2,1,0:T(8,128)S(1)}, u32[]{:S(2)}, u32[]{:S(2)}) collective-permute-start(f32[8,128,128]{2,1,0:T(8,128)} %get-tuple-element.127), channel_id=1, source_target_pairs={{0,6},{2,4},{4,2},{6,0},{1,7},{3,5},{5,3},{7,1},{8,14},{10,12},{12... | collective-permute-start | bytes 1572872 | tf_op jit(solution)/shard_map/ppermute | solution.py:19
  55.4 31.5 %collective-permute-start.9 = (f32[8,128,128]{2,1,0:T(8,128)S(1)}, f32[8,128,128]{2,1,0:T(8,128)S(1)}, u32[]{:S(2)}, u32[]{:S(2)}) collective-permute-start(f32[8,128,128]{2,1,0:T(8,128)S(1)} %get-tuple-element.120), channel_id=1, source_target_pairs={{0,2},{2,0},{4,6},{6,4},{1,3},{3,1},{5,7},{7,5},{8,10},{10,8},{12,... | collective-permute-start | bytes 1572872 | tf_op jit(solution)/shard_map/ppermute | solution.py:19
  61.8 13.8 %copy-start.21 = (f32[8,128,128]{2,1,0:T(8,128)S(1)}, f32[8,128,128]{2,1,0:T(8,128)}, u32[]{:S(2)}) copy-start(f32[8,128,128]{2,1,0:T(8,128)} %get-tuple-element.117) | copy-start | bytes 1572868
  75.5 29.3 %collective-permute-start.7 = (f32[8,128,128]{2,1,0:T(8,128)S(1)}, f32[8,128,128]{2,1,0:T(8,128)S(1)}, u32[]{:S(2)}, u32[]{:S(2)}) collective-permute-start(f32[8,128,128]{2,1,0:T(8,128)S(1)} %copy-done.21), channel_id=1, source_target_pairs={{0,6},{2,4},{4,2},{6,0},{1,7},{3,5},{5,3},{7,1},{8,14},{10,12},{12... | collective-permute-start | bytes 1572872 | tf_op jit(solution)/shard_map/ppermute | solution.py:19
  77.1 24.4 %collective-permute-start.16 = (f32[8,128,128]{2,1,0:T(8,128)}, f32[8,128,128]{2,1,0:T(8,128)S(1)}, u32[]{:S(2)}, u32[]{:S(2)}) collective-permute-start(f32[8,128,128]{2,1,0:T(8,128)} %get-tuple-element.137), channel_id=1, source_target_pairs={{0,4},{2,6},{4,0},{6,2},{1,5},{3,7},{5,1},{7,3},{8,12},{10,14},{12... | collective-permute-start | bytes 1572872 | tf_op jit(solution)/shard_map/ppermute | solution.py:19
  82.4 23.0 %collective-permute-start.11 = (f32[16,16,128]{2,1,0:T(8,128)S(1)}, f32[16,16,128]{2,1,0:T(8,128)S(1)}, u32[]{:S(2)}, u32[]{:S(2)}) collective-permute-start(f32[16,16,128]{2,1,0:T(8,128)S(1)} %pad_maximum_fusion.5), channel_id=1, source_target_pairs={{0,2},{2,0},{4,6},{6,4},{1,3},{3,1},{5,7},{7,5},{8,10},{10,8},{12,... | collective-permute-start | bytes 393224 | tf_op jit(solution)/shard_map/ppermute | solution.py:19
  86.9 18.5 %collective-permute-start.13 = (f32[16,16,128]{2,1,0:T(8,128)S(1)}, f32[16,16,128]{2,1,0:T(8,128)S(1)}, u32[]{:S(2)}, u32[]{:S(2)}) collective-permute-start(f32[16,16,128]{2,1,0:T(8,128)S(1)} %pad_maximum_fusion.6), channel_id=1, source_target_pairs={{0,4},{2,6},{4,0},{6,2},{1,5},{3,7},{5,1},{7,3},{8,12},{10,14},{12... | collective-permute-start | bytes 393224 | tf_op jit(solution)/shard_map/ppermute | solution.py:19
  101.5 7.7 %collective-permute-start.17 = (f32[16,16,128]{2,1,0:T(8,128)S(1)}, f32[16,16,128]{2,1,0:T(8,128)S(1)}, u32[]{:S(2)}, u32[]{:S(2)}) collective-permute-start(f32[16,16,128]{2,1,0:T(8,128)S(1)} %pad_maximum_fusion.7), channel_id=1, source_target_pairs={{0,6},{2,4},{4,2},{6,0},{1,7},{3,5},{5,3},{7,1},{8,14},{10,12},{12... | collective-permute-start | bytes 393224 | tf_op jit(solution)/shard_map/ppermute | solution.py:19
  104.8 15.0 %collective-permute-start.8 = (f32[8,128,128]{2,1,0:T(8,128)S(1)}, f32[8,128,128]{2,1,0:T(8,128)S(1)}, u32[]{:S(2)}, u32[]{:S(2)}) collective-permute-start(f32[8,128,128]{2,1,0:T(8,128)S(1)} %get-tuple-element.118), channel_id=1, source_target_pairs={{0,2},{2,0},{4,6},{6,4},{1,3},{3,1},{5,7},{7,5},{8,10},{10,8},{12,... | collective-permute-start | bytes 1572872 | tf_op jit(solution)/shard_map/ppermute | solution.py:19
  105.4 26.6 %collective-permute-start.14 = (f32[8,128,128]{2,1,0:T(8,128)}, f32[8,128,128]{2,1,0:T(8,128)S(1)}, u32[]{:S(2)}, u32[]{:S(2)}) collective-permute-start(f32[8,128,128]{2,1,0:T(8,128)} %get-tuple-element.134), channel_id=1, source_target_pairs={{0,6},{2,4},{4,2},{6,0},{1,7},{3,5},{5,3},{7,1},{8,14},{10,12},{12... | collective-permute-start | bytes 1572872 | tf_op jit(solution)/shard_map/ppermute | solution.py:19
  108.0 21.1 %collective-permute-start.12 = (f32[8,128,128]{2,1,0:T(8,128)}, f32[8,128,128]{2,1,0:T(8,128)S(1)}, u32[]{:S(2)}, u32[]{:S(2)}) collective-permute-start(f32[8,128,128]{2,1,0:T(8,128)} %get-tuple-element.129), channel_id=1, source_target_pairs={{0,4},{2,6},{4,0},{6,2},{1,5},{3,7},{5,1},{7,3},{8,12},{10,14},{12... | collective-permute-start | bytes 1572872 | tf_op jit(solution)/shard_map/ppermute | solution.py:19
  110.1 31.7 %collective-permute-start.21 = (f32[16,32,256]{2,1,0:T(8,128)}, f32[16,32,256]{2,1,0:T(8,128)}, u32[]{:S(2)}, u32[]{:S(2)}) collective-permute-start(f32[16,32,256]{2,1,0:T(8,128)} %pad_maximum_fusion), channel_id=1, source_target_pairs={{0,1},{1,0},{2,3},{3,2},{4,5},{5,4},{6,7},{7,6},{8,9},{9,8},{10,11... | collective-permute-start | bytes 1572872 | tf_op jit(solution)/shard_map/ppermute | solution.py:19
  113.1 23.8 %copy-start.1 = (f32[64,8,128]{2,1,0:T(8,128)}, f32[64,8,128]{2,1,0:T(8,128)S(1)}, u32[]{:S(2)}) copy-start(f32[64,8,128]{2,1,0:T(8,128)S(1)} %get-tuple-element.155.refs_0_) | copy-start | bytes 786436
  113.2 28.7 %collective-permute-start.22 = (f32[64,8,128]{2,1,0:T(8,128)S(1)}, f32[64,8,128]{2,1,0:T(8,128)S(1)}, u32[]{:S(2)}, u32[]{:S(2)}) collective-permute-start(f32[64,8,128]{2,1,0:T(8,128)S(1)} %get-tuple-element.155.refs_0_), channel_id=1, source_target_pairs={{0,1},{1,0},{2,3},{3,2},{4,5},{5,4},{6,7},{7,6},{8,9},{9,8},{10,11... | collective-permute-start | bytes 786440 | tf_op jit(solution)/shard_map/ppermute | solution.py:19
  119.8 27.4 %collective-permute-start.18 = (f32[8,128,128]{2,1,0:T(8,128)}, f32[8,128,128]{2,1,0:T(8,128)S(1)}, u32[]{:S(2)}, u32[]{:S(2)}) collective-permute-start(f32[8,128,128]{2,1,0:T(8,128)} %get-tuple-element.148), channel_id=1, source_target_pairs={{0,2},{2,0},{4,6},{6,4},{1,3},{3,1},{5,7},{7,5},{8,10},{10,8},{12,... | collective-permute-start | bytes 1572872 | tf_op jit(solution)/shard_map/ppermute | solution.py:19
  129.1 24.2 %collective-permute-start.19 = (f32[8,128,128]{2,1,0:T(8,128)}, f32[8,128,128]{2,1,0:T(8,128)S(1)}, u32[]{:S(2)}, u32[]{:S(2)}) collective-permute-start(f32[8,128,128]{2,1,0:T(8,128)} %get-tuple-element.150), channel_id=1, source_target_pairs={{0,4},{2,6},{4,0},{6,2},{1,5},{3,7},{5,1},{7,3},{8,12},{10,14},{12... | collective-permute-start | bytes 1572872 | tf_op jit(solution)/shard_map/ppermute | solution.py:19
  132.0 21.3 %collective-permute-start.20 = (f32[8,128,128]{2,1,0:T(8,128)}, f32[8,128,128]{2,1,0:T(8,128)}, u32[]{:S(2)}, u32[]{:S(2)}) collective-permute-start(f32[8,128,128]{2,1,0:T(8,128)} %get-tuple-element.152), channel_id=1, source_target_pairs={{0,6},{2,4},{4,2},{6,0},{1,7},{3,5},{5,3},{7,1},{8,14},{10,12},{12... | collective-permute-start | bytes 1572872 | tf_op jit(solution)/shard_map/ppermute | solution.py:19
  135.1 1.8 copy-start.14
  135.1 8.9 %copy-start.2 = (f32[64,8,128]{2,1,0:T(8,128)}, f32[64,8,128]{2,1,0:T(8,128)S(1)}, u32[]{:S(2)}) copy-start(f32[64,8,128]{2,1,0:T(8,128)S(1)} %get-tuple-element.156.refs_1_) | copy-start | bytes 786436
  141.9 17.2 %copy-start.3 = (f32[64,8,128]{2,1,0:T(8,128)}, f32[64,8,128]{2,1,0:T(8,128)S(1)}, u32[]{:S(2)}) copy-start(f32[64,8,128]{2,1,0:T(8,128)S(1)} %get-tuple-element.157.refs_2_) | copy-start | bytes 786436
  141.9 5.4 %collective-permute-start.23 = (f32[64,8,128]{2,1,0:T(8,128)S(1)}, f32[64,8,128]{2,1,0:T(8,128)}, u32[]{:S(2)}, u32[]{:S(2)}) collective-permute-start(f32[64,8,128]{2,1,0:T(8,128)S(1)} %get-tuple-element.156.refs_1_), channel_id=1, source_target_pairs={{0,1},{1,0},{2,3},{3,2},{4,5},{5,4},{6,7},{7,6},{8,9},{9,8},{10,11... | collective-permute-start | bytes 786440 | tf_op jit(solution)/shard_map/ppermute | solution.py:19
  142.6 4.7 %collective-permute-start.24 = (f32[64,8,128]{2,1,0:T(8,128)S(1)}, f32[64,8,128]{2,1,0:T(8,128)}, u32[]{:S(2)}, u32[]{:S(2)}) collective-permute-start(f32[64,8,128]{2,1,0:T(8,128)S(1)} %get-tuple-element.157.refs_2_), channel_id=1, source_target_pairs={{0,1},{1,0},{2,3},{3,2},{4,5},{5,4},{6,7},{7,6},{8,9},{9,8},{10,11... | collective-permute-start | bytes 786440 | tf_op jit(solution)/shard_map/ppermute | solution.py:19
  142.6 10.7 %copy-start.13 = (f32[512,512]{1,0:T(8,128)S(1)}, f32[512,512]{1,0:T(8,128)}, u32[]{:S(2)}) copy-start(f32[512,512]{1,0:T(8,128)} %copy-done.12) | copy-start | bytes 3145732
  158.5 3.6 %collective-permute-start.25 = (f32[4,64,512]{2,1,0:T(8,128)}, f32[4,64,512]{2,1,0:T(8,128)S(1)}, u32[]{:S(2)}, u32[]{:S(2)}) collective-permute-start(f32[4,64,512]{2,1,0:T(8,128)} %get-tuple-element.163), channel_id=1, source_target_pairs={{0,1},{1,0},{2,3},{3,2},{4,5},{5,4},{6,7},{7,6},{8,9},{9,8},{10,11... | collective-permute-start | bytes 1572872 | tf_op jit(solution)/shard_map/ppermute | solution.py:19
  158.5 3.6 %collective-permute-start.26 = (f32[64,8,128]{2,1,0:T(8,128)S(1)}, f32[64,8,128]{2,1,0:T(8,128)S(1)}, u32[]{:S(2)}, u32[]{:S(2)}) collective-permute-start(f32[64,8,128]{2,1,0:T(8,128)S(1)} %get-tuple-element.164.refs_3_), channel_id=1, source_target_pairs={{0,1},{1,0},{2,3},{3,2},{4,5},{5,4},{6,7},{7,6},{8,9},{9,8},{10,11... | collective-permute-start | bytes 786440 | tf_op jit(solution)/shard_map/ppermute | solution.py:19
  166.1 7.8 %collective-permute-start.29 = (f32[72,512]{1,0:T(8,128)}, f32[72,512]{1,0:T(8,128)S(1)}, u32[]{:S(2)}, u32[]{:S(2)}) collective-permute-start(f32[72,512]{1,0:T(8,128)} %get-tuple-element.171), channel_id=1, source_target_pairs={{0,6},{2,4},{4,2},{6,0},{1,7},{3,5},{5,3},{7,1},{8,14},{10,12},{12... | collective-permute-start | bytes 442376 | tf_op jit(solution)/shard_map/ppermute | solution.py:19
  166.7 8.7 %collective-permute-start.28 = (f32[72,512]{1,0:T(8,128)}, f32[72,512]{1,0:T(8,128)S(1)}, u32[]{:S(2)}, u32[]{:S(2)}) collective-permute-start(f32[72,512]{1,0:T(8,128)} %get-tuple-element.169), channel_id=1, source_target_pairs={{0,4},{2,6},{4,0},{6,2},{1,5},{3,7},{5,1},{7,3},{8,12},{10,14},{12... | collective-permute-start | bytes 442376 | tf_op jit(solution)/shard_map/ppermute | solution.py:19
  167.8 8.4 %collective-permute-start.27 = (f32[72,512]{1,0:T(8,128)}, f32[72,512]{1,0:T(8,128)S(1)}, u32[]{:S(2)}, u32[]{:S(2)}) collective-permute-start(f32[72,512]{1,0:T(8,128)} %get-tuple-element.167), channel_id=1, source_target_pairs={{0,2},{2,0},{4,6},{6,4},{1,3},{3,1},{5,7},{7,5},{8,10},{10,8},{12,... | collective-permute-start | bytes 442376 | tf_op jit(solution)/shard_map/ppermute | solution.py:19
  169.6 15.1 %collective-permute-start.33 = (f32[16,32,128]{2,1,0:T(8,128)S(1)}, f32[16,32,128]{2,1,0:T(8,128)S(1)}, u32[]{:S(2)}, u32[]{:S(2)}) collective-permute-start(f32[16,32,128]{2,1,0:T(8,128)S(1)} %pad_maximum_fusion.1), channel_id=1, source_target_pairs={{0,2},{2,0},{4,6},{6,4},{1,3},{3,1},{5,7},{7,5},{8,10},{10,8},{12,... | collective-permute-start | bytes 786440 | tf_op jit(solution)/shard_map/ppermute | solution.py:19
  177.2 5.2 %collective-permute-start.30 = (f32[72,512]{1,0:T(8,128)S(1)}, f32[72,512]{1,0:T(8,128)S(1)}, u32[]{:S(2)}, u32[]{:S(2)}) collective-permute-start(f32[72,512]{1,0:T(8,128)S(1)} %add_add_fusion), channel_id=1, source_target_pairs={{0,8},{8,0},{16,24},{24,16},{1,9},{9,1},{17,25},{25,17},{2,10},{10... | collective-permute-start | bytes 442376 | tf_op jit(solution)/shard_map/ppermute | solution.py:19
  178.5 12.3 %collective-permute-start.34 = (f32[16,32,128]{2,1,0:T(8,128)S(1)}, f32[16,32,128]{2,1,0:T(8,128)S(1)}, u32[]{:S(2)}, u32[]{:S(2)}) collective-permute-start(f32[16,32,128]{2,1,0:T(8,128)S(1)} %pad_maximum_fusion.2), channel_id=1, source_target_pairs={{0,4},{2,6},{4,0},{6,2},{1,5},{3,7},{5,1},{7,3},{8,12},{10,14},{12... | collective-permute-start | bytes 786440 | tf_op jit(solution)/shard_map/ppermute | solution.py:19
  178.9 11.9 %collective-permute-start.35 = (f32[16,32,128]{2,1,0:T(8,128)S(1)}, f32[16,32,128]{2,1,0:T(8,128)S(1)}, u32[]{:S(2)}, u32[]{:S(2)}) collective-permute-start(f32[16,32,128]{2,1,0:T(8,128)S(1)} %pad_maximum_fusion.3), channel_id=1, source_target_pairs={{0,6},{2,4},{4,2},{6,0},{1,7},{3,5},{5,3},{7,1},{8,14},{10,12},{12... | collective-permute-start | bytes 786440 | tf_op jit(solution)/shard_map/ppermute | solution.py:19
  182.4 9.6 %collective-permute-start.31 = (f32[72,512]{1,0:T(8,128)S(1)}, f32[72,512]{1,0:T(8,128)S(1)}, u32[]{:S(2)}, u32[]{:S(2)}) collective-permute-start(f32[72,512]{1,0:T(8,128)S(1)} %add.49), channel_id=1, source_target_pairs={{0,16},{8,24},{16,0},{24,8},{1,17},{9,25},{17,1},{25,9},{2,18},{10... | collective-permute-start | bytes 442376 | tf_op jit(solution)/shard_map/ppermute | solution.py:19
  192.1 1.4 collective-permute-start.32
  (10 other events, 8.7 us)

commit v3 on v2

--- a/solution.py
+++ b/solution.py
@@ -144,7 +144,7 @@
         functools.partial(chunk_kernel, n, first, last),
         out_shape=shapes,
         scratch_shapes=scratch,
-        compiler_params=pltpu.CompilerParams(vmem_limit_bytes=40 * 2**20),
+        compiler_params=pltpu.CompilerParams(vmem_limit_bytes=24 * 2**20),
         cost_estimate=pl.CostEstimate(
             flops=2 * steps * points * (3 * steps + 4 * rank),
             bytes_accessed=4 * steps * (points + 2 * steps),
@@ -183,6 +183,7 @@
     return pl.pallas_call(
         functools.partial(load_gram_kernel, len(own)),
         out_shape=jax.ShapeDtypeStruct((loads, both), jnp.float32),
+        compiler_params=pltpu.CompilerParams(vmem_limit_bytes=12 * 2**20),
     )(*own, *far)
 
 
@@ -209,6 +210,7 @@
     return pl.pallas_call(
         functools.partial(fold_kernel, n, len(own)),
         out_shape=[shape] * n,
+        compiler_params=pltpu.CompilerParams(vmem_limit_bytes=12 * 2**20),
     )(keep, got, far, part, rest, *own)
 
 
@@ -233,7 +235,7 @@
         grid=(1,),
         in_specs=specs,
         out_specs=pl.BlockSpec(shape, lambda i: (0, 0, 0)),
-        compiler_params=pltpu.CompilerParams(vmem_limit_bytes=16 * 2**20),
+        compiler_params=pltpu.CompilerParams(vmem_limit_bytes=8 * 2**20),
     )(*pieces)
 
 

time: 195 us -> 189 us (0.969)
  Pallas kernels: 54.1 us -> 49.8 us
    pallas_call x1, Pallas kernels: 3.09 us -> 0.63 us  [fold(): pl.pallas_call(functools.partial(fold_kernel, n, len(own)), out_shape=[sh...]
    pallas_call x1, Pallas kernels: 2.89 us -> 0.82 us  [load_gram(): pl.pallas_call(functools.partial(load_gram_kernel, len(own)), out_shape=j...]
    unnamed x44 -> x30, local copies, waits for them, and re-layouts: 5.69 us -> 5.11 us
  transfers between devices with their start and end apart: 36 -> 36, of which waited for: 18 -> 19; matrix products, arithmetic and copies ran while one was open for 3% -> 2% of each run, Pallas kernels for 23% -> 22%
where the time goes in v3:
time: 189 us; the launch traced here: 188 us
  waiting for transfers between devices  79 us (42%)
  Pallas kernels  49.8 us (26%)
  starting transfers between devices  47.9 us (25%)
  local copies, waits for them, and re-layouts  5.81 us (3%)
  other arithmetic  2.4 us (1%)
  matrix products  2.16 us (1%)
    ppermute x36, waiting for transfers between devices, swap(): return lax.ppermute(v, axis, xor_pairs(k, lax.axis_size(axis)))  79 us
    ppermute x36, starting transfers between devices, swap(): return lax.ppermute(v, axis, xor_pairs(k, lax.axis_size(axis)))  47.9 us
    pallas_call x12, Pallas kernels, pack(): pl.pallas_call(functools.partial(pack_kernel, shifts, corner), out_shape=...  26.3 us
    pallas_call x6, Pallas kernels, run_chunk(): pl.pallas_call(functools.partial(chunk_kernel, n, first, last), out_shape...  20.8 us
    unnamed x30, local copies, waits for them, and re-layouts  5.11 us
  transfers between devices with their start and end apart: 36, of which 19 were waited for; matrix products, arithmetic and copies ran while one was open for 2% of the time, Pallas kernels for 22%

profile of v3, /device:TPU:0, one launch (start us, length us, event | category | flops | bytes accessed | tf_op | source)
XLA Modules:
  0.0 188.3 jit_solution(14274679743466921711)
XLA Ops:
  0.6 2.9 %shard_map.49 = (f32[8,128,128]{2,1,0:T(8,128)S(1)}, f32[8,128,128]{2,1,0:T(8,128)}, f32[8,128,128]{2,1,0:T(8,128)}) custom-call(f32[128,32,768]{2,1,0:T(8,128)} %snapshots.12), custom_call_target="tpu_custom_call" | custom-call | bytes 3145728 | tf_op jit(solution)/shard_map/pallas_call | solution.py:66
  3.6 3.0 %collective-permute-start = (f32[8,128,128]{2,1,0:T(8,128)S(1)}, f32[8,128,128]{2,1,0:T(8,128)S(1)}, u32[]{:S(2)}, u32[]{:S(2)}) collective-permute-start(f32[8,128,128]{2,1,0:T(8,128)S(1)} %get-tuple-element.97), channel_id=1, source_target_pairs={{0,2},{2,0},{4,6},{6,4},{1,3},{3,1},{5,7},{7,5},{8,10},{10,8},{12,... | collective-permute-start | bytes 1572872 | tf_op jit(solution)/shard_map/ppermute | solution.py:19
  6.6 1.5 collective-permute-start.1
  8.1 2.9 %shard_map.50 = (f32[8,128,128]{2,1,0:T(8,128)S(1)}, f32[8,128,128]{2,1,0:T(8,128)}, f32[8,128,128]{2,1,0:T(8,128)}) custom-call(f32[128,32,768]{2,1,0:T(8,128)} %snapshots.12), custom_call_target="tpu_custom_call" | custom-call | bytes 3145728 | tf_op jit(solution)/shard_map/pallas_call | solution.py:66
  11.0 2.0 %collective-permute-start.3 = (f32[8,128,128]{2,1,0:T(8,128)S(1)}, f32[8,128,128]{2,1,0:T(8,128)S(1)}, u32[]{:S(2)}, u32[]{:S(2)}) collective-permute-start(f32[8,128,128]{2,1,0:T(8,128)S(1)} %get-tuple-element.101), channel_id=1, source_target_pairs={{0,2},{2,0},{4,6},{6,4},{1,3},{3,1},{5,7},{7,5},{8,10},{10,8},{12,... | collective-permute-start | bytes 1572872 | tf_op jit(solution)/shard_map/ppermute | solution.py:19
  13.0 6.3 %collective-permute-done.refs_1_ = f32[8,128,128]{2,1,0:T(8,128)S(1)} collective-permute-done((f32[8,128,128]{2,1,0:T(8,128)S(1)}, f32[8,128,128]{2,1,0:T(8,128)S(1)}, u32[]{:S(2)}, u32[]{:S(2)}) %collective-permute-start) | collective-permute-done | bytes 524320 | tf_op jit(solution)/shard_map/ppermute | solution.py:19
  19.3 2.1 %collective-permute-start.4 = (f32[8,128,128]{2,1,0:T(8,128)}, f32[8,128,128]{2,1,0:T(8,128)}, u32[]{:S(2)}, u32[]{:S(2)}) collective-permute-start(f32[8,128,128]{2,1,0:T(8,128)} %get-tuple-element.112), channel_id=1, source_target_pairs={{0,4},{2,6},{4,0},{6,2},{1,5},{3,7},{5,1},{7,3},{8,12},{10,14},{12... | collective-permute-start | bytes 1572872 | tf_op jit(solution)/shard_map/ppermute | solution.py:19
  21.4 10.6 %collective-permute-done.1.refs_2_ = f32[8,128,128]{2,1,0:T(8,128)S(1)} collective-permute-done((f32[8,128,128]{2,1,0:T(8,128)}, f32[8,128,128]{2,1,0:T(8,128)S(1)}, u32[]{:S(2)}, u32[]{:S(2)}) %collective-permute-start.1) | collective-permute-done | bytes 524320 | tf_op jit(solution)/shard_map/ppermute | solution.py:19
  32.9 3.0 %shard_map.51 = (f32[8,128,128]{2,1,0:T(8,128)}, f32[8,128,128]{2,1,0:T(8,128)}, f32[8,128,128]{2,1,0:T(8,128)}) custom-call(f32[128,32,768]{2,1,0:T(8,128)} %snapshots.12), custom_call_target="tpu_custom_call" | custom-call | bytes 3145728 | tf_op jit(solution)/shard_map/pallas_call | solution.py:66
  36.8 2.9 %collective-permute-start.15 = (f32[8,128,128]{2,1,0:T(8,128)}, f32[8,128,128]{2,1,0:T(8,128)S(1)}, u32[]{:S(2)}, u32[]{:S(2)}) collective-permute-start(f32[8,128,128]{2,1,0:T(8,128)} %get-tuple-element.135), channel_id=1, source_target_pairs={{0,2},{2,0},{4,6},{6,4},{1,3},{3,1},{5,7},{7,5},{8,10},{10,8},{12,... | collective-permute-start | bytes 1572872 | tf_op jit(solution)/shard_map/ppermute | solution.py:19
  39.7 2.1 %collective-permute-done.3.refs_1_ = f32[8,128,128]{2,1,0:T(8,128)S(1)} collective-permute-done((f32[8,128,128]{2,1,0:T(8,128)S(1)}, f32[8,128,128]{2,1,0:T(8,128)S(1)}, u32[]{:S(2)}, u32[]{:S(2)}) %collective-permute-start.3) | collective-permute-done | bytes 524320 | tf_op jit(solution)/shard_map/ppermute | solution.py:19
  41.8 2.1 %collective-permute-start.6 = (f32[8,128,128]{2,1,0:T(8,128)}, f32[8,128,128]{2,1,0:T(8,128)S(1)}, u32[]{:S(2)}, u32[]{:S(2)}) collective-permute-start(f32[8,128,128]{2,1,0:T(8,128)} %get-tuple-element.116), channel_id=1, source_target_pairs={{0,4},{2,6},{4,0},{6,2},{1,5},{3,7},{5,1},{7,3},{8,12},{10,14},{12... | collective-permute-start | bytes 1572872 | tf_op jit(solution)/shard_map/ppermute | solution.py:19
  45.9 2.9 %shard_map.52 = (f32[8,128,128]{2,1,0:T(8,128)S(1)}, f32[8,128,128]{2,1,0:T(8,128)}, f32[8,128,128]{2,1,0:T(8,128)}) custom-call(f32[128,32,768]{2,1,0:T(8,128)} %snapshots.12), custom_call_target="tpu_custom_call" | custom-call | bytes 3145728 | tf_op jit(solution)/shard_map/pallas_call | solution.py:66
  48.8 5.7 %collective-permute-done.4.refs_2_ = f32[8,128,128]{2,1,0:T(8,128)} collective-permute-done((f32[8,128,128]{2,1,0:T(8,128)}, f32[8,128,128]{2,1,0:T(8,128)}, u32[]{:S(2)}, u32[]{:S(2)}) %collective-permute-start.4) | collective-permute-done | bytes 524320 | tf_op jit(solution)/shard_map/ppermute | solution.py:19
  55.5 3.0 %collective-permute-start.9 = (f32[8,128,128]{2,1,0:T(8,128)S(1)}, f32[8,128,128]{2,1,0:T(8,128)S(1)}, u32[]{:S(2)}, u32[]{:S(2)}) collective-permute-start(f32[8,128,128]{2,1,0:T(8,128)S(1)} %get-tuple-element.120), channel_id=1, source_target_pairs={{0,2},{2,0},{4,6},{6,4},{1,3},{3,1},{5,7},{7,5},{8,10},{10,8},{12,... | collective-permute-start | bytes 1572872 | tf_op jit(solution)/shard_map/ppermute | solution.py:19
  60.5 3.4 %shard_map.57 = (f32[64,8,128]{2,1,0:T(8,128)}, f32[16,8,128]{2,1,0:T(8,128)S(1)}, f32[16,8,128]{2,1,0:T(8,128)S(1)}, f32[16,8,128]{2,1,0:T(8,128)S(1)}, f32[16,...) custom-call(f32[64,512]{1,0:T(8,128)S(1)} %bitcast.17, f32[8,128,128]{2,1,0:T(8,128)S(1)} %shard_map.56.refs_0_, ...), custom_call_target="tpu_custom_call" | custom-call | flops 1879048192 | bytes 4194304 | tf_op jit(solution)/shard_map/pallas_call | solution.py:143
  64.0 1.4 shard_map.58.refs_0_
  66.8 8.7 %collective-permute-done.6.refs_2_ = f32[8,128,128]{2,1,0:T(8,128)S(1)} collective-permute-done((f32[8,128,128]{2,1,0:T(8,128)}, f32[8,128,128]{2,1,0:T(8,128)S(1)}, u32[]{:S(2)}, u32[]{:S(2)}) %collective-permute-start.6) | collective-permute-done | bytes 524320 | tf_op jit(solution)/shard_map/ppermute | solution.py:19
  75.5 1.5 collective-permute-start.7
  77.9 4.6 %shard_map.59 = (f32[64,8,128]{2,1,0:T(8,128)}, f32[16,8,128]{2,1,0:T(8,128)S(1)}, f32[16,8,128]{2,1,0:T(8,128)S(1)}, f32[16,8,128]{2,1,0:T(8,128)S(1)}, f32[16,...) custom-call(f32[64,512]{1,0:T(8,128)S(1)} %bitcast.18, f32[8,128,128]{2,1,0:T(8,128)S(1)} %shard_map.58.refs_0_, ...), custom_call_target="tpu_custom_call" | custom-call | flops 1879048192 | bytes 4194304 | tf_op jit(solution)/shard_map/pallas_call | solution.py:143
  82.6 1.5 collective-permute-start.11
  84.1 2.8 %collective-permute-done.9.refs_1_ = f32[8,128,128]{2,1,0:T(8,128)S(1)} collective-permute-done((f32[8,128,128]{2,1,0:T(8,128)S(1)}, f32[8,128,128]{2,1,0:T(8,128)S(1)}, u32[]{:S(2)}, u32[]{:S(2)}) %collective-permute-start.9) | collective-permute-done | bytes 524320 | tf_op jit(solution)/shard_map/ppermute | solution.py:19
  86.9 2.1 %collective-permute-start.13 = (f32[16,16,128]{2,1,0:T(8,128)S(1)}, f32[16,16,128]{2,1,0:T(8,128)S(1)}, u32[]{:S(2)}, u32[]{:S(2)}) collective-permute-start(f32[16,16,128]{2,1,0:T(8,128)S(1)} %pad_maximum_fusion.6), channel_id=1, source_target_pairs={{0,4},{2,6},{4,0},{6,2},{1,5},{3,7},{5,1},{7,3},{8,12},{10,14},{12... | collective-permute-start | bytes 393224 | tf_op jit(solution)/shard_map/ppermute | solution.py:19
  89.0 1.3 shard_map.60.refs_0_
  90.3 2.9 %shard_map.53 = (f32[8,128,128]{2,1,0:T(8,128)S(1)}, f32[8,128,128]{2,1,0:T(8,128)}, f32[8,128,128]{2,1,0:T(8,128)}) custom-call(f32[128,32,768]{2,1,0:T(8,128)} %snapshots.12), custom_call_target="tpu_custom_call" | custom-call | bytes 3145728 | tf_op jit(solution)/shard_map/pallas_call | solution.py:66
  93.3 8.0 %collective-permute-done.16.refs_2_ = f32[8,128,128]{2,1,0:T(8,128)S(1)} collective-permute-done((f32[8,128,128]{2,1,0:T(8,128)S(1)}, f32[8,128,128]{2,1,0:T(8,128)S(1)}, u32[]{:S(2)}, u32[]{:S(2)}) %collective-permute-start.16) | collective-permute-done | bytes 524320 | tf_op jit(solution)/shard_map/ppermute | solution.py:19
  101.3 3.3 %collective-permute-start.17 = (f32[16,16,128]{2,1,0:T(8,128)S(1)}, f32[16,16,128]{2,1,0:T(8,128)S(1)}, u32[]{:S(2)}, u32[]{:S(2)}) collective-permute-start(f32[16,16,128]{2,1,0:T(8,128)S(1)} %pad_maximum_fusion.7), channel_id=1, source_target_pairs={{0,6},{2,4},{4,2},{6,0},{1,7},{3,5},{5,3},{7,1},{8,14},{10,12},{12... | collective-permute-start | bytes 393224 | tf_op jit(solution)/shard_map/ppermute | solution.py:19
  105.2 2.6 %collective-permute-start.14 = (f32[8,128,128]{2,1,0:T(8,128)}, f32[8,128,128]{2,1,0:T(8,128)S(1)}, u32[]{:S(2)}, u32[]{:S(2)}) collective-permute-start(f32[8,128,128]{2,1,0:T(8,128)} %get-tuple-element.134), channel_id=1, source_target_pairs={{0,6},{2,4},{4,2},{6,0},{1,7},{3,5},{5,3},{7,1},{8,14},{10,12},{12... | collective-permute-start | bytes 1572872 | tf_op jit(solution)/shard_map/ppermute | solution.py:19
  109.9 2.9 %shard_map.62 = (f32[64,8,128]{2,1,0:T(8,128)S(1)}, f32[16,8,128]{2,1,0:T(8,128)S(1)}, f32[16,8,128]{2,1,0:T(8,128)S(1)}, f32[16,8,128]{2,1,0:T(8,128)S(1)}, f32...) custom-call(f32[64,512]{1,0:T(8,128)S(1)} %bitcast.19, f32[8,128,128]{2,1,0:T(8,128)S(1)} %shard_map.61.refs_0_, ...), custom_call_target="tpu_custom_call" | custom-call | flops 1879048192 | bytes 4194304 | tf_op jit(solution)/shard_map/pallas_call | solution.py:143
  113.4 3.1 %shard_map.65 = (f32[8,128,128]{2,1,0:T(8,128)}, f32[8,128,128]{2,1,0:T(8,128)}, f32[8,128,128]{2,1,0:T(8,128)}) custom-call(f32[128,32,768]{2,1,0:T(8,128)} %snapshots.12), custom_call_target="tpu_custom_call" | custom-call | bytes 3145728 | tf_op jit(solution)/shard_map/pallas_call | solution.py:66
  116.5 3.4 %collective-permute-done.8.refs_1_ = f32[8,128,128]{2,1,0:T(8,128)S(1)} collective-permute-done((f32[8,128,128]{2,1,0:T(8,128)S(1)}, f32[8,128,128]{2,1,0:T(8,128)S(1)}, u32[]{:S(2)}, u32[]{:S(2)}) %collective-permute-start.8) | collective-permute-done | bytes 524320 | tf_op jit(solution)/shard_map/ppermute | solution.py:19
  119.8 1.7 collective-permute-start.18
  121.6 7.4 %collective-permute-done.12.refs_2_ = f32[8,128,128]{2,1,0:T(8,128)S(1)} collective-permute-done((f32[8,128,128]{2,1,0:T(8,128)}, f32[8,128,128]{2,1,0:T(8,128)S(1)}, u32[]{:S(2)}, u32[]{:S(2)}) %collective-permute-start.12) | collective-permute-done | bytes 524320 | tf_op jit(solution)/shard_map/ppermute | solution.py:19
  129.0 2.4 %collective-permute-start.19 = (f32[8,128,128]{2,1,0:T(8,128)}, f32[8,128,128]{2,1,0:T(8,128)}, u32[]{:S(2)}, u32[]{:S(2)}) collective-permute-start(f32[8,128,128]{2,1,0:T(8,128)} %get-tuple-element.150), channel_id=1, source_target_pairs={{0,4},{2,6},{4,0},{6,2},{1,5},{3,7},{5,1},{7,3},{8,12},{10,14},{12... | collective-permute-start | bytes 1572872 | tf_op jit(solution)/shard_map/ppermute | solution.py:19
  132.6 2.7 %shard_map.63 = (f32[64,8,128]{2,1,0:T(8,128)S(1)}, f32[16,8,128]{2,1,0:T(8,128)S(1)}, f32[16,8,128]{2,1,0:T(8,128)S(1)}, f32[16,8,128]{2,1,0:T(8,128)S(1)}, f32...) custom-call(f32[64,512]{1,0:T(8,128)S(1)} %bitcast.20, f32[8,128,128]{2,1,0:T(8,128)S(1)} %shard_map.60.refs_0_, ...), custom_call_target="tpu_custom_call" | custom-call | flops 1879048192 | bytes 4194304 | tf_op jit(solution)/shard_map/pallas_call | solution.py:143
  135.4 1.7 shard_map.55.refs_0_
  138.3 2.7 %shard_map.64 = (f32[64,8,128]{2,1,0:T(8,128)S(1)}, f32[16,8,128]{2,1,0:T(8,128)S(1)}, f32[16,8,128]{2,1,0:T(8,128)S(1)}, f32[16,8,128]{2,1,0:T(8,128)S(1)}, f32...) custom-call(f32[64,512]{1,0:T(8,128)S(1)} %bitcast.21, f32[8,128,128]{2,1,0:T(8,128)S(1)} %shard_map.55.refs_0_, ...), custom_call_target="tpu_custom_call" | custom-call | flops 1879048192 | bytes 4194304 | tf_op jit(solution)/shard_map/pallas_call | solution.py:143
  142.6 1.4 shard_map.54.refs_0_
  144.0 2.2 %convolution_bitcast_fusion.rest = f32[32,64]{1,0:T(8,128)S(1)} fusion(f32[16,32,256]{2,1,0:T(8,128)} %collective-permute-done.21, f32[16,32,128]{2,1,0:T(8,128)S(1)} %get-tuple-element.193, f32[16,32,128]{2,1,0:T(8,128)S(1)} %copy-done.12, pred[]{:T(512)S(6)} %eq.4), kind=kOutput, calls=%fused_computation.1 | convolution fusion | flops 102105088 | bytes 1056769 | tf_op jit(solution)/shard_map/rps,rqs->pq/dot_general | solution.py:349
  146.2 7.1 %collective-permute-done.19.refs_2_ = f32[8,128,128]{2,1,0:T(8,128)} collective-permute-done((f32[8,128,128]{2,1,0:T(8,128)}, f32[8,128,128]{2,1,0:T(8,128)}, u32[]{:S(2)}, u32[]{:S(2)}) %collective-permute-start.19) | collective-permute-done | bytes 524320 | tf_op jit(solution)/shard_map/ppermute | solution.py:19
  153.3 4.4 %shard_map.66 = (f32[64,8,128]{2,1,0:T(8,128)S(1)}, f32[16,8,128]{2,1,0:T(8,128)S(1)}, f32[16,8,128]{2,1,0:T(8,128)S(1)}, f32[16,8,128]{2,1,0:T(8,128)S(1)}, f32...) custom-call(f32[64,512]{1,0:T(8,128)S(1)} %bitcast.22, ...), custom_call_target="tpu_custom_call" | custom-call | flops 1879048192 | bytes 4194304 | tf_op jit(solution)/shard_map/pallas_call | solution.py:143
  162.6 1.6 collective-permute-start.27
  164.7 3.6 %collective-permute-done.29 = f32[72,512]{1,0:T(8,128)S(1)} collective-permute-done((f32[72,512]{1,0:T(8,128)S(1)}, f32[72,512]{1,0:T(8,128)S(1)}, u32[]{:S(2)}, u32[]{:S(2)}) %collective-permute-start.29) | collective-permute-done | bytes 147488 | tf_op jit(solution)/shard_map/ppermute | solution.py:19
  168.3 1.9 %collective-permute-done.28 = f32[72,512]{1,0:T(8,128)S(1)} collective-permute-done((f32[72,512]{1,0:T(8,128)S(1)}, f32[72,512]{1,0:T(8,128)S(1)}, u32[]{:S(2)}, u32[]{:S(2)}) %collective-permute-start.28) | collective-permute-done | bytes 147488 | tf_op jit(solution)/shard_map/ppermute | solution.py:19
  172.8 1.7 collective-permute-start.35
  174.6 1.5 collective-permute-done.30
  176.1 2.3 %collective-permute-start.31 = (f32[72,512]{1,0:T(8,128)S(1)}, f32[72,512]{1,0:T(8,128)S(1)}, u32[]{:S(2)}, u32[]{:S(2)}) collective-permute-start(f32[72,512]{1,0:T(8,128)S(1)} %add.49), channel_id=1, source_target_pairs={{0,16},{8,24},{16,0},{24,8},{1,17},{9,25},{17,1},{25,9},{2,18},{10... | collective-permute-start | bytes 442376 | tf_op jit(solution)/shard_map/ppermute | solution.py:19
  178.3 6.4 %collective-permute-done.34.refs_13_ = f32[16,32,128]{2,1,0:T(8,128)S(1)} collective-permute-done((f32[16,32,128]{2,1,0:T(8,128)S(1)}, f32[16,32,128]{2,1,0:T(8,128)S(1)}, u32[]{:S(2)}, u32[]{:S(2)}) %collective-permute-start.34) | collective-permute-done | bytes 262176 | tf_op jit(solution)/shard_map/ppermute | solution.py:19
  (101 shorter events, 27.7 us)
Async XLA Ops:
  0.6 44.7 %copy-start = (f32[512,64]{0,1:T(8,128)S(1)}, f32[512,64]{0,1:T(8,128)}, u32[]{:S(2)}) copy-start(f32[512,64]{0,1:T(8,128)} %param.3) | copy-start | bytes 393220
  3.6 15.8 %collective-permute-start = (f32[8,128,128]{2,1,0:T(8,128)S(1)}, f32[8,128,128]{2,1,0:T(8,128)S(1)}, u32[]{:S(2)}, u32[]{:S(2)}) collective-permute-start(f32[8,128,128]{2,1,0:T(8,128)S(1)} %get-tuple-element.97), channel_id=1, source_target_pairs={{0,2},{2,0},{4,6},{6,4},{1,3},{3,1},{5,7},{7,5},{8,10},{10,8},{12,... | collective-permute-start | bytes 1572872 | tf_op jit(solution)/shard_map/ppermute | solution.py:19
  6.6 25.4 %collective-permute-start.1 = (f32[8,128,128]{2,1,0:T(8,128)}, f32[8,128,128]{2,1,0:T(8,128)S(1)}, u32[]{:S(2)}, u32[]{:S(2)}) collective-permute-start(f32[8,128,128]{2,1,0:T(8,128)} %get-tuple-element.98), channel_id=1, source_target_pairs={{0,4},{2,6},{4,0},{6,2},{1,5},{3,7},{5,1},{7,3},{8,12},{10,14},{12... | collective-permute-start | bytes 1572872 | tf_op jit(solution)/shard_map/ppermute | solution.py:19
  8.1 27.9 %collective-permute-start.2 = (f32[8,128,128]{2,1,0:T(8,128)}, f32[8,128,128]{2,1,0:T(8,128)S(1)}, u32[]{:S(2)}, u32[]{:S(2)}) collective-permute-start(f32[8,128,128]{2,1,0:T(8,128)} %get-tuple-element.99), channel_id=1, source_target_pairs={{0,6},{2,4},{4,2},{6,0},{1,7},{3,5},{5,3},{7,1},{8,14},{10,12},{12... | collective-permute-start | bytes 1572872 | tf_op jit(solution)/shard_map/ppermute | solution.py:19
  11.0 30.8 %collective-permute-start.3 = (f32[8,128,128]{2,1,0:T(8,128)S(1)}, f32[8,128,128]{2,1,0:T(8,128)S(1)}, u32[]{:S(2)}, u32[]{:S(2)}) collective-permute-start(f32[8,128,128]{2,1,0:T(8,128)S(1)} %get-tuple-element.101), channel_id=1, source_target_pairs={{0,2},{2,0},{4,6},{6,4},{1,3},{3,1},{5,7},{7,5},{8,10},{10,8},{12,... | collective-permute-start | bytes 1572872 | tf_op jit(solution)/shard_map/ppermute | solution.py:19
  19.3 24.6 %copy-start.1 = (f32[8,128,128]{2,1,0:T(8,128)}, f32[8,128,128]{2,1,0:T(8,128)S(1)}, u32[]{:S(2)}) copy-start(f32[8,128,128]{2,1,0:T(8,128)S(1)} %collective-permute-done.refs_1_) | copy-start | bytes 1572868
  19.3 35.2 %collective-permute-start.4 = (f32[8,128,128]{2,1,0:T(8,128)}, f32[8,128,128]{2,1,0:T(8,128)}, u32[]{:S(2)}, u32[]{:S(2)}) collective-permute-start(f32[8,128,128]{2,1,0:T(8,128)} %get-tuple-element.112), channel_id=1, source_target_pairs={{0,4},{2,6},{4,0},{6,2},{1,5},{3,7},{5,1},{7,3},{8,12},{10,14},{12... | collective-permute-start | bytes 1572872 | tf_op jit(solution)/shard_map/ppermute | solution.py:19
  32.0 4.0 %copy-start.3 = (f32[8,128,128]{2,1,0:T(8,128)}, f32[8,128,128]{2,1,0:T(8,128)S(1)}, u32[]{:S(2)}) copy-start(f32[8,128,128]{2,1,0:T(8,128)S(1)} %collective-permute-done.1.refs_2_) | copy-start | bytes 1572868
  32.0 23.5 %collective-permute-start.5 = (f32[8,128,128]{2,1,0:T(8,128)}, f32[8,128,128]{2,1,0:T(8,128)}, u32[]{:S(2)}, u32[]{:S(2)}) collective-permute-start(f32[8,128,128]{2,1,0:T(8,128)} %get-tuple-element.113), channel_id=1, source_target_pairs={{0,6},{2,4},{4,2},{6,0},{1,7},{3,5},{5,3},{7,1},{8,14},{10,12},{12... | collective-permute-start | bytes 1572872 | tf_op jit(solution)/shard_map/ppermute | solution.py:19
  36.8 30.0 %collective-permute-start.15 = (f32[8,128,128]{2,1,0:T(8,128)}, f32[8,128,128]{2,1,0:T(8,128)S(1)}, u32[]{:S(2)}, u32[]{:S(2)}) collective-permute-start(f32[8,128,128]{2,1,0:T(8,128)} %get-tuple-element.135), channel_id=1, source_target_pairs={{0,2},{2,0},{4,6},{6,4},{1,3},{3,1},{5,7},{7,5},{8,10},{10,8},{12,... | collective-permute-start | bytes 1572872 | tf_op jit(solution)/shard_map/ppermute | solution.py:19
  41.8 33.7 %collective-permute-start.6 = (f32[8,128,128]{2,1,0:T(8,128)}, f32[8,128,128]{2,1,0:T(8,128)S(1)}, u32[]{:S(2)}, u32[]{:S(2)}) collective-permute-start(f32[8,128,128]{2,1,0:T(8,128)} %get-tuple-element.116), channel_id=1, source_target_pairs={{0,4},{2,6},{4,0},{6,2},{1,5},{3,7},{5,1},{7,3},{8,12},{10,14},{12... | collective-permute-start | bytes 1572872 | tf_op jit(solution)/shard_map/ppermute | solution.py:19
  45.9 12.6 %copy-start.2 = (f32[8,128,128]{2,1,0:T(8,128)S(1)}, f32[8,128,128]{2,1,0:T(8,128)}, u32[]{:S(2)}) copy-start(f32[8,128,128]{2,1,0:T(8,128)} %copy-done.1) | copy-start | bytes 1572868
  54.5 28.1 %collective-permute-start.10 = (f32[8,128,128]{2,1,0:T(8,128)}, f32[8,128,128]{2,1,0:T(8,128)S(1)}, u32[]{:S(2)}, u32[]{:S(2)}) collective-permute-start(f32[8,128,128]{2,1,0:T(8,128)} %get-tuple-element.127), channel_id=1, source_target_pairs={{0,6},{2,4},{4,2},{6,0},{1,7},{3,5},{5,3},{7,1},{8,14},{10,12},{12... | collective-permute-start | bytes 1572872 | tf_op jit(solution)/shard_map/ppermute | solution.py:19
  55.5 31.4 %collective-permute-start.9 = (f32[8,128,128]{2,1,0:T(8,128)S(1)}, f32[8,128,128]{2,1,0:T(8,128)S(1)}, u32[]{:S(2)}, u32[]{:S(2)}) collective-permute-start(f32[8,128,128]{2,1,0:T(8,128)S(1)} %get-tuple-element.120), channel_id=1, source_target_pairs={{0,2},{2,0},{4,6},{6,4},{1,3},{3,1},{5,7},{7,5},{8,10},{10,8},{12,... | collective-permute-start | bytes 1572872 | tf_op jit(solution)/shard_map/ppermute | solution.py:19
  58.4 1.0 copy-start.4
  59.5 1.0 copy-start.6
  63.9 11.6 %copy-start.13 = (f32[8,128,128]{2,1,0:T(8,128)S(1)}, f32[8,128,128]{2,1,0:T(8,128)}, u32[]{:S(2)}) copy-start(f32[8,128,128]{2,1,0:T(8,128)} %get-tuple-element.117) | copy-start | bytes 1572868
  63.9 13.1 %copy-start.14 = (f32[8,128,128]{2,1,0:T(8,128)S(1)}, f32[8,128,128]{2,1,0:T(8,128)}, u32[]{:S(2)}) copy-start(f32[8,128,128]{2,1,0:T(8,128)} %get-tuple-element.137) | copy-start | bytes 1572868
  75.5 29.1 %collective-permute-start.7 = (f32[8,128,128]{2,1,0:T(8,128)S(1)}, f32[8,128,128]{2,1,0:T(8,128)S(1)}, u32[]{:S(2)}, u32[]{:S(2)}) collective-permute-start(f32[8,128,128]{2,1,0:T(8,128)S(1)} %copy-done.13), channel_id=1, source_target_pairs={{0,6},{2,4},{4,2},{6,0},{1,7},{3,5},{5,3},{7,1},{8,14},{10,12},{12... | collective-permute-start | bytes 1572872 | tf_op jit(solution)/shard_map/ppermute | solution.py:19
  77.1 24.2 %collective-permute-start.16 = (f32[8,128,128]{2,1,0:T(8,128)S(1)}, f32[8,128,128]{2,1,0:T(8,128)S(1)}, u32[]{:S(2)}, u32[]{:S(2)}) collective-permute-start(f32[8,128,128]{2,1,0:T(8,128)S(1)} %copy-done.14), channel_id=1, source_target_pairs={{0,4},{2,6},{4,0},{6,2},{1,5},{3,7},{5,1},{7,3},{8,12},{10,14},{12... | collective-permute-start | bytes 1572872 | tf_op jit(solution)/shard_map/ppermute | solution.py:19
  82.6 22.6 %collective-permute-start.11 = (f32[16,16,128]{2,1,0:T(8,128)S(1)}, f32[16,16,128]{2,1,0:T(8,128)S(1)}, u32[]{:S(2)}, u32[]{:S(2)}) collective-permute-start(f32[16,16,128]{2,1,0:T(8,128)S(1)} %pad_maximum_fusion.5), channel_id=1, source_target_pairs={{0,2},{2,0},{4,6},{6,4},{1,3},{3,1},{5,7},{7,5},{8,10},{10,8},{12,... | collective-permute-start | bytes 393224 | tf_op jit(solution)/shard_map/ppermute | solution.py:19
  86.9 18.4 %collective-permute-start.13 = (f32[16,16,128]{2,1,0:T(8,128)S(1)}, f32[16,16,128]{2,1,0:T(8,128)S(1)}, u32[]{:S(2)}, u32[]{:S(2)}) collective-permute-start(f32[16,16,128]{2,1,0:T(8,128)S(1)} %pad_maximum_fusion.6), channel_id=1, source_target_pairs={{0,4},{2,6},{4,0},{6,2},{1,5},{3,7},{5,1},{7,3},{8,12},{10,14},{12... | collective-permute-start | bytes 393224 | tf_op jit(solution)/shard_map/ppermute | solution.py:19
  101.3 7.7 %collective-permute-start.17 = (f32[16,16,128]{2,1,0:T(8,128)S(1)}, f32[16,16,128]{2,1,0:T(8,128)S(1)}, u32[]{:S(2)}, u32[]{:S(2)}) collective-permute-start(f32[16,16,128]{2,1,0:T(8,128)S(1)} %pad_maximum_fusion.7), channel_id=1, source_target_pairs={{0,6},{2,4},{4,2},{6,0},{1,7},{3,5},{5,3},{7,1},{8,14},{10,12},{12... | collective-permute-start | bytes 393224 | tf_op jit(solution)/shard_map/ppermute | solution.py:19
  104.6 15.3 %collective-permute-start.8 = (f32[8,128,128]{2,1,0:T(8,128)S(1)}, f32[8,128,128]{2,1,0:T(8,128)S(1)}, u32[]{:S(2)}, u32[]{:S(2)}) collective-permute-start(f32[8,128,128]{2,1,0:T(8,128)S(1)} %get-tuple-element.118), channel_id=1, source_target_pairs={{0,2},{2,0},{4,6},{6,4},{1,3},{3,1},{5,7},{7,5},{8,10},{10,8},{12,... | collective-permute-start | bytes 1572872 | tf_op jit(solution)/shard_map/ppermute | solution.py:19
  105.2 26.6 %collective-permute-start.14 = (f32[8,128,128]{2,1,0:T(8,128)}, f32[8,128,128]{2,1,0:T(8,128)S(1)}, u32[]{:S(2)}, u32[]{:S(2)}) collective-permute-start(f32[8,128,128]{2,1,0:T(8,128)} %get-tuple-element.134), channel_id=1, source_target_pairs={{0,6},{2,4},{4,2},{6,0},{1,7},{3,5},{5,3},{7,1},{8,14},{10,12},{12... | collective-permute-start | bytes 1572872 | tf_op jit(solution)/shard_map/ppermute | solution.py:19
  107.8 21.2 %collective-permute-start.12 = (f32[8,128,128]{2,1,0:T(8,128)}, f32[8,128,128]{2,1,0:T(8,128)S(1)}, u32[]{:S(2)}, u32[]{:S(2)}) collective-permute-start(f32[8,128,128]{2,1,0:T(8,128)} %get-tuple-element.129), channel_id=1, source_target_pairs={{0,4},{2,6},{4,0},{6,2},{1,5},{3,7},{5,1},{7,3},{8,12},{10,14},{12... | collective-permute-start | bytes 1572872 | tf_op jit(solution)/shard_map/ppermute | solution.py:19
  109.9 32.2 %collective-permute-start.21 = (f32[16,32,256]{2,1,0:T(8,128)}, f32[16,32,256]{2,1,0:T(8,128)}, u32[]{:S(2)}, u32[]{:S(2)}) collective-permute-start(f32[16,32,256]{2,1,0:T(8,128)} %pad_maximum_fusion), channel_id=1, source_target_pairs={{0,1},{1,0},{2,3},{3,2},{4,5},{5,4},{6,7},{7,6},{8,9},{9,8},{10,11... | collective-permute-start | bytes 1572872 | tf_op jit(solution)/shard_map/ppermute | solution.py:19
  112.8 29.2 %collective-permute-start.22 = (f32[64,8,128]{2,1,0:T(8,128)S(1)}, f32[64,8,128]{2,1,0:T(8,128)S(1)}, u32[]{:S(2)}, u32[]{:S(2)}) collective-permute-start(f32[64,8,128]{2,1,0:T(8,128)S(1)} %get-tuple-element.155.refs_0_), channel_id=1, source_target_pairs={{0,1},{1,0},{2,3},{3,2},{4,5},{5,4},{6,7},{7,6},{8,9},{9,8},{10,11... | collective-permute-start | bytes 786440 | tf_op jit(solution)/shard_map/ppermute | solution.py:19
  119.8 26.4 %collective-permute-start.18 = (f32[8,128,128]{2,1,0:T(8,128)}, f32[8,128,128]{2,1,0:T(8,128)}, u32[]{:S(2)}, u32[]{:S(2)}) collective-permute-start(f32[8,128,128]{2,1,0:T(8,128)} %get-tuple-element.148), channel_id=1, source_target_pairs={{0,2},{2,0},{4,6},{6,4},{1,3},{3,1},{5,7},{7,5},{8,10},{10,8},{12,... | collective-permute-start | bytes 1572872 | tf_op jit(solution)/shard_map/ppermute | solution.py:19
  129.0 24.3 %collective-permute-start.19 = (f32[8,128,128]{2,1,0:T(8,128)}, f32[8,128,128]{2,1,0:T(8,128)}, u32[]{:S(2)}, u32[]{:S(2)}) collective-permute-start(f32[8,128,128]{2,1,0:T(8,128)} %get-tuple-element.150), channel_id=1, source_target_pairs={{0,4},{2,6},{4,0},{6,2},{1,5},{3,7},{5,1},{7,3},{8,12},{10,14},{12... | collective-permute-start | bytes 1572872 | tf_op jit(solution)/shard_map/ppermute | solution.py:19
  131.9 21.4 %collective-permute-start.20 = (f32[8,128,128]{2,1,0:T(8,128)}, f32[8,128,128]{2,1,0:T(8,128)}, u32[]{:S(2)}, u32[]{:S(2)}) collective-permute-start(f32[8,128,128]{2,1,0:T(8,128)} %get-tuple-element.152), channel_id=1, source_target_pairs={{0,6},{2,4},{4,2},{6,0},{1,7},{3,5},{5,3},{7,1},{8,14},{10,12},{12... | collective-permute-start | bytes 1572872 | tf_op jit(solution)/shard_map/ppermute | solution.py:19
  135.4 1.7 copy-start.9
  137.1 1.2 copy-start.10
  142.0 4.1 %collective-permute-start.23 = (f32[64,8,128]{2,1,0:T(8,128)S(1)}, f32[64,8,128]{2,1,0:T(8,128)S(1)}, u32[]{:S(2)}, u32[]{:S(2)}) collective-permute-start(f32[64,8,128]{2,1,0:T(8,128)S(1)} %get-tuple-element.156.refs_1_), channel_id=1, source_target_pairs={{0,1},{1,0},{2,3},{3,2},{4,5},{5,4},{6,7},{7,6},{8,9},{9,8},{10,11... | collective-permute-start | bytes 786440 | tf_op jit(solution)/shard_map/ppermute | solution.py:19
  142.1 4.1 %collective-permute-start.24 = (f32[64,8,128]{2,1,0:T(8,128)S(1)}, f32[64,8,128]{2,1,0:T(8,128)S(1)}, u32[]{:S(2)}, u32[]{:S(2)}) collective-permute-start(f32[64,8,128]{2,1,0:T(8,128)S(1)} %get-tuple-element.157.refs_2_), channel_id=1, source_target_pairs={{0,1},{1,0},{2,3},{3,2},{4,5},{5,4},{6,7},{7,6},{8,9},{9,8},{10,11... | collective-permute-start | bytes 786440 | tf_op jit(solution)/shard_map/ppermute | solution.py:19
  142.6 1.4 copy-start.12
  142.6 10.7 %copy-start.8 = (f32[512,512]{1,0:T(8,128)S(1)}, f32[512,512]{1,0:T(8,128)}, u32[]{:S(2)}) copy-start(f32[512,512]{1,0:T(8,128)} %copy-done.7) | copy-start | bytes 3145732
  157.7 2.4 %collective-permute-start.25 = (f32[4,64,512]{2,1,0:T(8,128)S(1)}, f32[4,64,512]{2,1,0:T(8,128)S(1)}, u32[]{:S(2)}, u32[]{:S(2)}) collective-permute-start(f32[4,64,512]{2,1,0:T(8,128)S(1)} %get-tuple-element.163), channel_id=1, source_target_pairs={{0,1},{1,0},{2,3},{3,2},{4,5},{5,4},{6,7},{7,6},{8,9},{9,8},{10,11... | collective-permute-start | bytes 1572872 | tf_op jit(solution)/shard_map/ppermute | solution.py:19
  157.7 2.3 %collective-permute-start.26 = (f32[64,8,128]{2,1,0:T(8,128)S(1)}, f32[64,8,128]{2,1,0:T(8,128)S(1)}, u32[]{:S(2)}, u32[]{:S(2)}) collective-permute-start(f32[64,8,128]{2,1,0:T(8,128)S(1)} %get-tuple-element.164.refs_3_), channel_id=1, source_target_pairs={{0,1},{1,0},{2,3},{3,2},{4,5},{5,4},{6,7},{7,6},{8,9},{9,8},{10,11... | collective-permute-start | bytes 786440 | tf_op jit(solution)/shard_map/ppermute | solution.py:19
  160.6 7.7 %collective-permute-start.29 = (f32[72,512]{1,0:T(8,128)S(1)}, f32[72,512]{1,0:T(8,128)S(1)}, u32[]{:S(2)}, u32[]{:S(2)}) collective-permute-start(f32[72,512]{1,0:T(8,128)S(1)} %get-tuple-element.171), channel_id=1, source_target_pairs={{0,6},{2,4},{4,2},{6,0},{1,7},{3,5},{5,3},{7,1},{8,14},{10,12},{12... | collective-permute-start | bytes 442376 | tf_op jit(solution)/shard_map/ppermute | solution.py:19
  161.5 8.8 %collective-permute-start.28 = (f32[72,512]{1,0:T(8,128)S(1)}, f32[72,512]{1,0:T(8,128)S(1)}, u32[]{:S(2)}, u32[]{:S(2)}) collective-permute-start(f32[72,512]{1,0:T(8,128)S(1)} %get-tuple-element.169), channel_id=1, source_target_pairs={{0,4},{2,6},{4,0},{6,2},{1,5},{3,7},{5,1},{7,3},{8,12},{10,14},{12... | collective-permute-start | bytes 442376 | tf_op jit(solution)/shard_map/ppermute | solution.py:19
  162.6 8.2 %collective-permute-start.27 = (f32[72,512]{1,0:T(8,128)S(1)}, f32[72,512]{1,0:T(8,128)S(1)}, u32[]{:S(2)}, u32[]{:S(2)}) collective-permute-start(f32[72,512]{1,0:T(8,128)S(1)} %get-tuple-element.167), channel_id=1, source_target_pairs={{0,2},{2,0},{4,6},{6,4},{1,3},{3,1},{5,7},{7,5},{8,10},{10,8},{12,... | collective-permute-start | bytes 442376 | tf_op jit(solution)/shard_map/ppermute | solution.py:19
  164.2 14.1 %collective-permute-start.33 = (f32[16,32,128]{2,1,0:T(8,128)S(1)}, f32[16,32,128]{2,1,0:T(8,128)S(1)}, u32[]{:S(2)}, u32[]{:S(2)}) collective-permute-start(f32[16,32,128]{2,1,0:T(8,128)S(1)} %pad_maximum_fusion.1), channel_id=1, source_target_pairs={{0,2},{2,0},{4,6},{6,4},{1,3},{3,1},{5,7},{7,5},{8,10},{10,8},{12,... | collective-permute-start | bytes 786440 | tf_op jit(solution)/shard_map/ppermute | solution.py:19
  170.8 5.2 %collective-permute-start.30 = (f32[72,512]{1,0:T(8,128)S(1)}, f32[72,512]{1,0:T(8,128)S(1)}, u32[]{:S(2)}, u32[]{:S(2)}) collective-permute-start(f32[72,512]{1,0:T(8,128)S(1)} %add_add_fusion), channel_id=1, source_target_pairs={{0,8},{8,0},{16,24},{24,16},{1,9},{9,1},{17,25},{25,17},{2,10},{10... | collective-permute-start | bytes 442376 | tf_op jit(solution)/shard_map/ppermute | solution.py:19
  172.1 12.6 %collective-permute-start.34 = (f32[16,32,128]{2,1,0:T(8,128)S(1)}, f32[16,32,128]{2,1,0:T(8,128)S(1)}, u32[]{:S(2)}, u32[]{:S(2)}) collective-permute-start(f32[16,32,128]{2,1,0:T(8,128)S(1)} %pad_maximum_fusion.2), channel_id=1, source_target_pairs={{0,4},{2,6},{4,0},{6,2},{1,5},{3,7},{5,1},{7,3},{8,12},{10,14},{12... | collective-permute-start | bytes 786440 | tf_op jit(solution)/shard_map/ppermute | solution.py:19
  172.8 11.9 %collective-permute-start.35 = (f32[16,32,128]{2,1,0:T(8,128)S(1)}, f32[16,32,128]{2,1,0:T(8,128)S(1)}, u32[]{:S(2)}, u32[]{:S(2)}) collective-permute-start(f32[16,32,128]{2,1,0:T(8,128)S(1)} %pad_maximum_fusion.3), channel_id=1, source_target_pairs={{0,6},{2,4},{4,2},{6,0},{1,7},{3,5},{5,3},{7,1},{8,14},{10,12},{12... | collective-permute-start | bytes 786440 | tf_op jit(solution)/shard_map/ppermute | solution.py:19
  176.1 10.0 %collective-permute-start.31 = (f32[72,512]{1,0:T(8,128)S(1)}, f32[72,512]{1,0:T(8,128)S(1)}, u32[]{:S(2)}, u32[]{:S(2)}) collective-permute-start(f32[72,512]{1,0:T(8,128)S(1)} %add.49), channel_id=1, source_target_pairs={{0,16},{8,24},{16,0},{24,8},{1,17},{9,25},{17,1},{25,9},{2,18},{10... | collective-permute-start | bytes 442376 | tf_op jit(solution)/shard_map/ppermute | solution.py:19
  186.1 1.4 collective-permute-start.32
  (3 other events, 2.7 us)

commit v4 on v3

--- a/solution.py
+++ b/solution.py
@@ -38,10 +38,9 @@
     )
 
 
-def pack_kernel(shifts, corner, snapshots, *refs):
+def pack_kernel(shifts, corner, width, turn, snapshots, *refs):
     count = len(shifts)
-    packed, (taken, taken_sem) = refs[:count], refs[count:]
-    width = taken.shape[2]
+    packed, (*taken, taken_sem) = refs[:count], refs[count:]
     me = lax.axis_index("tm")
     loads = []
     for i, k in enumerate(shifts):
@@ -51,27 +50,28 @@
             pl.ds(pl.multiple_of(load, 8), width),
             pl.ds(pl.multiple_of(lane, LANES), LANES),
         ]
-        loads.append(pltpu.make_async_copy(source, taken.at[i], taken_sem.at[i]))
+        target = taken[0].at[i] if turn else packed[i]
+        loads.append(pltpu.make_async_copy(source, target, taken_sem.at[i]))
         loads[-1].start()
     for i in range(count):
         loads[i].wait()
-        for p in range(width):
-            packed[i][p] = taken[i, :, p, :]
-
-
-def pack(snapshots, shifts, corner, width):
+        if turn:
+            for p in range(width):
+                packed[i][p] = taken[0][i, :, p, :]
+
+
+def pack(snapshots, shifts, corner, width, turn):
     rows = snapshots.shape[0]
     count = len(shifts)
     f32 = jnp.float32
+    shape = (width, rows, LANES) if turn else (rows, width, LANES)
+    scratch = [pltpu.VMEM((count, rows, width, LANES), f32)] if turn else []
     return pl.pallas_call(
-        functools.partial(pack_kernel, shifts, corner),
-        out_shape=[jax.ShapeDtypeStruct((width, rows, LANES), f32)] * count,
+        functools.partial(pack_kernel, shifts, corner, width, turn),
+        out_shape=[jax.ShapeDtypeStruct(shape, f32)] * count,
         in_specs=[pl.BlockSpec(memory_space=pl.ANY)],
         out_specs=[pl.BlockSpec(memory_space=pltpu.VMEM)] * count,
-        scratch_shapes=[
-            pltpu.VMEM((count, rows, width, LANES), f32),
-            pltpu.SemaphoreType.DMA((count,)),
-        ],
+        scratch_shapes=scratch + [pltpu.SemaphoreType.DMA((count,))],
         compiler_params=pltpu.CompilerParams(vmem_limit_bytes=53 * 2**20),
         cost_estimate=pl.CostEstimate(
             flops=0, bytes_accessed=8 * count * width * rows * LANES, transcendentals=0
@@ -85,16 +85,21 @@
         before, refs = refs[0], refs[1:]
     core, pieces, refs = refs[0], refs[1 : n + 1], refs[n + 1 :]
     if last:
-        keep, send, total, high, low = refs
+        keep, send, total, high, low, turned = refs
     else:
-        total, high, low = refs
+        total, high, low, turned = refs
     me, half = lax.axis_index("tm"), lax.axis_index("param")
     loads, rows = blocks[0].shape[:2]
     rank = core.shape[0]
     for k in range(n):
         at = pl.ds(pl.multiple_of((me ^ k) * rows, rows), rows)
+        block = blocks[k]
+        if block.shape[0] != loads:
+            block = turned
+            for p in range(loads):
+                turned[p] = blocks[k][:, p, :]
         for p in range(loads):
-            h, l = split(blocks[k][p])
+            h, l = split(block[p])
             high[at, p * LANES : (p + 1) * LANES] = h
             low[at, p * LANES : (p + 1) * LANES] = l
     h, l = high[...], low[...]
@@ -134,6 +139,7 @@
     f32 = lambda *dims: jax.ShapeDtypeStruct(dims, jnp.float32)
     shapes = [f32(rank, loads, lanes)] + [f32(rank // n, loads, lanes)] * n
     scratch = [pltpu.VMEM((steps, loads * lanes), jnp.bfloat16)] * 2
+    scratch.append(pltpu.VMEM((loads, rows, lanes), jnp.float32))
     if last:
         shapes += [f32(n, rows // 2, steps)] * 2
         scratch = [pltpu.VMEM((steps, steps), jnp.float32)] + scratch
@@ -273,7 +279,8 @@
     def shares(x, chunk, shifts):
         width = cut if chunk[0] == "load" else group
         if width % 8 == 0:
-            return pack(x, shifts, functools.partial(corner, chunk), width)
+            turn = chunk != chunks[0] or shifts == (0,)
+            return pack(x, shifts, functools.partial(corner, chunk), width, turn)
         out = []
         for k in shifts:
             load, lane = corner(chunk, me ^ k)
@@ -286,8 +293,10 @@
     def send(v, k, depth=4):
         if len(sent) >= depth:
             v = after(v, sent[-depth])
-        sent.append(swap(v, "tm", k))
-        return sent[-1]
+        out = swap(v, "tm", k)
+        if depth < 99:
+            sent.append(out)
+        return out
 
     pick = lambda v, k: lax.dynamic_index_in_dim(v, me ^ k, 0, False)
     place_of = lambda i, k: lambda me: corner(chunks[i], me ^ k)
@@ -311,8 +320,10 @@
 
     def chunk_done(i):
         nonlocal total
-        x = after(snapshots, held[i - 1][0]) if i else snapshots
-        own = shares(x, chunks[i], (0,))[0]
+        if i not in own_early:
+            x = after(snapshots, held[i - 1][0]) if i else snapshots
+            own_early[i] = shares(x, chunks[i], (0,))[0]
+        own = own_early[i]
         before, partners = total, held[i]
         last = i == len(chunks) - 1
         if last and i:
@@ -351,14 +362,20 @@
     ahead = 2
     load_sent = n_load == 0
     packs = ()
+    own_early = {}
     for i, chunk in enumerate(chunks):
         x = after(snapshots, packs, held[i - 3] if i >= 3 else ())
         packs = parts = shares(x, chunk, others)
+        if i == len(chunks) - 1:
+            for j in range(max(0, i - ahead + 1), i + 1):
+                x = after(snapshots, held[i - 2][0]) if i >= 2 else snapshots
+                own_early[j] = shares(x, chunks[j], (0,))[0]
+            parts = after(parts, own_early, () if param_part is None else param_part)
         held.append([send(v, k) for v, k in zip(parts, others)])
         if i >= ahead:
             chunk_done(i - ahead)
         if len(cores) == n_load and not load_sent and mains:
-            send_pieces(0, n_load)
+            send_pieces(0, n_load, 99)
             load_sent = True
             param_part = load_part()
     for i in range(len(chunks) - ahead, len(chunks)):

time: 189 us -> 187 us (0.989)
  starting transfers between devices: 47.9 us -> 45.5 us
    ppermute x36, starting transfers between devices: 47.9 us -> 45.5 us  [swap(): return lax.ppermute(v, axis, xor_pairs(k, lax.axis_size(axis)))]
    unnamed x30 -> x26, local copies, waits for them, and re-layouts: 5.11 us -> 3.75 us
  transfers between devices with their start and end apart: 36 -> 36, of which waited for: 19 -> 18; matrix products, arithmetic and copies ran while one was open for 2% -> 2% of each run, Pallas kernels for 22% -> 24%
where the time goes in v4:
time: 187 us; the launch traced here: 186 us
  waiting for transfers between devices  80.1 us (43%)
  Pallas kernels  50.7 us (27%)
  starting transfers between devices  45.5 us (24%)
  local copies, waits for them, and re-layouts  4.45 us (2%)
  other arithmetic  2.46 us (1%)
  matrix products  2.16 us (1%)
    ppermute x36, waiting for transfers between devices, swap(): return lax.ppermute(v, axis, xor_pairs(k, lax.axis_size(axis)))  80.1 us
    ppermute x36, starting transfers between devices, swap(): return lax.ppermute(v, axis, xor_pairs(k, lax.axis_size(axis)))  45.5 us
    pallas_call x12, Pallas kernels, pack(): pl.pallas_call(functools.partial(pack_kernel, shifts, corner, width, turn...  25.6 us
    pallas_call x6, Pallas kernels, run_chunk(): pl.pallas_call(functools.partial(chunk_kernel, n, first, last), out_shape...  22.3 us
    unnamed x26, local copies, waits for them, and re-layouts  3.75 us
  transfers between devices with their start and end apart: 36, of which 18 were waited for; matrix products, arithmetic and copies ran while one was open for 2% of the time, Pallas kernels for 24%

profile of v4, /device:TPU:0, one launch (start us, length us, event | category | flops | bytes accessed | tf_op | source)
XLA Modules:
  0.0 186.5 jit_solution(6381462673963483697)
XLA Ops:
  0.6 2.5 %shard_map.49 = (f32[128,8,128]{2,1,0:T(8,128)S(1)}, f32[128,8,128]{2,1,0:T(8,128)}, f32[128,8,128]{2,1,0:T(8,128)}) custom-call(f32[128,32,768]{2,1,0:T(8,128)} %snapshots.12), custom_call_target="tpu_custom_call" | custom-call | bytes 3145728 | tf_op jit(solution)/shard_map/pallas_call | solution.py:69
  3.1 3.0 %collective-permute-start = (f32[128,8,128]{2,1,0:T(8,128)S(1)}, f32[128,8,128]{2,1,0:T(8,128)S(1)}, u32[]{:S(2)}, u32[]{:S(2)}) collective-permute-start(f32[128,8,128]{2,1,0:T(8,128)S(1)} %get-tuple-element.96), channel_id=1, source_target_pairs={{0,2},{2,0},{4,6},{6,4},{1,3},{3,1},{5,7},{7,5},{8,10},{10,8},{12,... | collective-permute-start | bytes 1572872 | tf_op jit(solution)/shard_map/ppermute | solution.py:19
  6.1 1.5 collective-permute-start.1
  7.7 3.0 %shard_map.50 = (f32[8,128,128]{2,1,0:T(8,128)}, f32[8,128,128]{2,1,0:T(8,128)}, f32[8,128,128]{2,1,0:T(8,128)}) custom-call(f32[128,32,768]{2,1,0:T(8,128)} %snapshots.12), custom_call_target="tpu_custom_call" | custom-call | bytes 3145728 | tf_op jit(solution)/shard_map/pallas_call | solution.py:69
  10.7 2.0 %collective-permute-start.5 = (f32[8,128,128]{2,1,0:T(8,128)}, f32[8,128,128]{2,1,0:T(8,128)S(1)}, u32[]{:S(2)}, u32[]{:S(2)}) collective-permute-start(f32[8,128,128]{2,1,0:T(8,128)} %get-tuple-element.100), channel_id=1, source_target_pairs={{0,2},{2,0},{4,6},{6,4},{1,3},{3,1},{5,7},{7,5},{8,10},{10,8},{12,... | collective-permute-start | bytes 1572872 | tf_op jit(solution)/shard_map/ppermute | solution.py:19
  12.7 6.2 %collective-permute-done.refs_1_ = f32[128,8,128]{2,1,0:T(8,128)S(1)} collective-permute-done((f32[128,8,128]{2,1,0:T(8,128)S(1)}, f32[128,8,128]{2,1,0:T(8,128)S(1)}, u32[]{:S(2)}, u32[]{:S(2)}) %collective-permute-start) | collective-permute-done | bytes 524320 | tf_op jit(solution)/shard_map/ppermute | solution.py:19
  18.9 11.3 %collective-permute-done.1.refs_2_ = f32[128,8,128]{2,1,0:T(8,128)S(1)} collective-permute-done((f32[128,8,128]{2,1,0:T(8,128)}, f32[128,8,128]{2,1,0:T(8,128)S(1)}, u32[]{:S(2)}, u32[]{:S(2)}) %collective-permute-start.1) | collective-permute-done | bytes 524320 | tf_op jit(solution)/shard_map/ppermute | solution.py:19
  31.0 1.5 collective-permute-start.3
  34.6 2.9 %shard_map.51 = (f32[8,128,128]{2,1,0:T(8,128)S(1)}, f32[8,128,128]{2,1,0:T(8,128)}, f32[8,128,128]{2,1,0:T(8,128)}) custom-call(f32[128,32,768]{2,1,0:T(8,128)} %snapshots.12), custom_call_target="tpu_custom_call" | custom-call | bytes 3145728 | tf_op jit(solution)/shard_map/pallas_call | solution.py:69
  39.0 2.4 %collective-permute-done.5.refs_1_ = f32[8,128,128]{2,1,0:T(8,128)S(1)} collective-permute-done((f32[8,128,128]{2,1,0:T(8,128)}, f32[8,128,128]{2,1,0:T(8,128)S(1)}, u32[]{:S(2)}, u32[]{:S(2)}) %collective-permute-start.5) | collective-permute-done | bytes 524320 | tf_op jit(solution)/shard_map/ppermute | solution.py:19
  41.4 2.1 %collective-permute-start.13 = (f32[8,128,128]{2,1,0:T(8,128)}, f32[8,128,128]{2,1,0:T(8,128)S(1)}, u32[]{:S(2)}, u32[]{:S(2)}) collective-permute-start(f32[8,128,128]{2,1,0:T(8,128)} %get-tuple-element.126), channel_id=1, source_target_pairs={{0,4},{2,6},{4,0},{6,2},{1,5},{3,7},{5,1},{7,3},{8,12},{10,14},{12... | collective-permute-start | bytes 1572872 | tf_op jit(solution)/shard_map/ppermute | solution.py:19
  43.5 1.4 collective-permute-start.10
  47.0 4.2 %shard_map.60 = (f32[64,8,128]{2,1,0:T(8,128)}, f32[16,8,128]{2,1,0:T(8,128)S(1)}, f32[16,8,128]{2,1,0:T(8,128)S(1)}, f32[16,8,128]{2,1,0:T(8,128)S(1)}, f32[16,...) custom-call(f32[64,512]{1,0:T(8,128)S(1)} %bitcast.17, f32[8,128,128]{2,1,0:T(8,128)S(1)} %shard_map.59.refs_0_, ...), custom_call_target="tpu_custom_call" | custom-call | flops 1879048192 | bytes 4194304 | tf_op jit(solution)/shard_map/pallas_call | solution.py:149
  51.3 1.3 shard_map.58.refs_0_
  52.6 3.0 %shard_map.52 = (f32[8,128,128]{2,1,0:T(8,128)S(1)}, f32[8,128,128]{2,1,0:T(8,128)}, f32[8,128,128]{2,1,0:T(8,128)}) custom-call(f32[128,32,768]{2,1,0:T(8,128)} %snapshots.12), custom_call_target="tpu_custom_call" | custom-call | bytes 3145728 | tf_op jit(solution)/shard_map/pallas_call | solution.py:69
  55.6 1.6 collective-permute-done.6.refs_2_
  57.2 4.5 %shard_map.61 = (f32[64,8,128]{2,1,0:T(8,128)}, f32[16,8,128]{2,1,0:T(8,128)S(1)}, f32[16,8,128]{2,1,0:T(8,128)S(1)}, f32[16,8,128]{2,1,0:T(8,128)S(1)}, f32[16,...) custom-call(f32[64,512]{1,0:T(8,128)S(1)} %bitcast.18, f32[8,128,128]{2,1,0:T(8,128)S(1)} %shard_map.58.refs_0_, ...), custom_call_target="tpu_custom_call" | custom-call | flops 1879048192 | bytes 4194304 | tf_op jit(solution)/shard_map/pallas_call | solution.py:149
  61.7 3.3 %collective-permute-start.17 = (f32[16,16,128]{2,1,0:T(8,128)S(1)}, f32[16,16,128]{2,1,0:T(8,128)S(1)}, u32[]{:S(2)}, u32[]{:S(2)}) collective-permute-start(f32[16,16,128]{2,1,0:T(8,128)S(1)} %pad_maximum_fusion.7), channel_id=1, source_target_pairs={{0,6},{2,4},{4,2},{6,0},{1,7},{3,5},{5,3},{7,1},{8,14},{10,12},{12... | collective-permute-start | bytes 393224 | tf_op jit(solution)/shard_map/ppermute | solution.py:19
  65.8 1.5 collective-permute-start.16
  67.3 1.5 collective-permute-start.7
  68.9 4.0 %collective-permute-done.15 = f32[16,16,128]{2,1,0:T(8,128)S(1)} collective-permute-done((f32[16,16,128]{2,1,0:T(8,128)S(1)}, f32[16,16,128]{2,1,0:T(8,128)S(1)}, u32[]{:S(2)}, u32[]{:S(2)}) %collective-permute-start.15) | collective-permute-done | bytes 131104 | tf_op jit(solution)/shard_map/ppermute | solution.py:19
  73.9 11.2 %collective-permute-done.16 = f32[16,16,128]{2,1,0:T(8,128)S(1)} collective-permute-done((f32[16,16,128]{2,1,0:T(8,128)S(1)}, f32[16,16,128]{2,1,0:T(8,128)S(1)}, u32[]{:S(2)}, u32[]{:S(2)}) %collective-permute-start.16) | collective-permute-done | bytes 131104 | tf_op jit(solution)/shard_map/ppermute | solution.py:19
  85.2 3.9 %collective-permute-start.4 = (f32[8,128,128]{2,1,0:T(8,128)S(1)}, f32[8,128,128]{2,1,0:T(8,128)S(1)}, u32[]{:S(2)}, u32[]{:S(2)}) collective-permute-start(f32[8,128,128]{2,1,0:T(8,128)S(1)} %get-tuple-element.110), channel_id=1, source_target_pairs={{0,2},{2,0},{4,6},{6,4},{1,3},{3,1},{5,7},{7,5},{8,10},{10,8},{12,... | collective-permute-start | bytes 1572872 | tf_op jit(solution)/shard_map/ppermute | solution.py:19
  90.3 3.1 %shard_map.55 = (f32[8,128,128]{2,1,0:T(8,128)}, f32[8,128,128]{2,1,0:T(8,128)}, f32[8,128,128]{2,1,0:T(8,128)}) custom-call(f32[128,32,768]{2,1,0:T(8,128)} %snapshots.12), custom_call_target="tpu_custom_call" | custom-call | bytes 3145728 | tf_op jit(solution)/shard_map/pallas_call | solution.py:69
  93.4 1.4 collective-permute-start.8
  94.7 5.6 %collective-permute-done.4.refs_1_ = f32[8,128,128]{2,1,0:T(8,128)S(1)} collective-permute-done((f32[8,128,128]{2,1,0:T(8,128)S(1)}, f32[8,128,128]{2,1,0:T(8,128)S(1)}, u32[]{:S(2)}, u32[]{:S(2)}) %collective-permute-start.4) | collective-permute-done | bytes 524320 | tf_op jit(solution)/shard_map/ppermute | solution.py:19
  100.4 4.0 %collective-permute-start.12 = (f32[8,128,128]{2,1,0:T(8,128)}, f32[8,128,128]{2,1,0:T(8,128)}, u32[]{:S(2)}, u32[]{:S(2)}) collective-permute-start(f32[8,128,128]{2,1,0:T(8,128)} %get-tuple-element.124), channel_id=1, source_target_pairs={{0,6},{2,4},{4,2},{6,0},{1,7},{3,5},{5,3},{7,1},{8,14},{10,12},{12... | collective-permute-start | bytes 1572872 | tf_op jit(solution)/shard_map/ppermute | solution.py:19
  107.1 1.5 shard_map.54.refs_0_
  108.6 1.4 shard_map.53.refs_0_
  110.0 3.0 %shard_map.65 = (f32[8,128,128]{2,1,0:T(8,128)S(1)}, f32[8,128,128]{2,1,0:T(8,128)}, f32[8,128,128]{2,1,0:T(8,128)}) custom-call(f32[128,32,768]{2,1,0:T(8,128)} %snapshots.12), custom_call_target="tpu_custom_call" | custom-call | bytes 3145728 | tf_op jit(solution)/shard_map/pallas_call | solution.py:69
  113.0 2.7 %shard_map.62 = (f32[64,8,128]{2,1,0:T(8,128)S(1)}, f32[16,8,128]{2,1,0:T(8,128)S(1)}, f32[16,8,128]{2,1,0:T(8,128)S(1)}, f32[16,8,128]{2,1,0:T(8,128)S(1)}, f32...) custom-call(f32[64,512]{1,0:T(8,128)S(1)} %bitcast.19, f32[8,128,128]{2,1,0:T(8,128)S(1)} %shard_map.57.refs_0_, ...), custom_call_target="tpu_custom_call" | custom-call | flops 1879048192 | bytes 4194304 | tf_op jit(solution)/shard_map/pallas_call | solution.py:149
  115.9 2.2 %convolution_bitcast_fusion.rest = f32[32,64]{1,0:T(8,128)S(1)} fusion(f32[16,32,256]{2,1,0:T(8,128)} %collective-permute-done.18, f32[16,32,128]{2,1,0:T(8,128)S(1)} %copy-done.9, f32[16,32,128]{2,1,0:T(8,128)S(1)} %copy-done.11, pred[]{:T(512)S(6)} %eq.4), kind=kOutput, calls=%fused_computation.1 | convolution fusion | flops 102105088 | bytes 1056769 | tf_op jit(solution)/shard_map/rps,rqs->pq/dot_general | solution.py:360
  118.1 4.9 %collective-permute-done.8.refs_1_ = f32[8,128,128]{2,1,0:T(8,128)} collective-permute-done((f32[8,128,128]{2,1,0:T(8,128)}, f32[8,128,128]{2,1,0:T(8,128)}, u32[]{:S(2)}, u32[]{:S(2)}) %collective-permute-start.8) | collective-permute-done | bytes 524320 | tf_op jit(solution)/shard_map/ppermute | solution.py:19
  123.4 3.5 %collective-permute-start.20 = (f32[8,128,128]{2,1,0:T(8,128)}, f32[8,128,128]{2,1,0:T(8,128)S(1)}, u32[]{:S(2)}, u32[]{:S(2)}) collective-permute-start(f32[8,128,128]{2,1,0:T(8,128)} %get-tuple-element.150), channel_id=1, source_target_pairs={{0,4},{2,6},{4,0},{6,2},{1,5},{3,7},{5,1},{7,3},{8,12},{10,14},{12... | collective-permute-start | bytes 1572872 | tf_op jit(solution)/shard_map/ppermute | solution.py:19
  126.9 3.8 %shard_map.63 = (f32[64,8,128]{2,1,0:T(8,128)S(1)}, f32[16,8,128]{2,1,0:T(8,128)S(1)}, f32[16,8,128]{2,1,0:T(8,128)S(1)}, f32[16,8,128]{2,1,0:T(8,128)S(1)}, f32...) custom-call(f32[64,512]{1,0:T(8,128)S(1)} %bitcast.20, f32[8,128,128]{2,1,0:T(8,128)S(1)} %shard_map.56.refs_0_, ...), custom_call_target="tpu_custom_call" | custom-call | flops 1879048192 | bytes 4194304 | tf_op jit(solution)/shard_map/pallas_call | solution.py:149
  130.7 3.6 %collective-permute-done.12.refs_3_ = f32[8,128,128]{2,1,0:T(8,128)} collective-permute-done((f32[8,128,128]{2,1,0:T(8,128)}, f32[8,128,128]{2,1,0:T(8,128)}, u32[]{:S(2)}, u32[]{:S(2)}) %collective-permute-start.12) | collective-permute-done | bytes 524320 | tf_op jit(solution)/shard_map/ppermute | solution.py:19
  134.3 4.1 %shard_map.64 = (f32[64,8,128]{2,1,0:T(8,128)S(1)}, f32[16,8,128]{2,1,0:T(8,128)S(1)}, f32[16,8,128]{2,1,0:T(8,128)S(1)}, f32[16,8,128]{2,1,0:T(8,128)S(1)}, f32...) custom-call(f32[64,512]{1,0:T(8,128)S(1)} %bitcast.21, f32[8,128,128]{2,1,0:T(8,128)S(1)} %shard_map.54.refs_0_, ...), custom_call_target="tpu_custom_call" | custom-call | flops 1879048192 | bytes 4194304 | tf_op jit(solution)/shard_map/pallas_call | solution.py:149
  138.9 6.5 %collective-permute-done.19.refs_1_ = f32[8,128,128]{2,1,0:T(8,128)S(1)} collective-permute-done((f32[8,128,128]{2,1,0:T(8,128)S(1)}, f32[8,128,128]{2,1,0:T(8,128)S(1)}, u32[]{:S(2)}, u32[]{:S(2)}) %collective-permute-start.19) | collective-permute-done | bytes 524320 | tf_op jit(solution)/shard_map/ppermute | solution.py:19
  145.4 7.2 %collective-permute-done.21.refs_3_ = f32[8,128,128]{2,1,0:T(8,128)S(1)} collective-permute-done((f32[8,128,128]{2,1,0:T(8,128)}, f32[8,128,128]{2,1,0:T(8,128)S(1)}, u32[]{:S(2)}, u32[]{:S(2)}) %collective-permute-start.21) | collective-permute-done | bytes 524320 | tf_op jit(solution)/shard_map/ppermute | solution.py:19
  152.6 3.0 %shard_map.66 = (f32[64,8,128]{2,1,0:T(8,128)S(1)}, f32[16,8,128]{2,1,0:T(8,128)S(1)}, f32[16,8,128]{2,1,0:T(8,128)S(1)}, f32[16,8,128]{2,1,0:T(8,128)S(1)}, f32...) custom-call(f32[64,512]{1,0:T(8,128)S(1)} %bitcast.22, ...), custom_call_target="tpu_custom_call" | custom-call | flops 1879048192 | bytes 4194304 | tf_op jit(solution)/shard_map/pallas_call | solution.py:149
  158.6 3.0 %collective-permute-start.29 = (f32[72,512]{1,0:T(8,128)S(1)}, f32[72,512]{1,0:T(8,128)S(1)}, u32[]{:S(2)}, u32[]{:S(2)}) collective-permute-start(f32[72,512]{1,0:T(8,128)S(1)} %get-tuple-element.169), channel_id=1, source_target_pairs={{0,6},{2,4},{4,2},{6,0},{1,7},{3,5},{5,3},{7,1},{8,14},{10,12},{12... | collective-permute-start | bytes 442376 | tf_op jit(solution)/shard_map/ppermute | solution.py:19
  162.2 1.5 collective-permute-start.33
  163.7 2.5 %collective-permute-done.29 = f32[72,512]{1,0:T(8,128)S(1)} collective-permute-done((f32[72,512]{1,0:T(8,128)S(1)}, f32[72,512]{1,0:T(8,128)S(1)}, u32[]{:S(2)}, u32[]{:S(2)}) %collective-permute-start.29) | collective-permute-done | bytes 147488 | tf_op jit(solution)/shard_map/ppermute | solution.py:19
  166.2 2.7 %collective-permute-done.28 = f32[72,512]{1,0:T(8,128)S(1)} collective-permute-done((f32[72,512]{1,0:T(8,128)S(1)}, f32[72,512]{1,0:T(8,128)S(1)}, u32[]{:S(2)}, u32[]{:S(2)}) %collective-permute-start.28) | collective-permute-done | bytes 147488 | tf_op jit(solution)/shard_map/ppermute | solution.py:19
  170.7 2.6 %collective-permute-start.35 = (f32[16,32,128]{2,1,0:T(8,128)S(1)}, f32[16,32,128]{2,1,0:T(8,128)S(1)}, u32[]{:S(2)}, u32[]{:S(2)}) collective-permute-start(f32[16,32,128]{2,1,0:T(8,128)S(1)} %pad_maximum_fusion.3), channel_id=1, source_target_pairs={{0,6},{2,4},{4,2},{6,0},{1,7},{3,5},{5,3},{7,1},{8,14},{10,12},{12... | collective-permute-start | bytes 786440 | tf_op jit(solution)/shard_map/ppermute | solution.py:19
  173.3 1.5 collective-permute-done.30
  174.8 1.5 collective-permute-start.31
  176.2 6.7 %collective-permute-done.34.refs_13_ = f32[16,32,128]{2,1,0:T(8,128)S(1)} collective-permute-done((f32[16,32,128]{2,1,0:T(8,128)S(1)}, f32[16,32,128]{2,1,0:T(8,128)S(1)}, u32[]{:S(2)}, u32[]{:S(2)}) %collective-permute-start.34) | collective-permute-done | bytes 262176 | tf_op jit(solution)/shard_map/ppermute | solution.py:19
  (97 shorter events, 22.2 us)
Async XLA Ops:
  0.6 36.9 %copy-start = (f32[512,64]{0,1:T(8,128)S(1)}, f32[512,64]{0,1:T(8,128)}, u32[]{:S(2)}) copy-start(f32[512,64]{0,1:T(8,128)} %param.3) | copy-start | bytes 393220
  3.1 15.8 %collective-permute-start = (f32[128,8,128]{2,1,0:T(8,128)S(1)}, f32[128,8,128]{2,1,0:T(8,128)S(1)}, u32[]{:S(2)}, u32[]{:S(2)}) collective-permute-start(f32[128,8,128]{2,1,0:T(8,128)S(1)} %get-tuple-element.96), channel_id=1, source_target_pairs={{0,2},{2,0},{4,6},{6,4},{1,3},{3,1},{5,7},{7,5},{8,10},{10,8},{12,... | collective-permute-start | bytes 1572872 | tf_op jit(solution)/shard_map/ppermute | solution.py:19
  6.1 24.1 %collective-permute-start.1 = (f32[128,8,128]{2,1,0:T(8,128)}, f32[128,8,128]{2,1,0:T(8,128)S(1)}, u32[]{:S(2)}, u32[]{:S(2)}) collective-permute-start(f32[128,8,128]{2,1,0:T(8,128)} %get-tuple-element.97), channel_id=1, source_target_pairs={{0,4},{2,6},{4,0},{6,2},{1,5},{3,7},{5,1},{7,3},{8,12},{10,14},{12... | collective-permute-start | bytes 1572872 | tf_op jit(solution)/shard_map/ppermute | solution.py:19
  7.6 30.5 %collective-permute-start.2 = (f32[128,8,128]{2,1,0:T(8,128)}, f32[128,8,128]{2,1,0:T(8,128)S(1)}, u32[]{:S(2)}, u32[]{:S(2)}) collective-permute-start(f32[128,8,128]{2,1,0:T(8,128)} %get-tuple-element.98), channel_id=1, source_target_pairs={{0,6},{2,4},{4,2},{6,0},{1,7},{3,5},{5,3},{7,1},{8,14},{10,12},{12... | collective-permute-start | bytes 1572872 | tf_op jit(solution)/shard_map/ppermute | solution.py:19
  10.7 30.7 %collective-permute-start.5 = (f32[8,128,128]{2,1,0:T(8,128)}, f32[8,128,128]{2,1,0:T(8,128)S(1)}, u32[]{:S(2)}, u32[]{:S(2)}) collective-permute-start(f32[8,128,128]{2,1,0:T(8,128)} %get-tuple-element.100), channel_id=1, source_target_pairs={{0,2},{2,0},{4,6},{6,4},{1,3},{3,1},{5,7},{7,5},{8,10},{10,8},{12,... | collective-permute-start | bytes 1572872 | tf_op jit(solution)/shard_map/ppermute | solution.py:19
  31.0 24.6 %collective-permute-start.3 = (f32[8,128,128]{2,1,0:T(8,128)}, f32[8,128,128]{2,1,0:T(8,128)S(1)}, u32[]{:S(2)}, u32[]{:S(2)}) collective-permute-start(f32[8,128,128]{2,1,0:T(8,128)} %get-tuple-element.109), channel_id=1, source_target_pairs={{0,6},{2,4},{4,2},{6,0},{1,7},{3,5},{5,3},{7,1},{8,14},{10,12},{12... | collective-permute-start | bytes 1572872 | tf_op jit(solution)/shard_map/ppermute | solution.py:19
  32.6 24.6 %collective-permute-start.6 = (f32[8,128,128]{2,1,0:T(8,128)}, f32[8,128,128]{2,1,0:T(8,128)}, u32[]{:S(2)}, u32[]{:S(2)}) collective-permute-start(f32[8,128,128]{2,1,0:T(8,128)} %get-tuple-element.114), channel_id=1, source_target_pairs={{0,4},{2,6},{4,0},{6,2},{1,5},{3,7},{5,1},{7,3},{8,12},{10,14},{12... | collective-permute-start | bytes 1572872 | tf_op jit(solution)/shard_map/ppermute | solution.py:19
  37.5 3.9 %copy-start.5 = (f32[8,128,128]{2,1,0:T(8,128)}, f32[8,128,128]{2,1,0:T(8,128)S(1)}, u32[]{:S(2)}) copy-start(f32[8,128,128]{2,1,0:T(8,128)S(1)} %get-tuple-element.122) | copy-start | bytes 1572868
  38.1 0.8 copy-start.3
  41.4 48.8 %collective-permute-start.13 = (f32[8,128,128]{2,1,0:T(8,128)}, f32[8,128,128]{2,1,0:T(8,128)S(1)}, u32[]{:S(2)}, u32[]{:S(2)}) collective-permute-start(f32[8,128,128]{2,1,0:T(8,128)} %get-tuple-element.126), channel_id=1, source_target_pairs={{0,4},{2,6},{4,0},{6,2},{1,5},{3,7},{5,1},{7,3},{8,12},{10,14},{12... | collective-permute-start | bytes 1572872 | tf_op jit(solution)/shard_map/ppermute | solution.py:19
  43.5 23.9 %collective-permute-start.10 = (f32[8,128,128]{2,1,0:T(8,128)}, f32[8,128,128]{2,1,0:T(8,128)S(1)}, u32[]{:S(2)}, u32[]{:S(2)}) collective-permute-start(f32[8,128,128]{2,1,0:T(8,128)} %copy-done.5), channel_id=1, source_target_pairs={{0,2},{2,0},{4,6},{6,4},{1,3},{3,1},{5,7},{7,5},{8,10},{10,8},{12,... | collective-permute-start | bytes 1572872 | tf_op jit(solution)/shard_map/ppermute | solution.py:19
  44.9 1.0 copy-start.2
  46.0 1.0 copy-start.4
  52.6 14.7 %copy-start.12 = (f32[8,128,128]{2,1,0:T(8,128)S(1)}, f32[8,128,128]{2,1,0:T(8,128)}, u32[]{:S(2)}) copy-start(f32[8,128,128]{2,1,0:T(8,128)} %get-tuple-element.117) | copy-start | bytes 1572868
  61.7 38.7 %copy-start.6 = (f32[512,512]{1,0:T(8,128)}, f32[512,512]{1,0:T(8,128)S(1)}, u32[]{:S(2)}) copy-start(f32[512,512]{1,0:T(8,128)S(1)} %get-tuple-element.131.refs_4_) | copy-start | bytes 3145732
  61.7 27.5 %collective-permute-start.17 = (f32[16,16,128]{2,1,0:T(8,128)S(1)}, f32[16,16,128]{2,1,0:T(8,128)S(1)}, u32[]{:S(2)}, u32[]{:S(2)}) collective-permute-start(f32[16,16,128]{2,1,0:T(8,128)S(1)} %pad_maximum_fusion.7), channel_id=1, source_target_pairs={{0,6},{2,4},{4,2},{6,0},{1,7},{3,5},{5,3},{7,1},{8,14},{10,12},{12... | collective-permute-start | bytes 393224 | tf_op jit(solution)/shard_map/ppermute | solution.py:19
  65.0 7.9 %collective-permute-start.15 = (f32[16,16,128]{2,1,0:T(8,128)S(1)}, f32[16,16,128]{2,1,0:T(8,128)S(1)}, u32[]{:S(2)}, u32[]{:S(2)}) collective-permute-start(f32[16,16,128]{2,1,0:T(8,128)S(1)} %pad_maximum_fusion.5), channel_id=1, source_target_pairs={{0,2},{2,0},{4,6},{6,4},{1,3},{3,1},{5,7},{7,5},{8,10},{10,8},{12,... | collective-permute-start | bytes 393224 | tf_op jit(solution)/shard_map/ppermute | solution.py:19
  65.8 19.4 %collective-permute-start.16 = (f32[16,16,128]{2,1,0:T(8,128)S(1)}, f32[16,16,128]{2,1,0:T(8,128)S(1)}, u32[]{:S(2)}, u32[]{:S(2)}) collective-permute-start(f32[16,16,128]{2,1,0:T(8,128)S(1)} %pad_maximum_fusion.6), channel_id=1, source_target_pairs={{0,4},{2,6},{4,0},{6,2},{1,5},{3,7},{5,1},{7,3},{8,12},{10,14},{12... | collective-permute-start | bytes 393224 | tf_op jit(solution)/shard_map/ppermute | solution.py:19
  67.3 26.0 %collective-permute-start.7 = (f32[8,128,128]{2,1,0:T(8,128)S(1)}, f32[8,128,128]{2,1,0:T(8,128)S(1)}, u32[]{:S(2)}, u32[]{:S(2)}) collective-permute-start(f32[8,128,128]{2,1,0:T(8,128)S(1)} %copy-done.12), channel_id=1, source_target_pairs={{0,6},{2,4},{4,2},{6,0},{1,7},{3,5},{5,3},{7,1},{8,14},{10,12},{12... | collective-permute-start | bytes 1572872 | tf_op jit(solution)/shard_map/ppermute | solution.py:19
  72.9 27.4 %collective-permute-start.11 = (f32[8,128,128]{2,1,0:T(8,128)}, f32[8,128,128]{2,1,0:T(8,128)S(1)}, u32[]{:S(2)}, u32[]{:S(2)}) collective-permute-start(f32[8,128,128]{2,1,0:T(8,128)} %get-tuple-element.123), channel_id=1, source_target_pairs={{0,4},{2,6},{4,0},{6,2},{1,5},{3,7},{5,1},{7,3},{8,12},{10,14},{12... | collective-permute-start | bytes 1572872 | tf_op jit(solution)/shard_map/ppermute | solution.py:19
  85.2 15.2 %collective-permute-start.4 = (f32[8,128,128]{2,1,0:T(8,128)S(1)}, f32[8,128,128]{2,1,0:T(8,128)S(1)}, u32[]{:S(2)}, u32[]{:S(2)}) collective-permute-start(f32[8,128,128]{2,1,0:T(8,128)S(1)} %get-tuple-element.110), channel_id=1, source_target_pairs={{0,2},{2,0},{4,6},{6,4},{1,3},{3,1},{5,7},{7,5},{8,10},{10,8},{12,... | collective-permute-start | bytes 1572872 | tf_op jit(solution)/shard_map/ppermute | solution.py:19
  89.2 1.0 copy-start.10
  89.2 11.2 %copy-start.8 = (f32[16,32,128]{2,1,0:T(8,128)}, f32[16,32,128]{2,1,0:T(8,128)S(1)}, u32[]{:S(2)}) copy-start(f32[16,32,128]{2,1,0:T(8,128)S(1)} %get-tuple-element.191) | copy-start | bytes 786436
  90.2 25.6 %collective-permute-start.18 = (f32[16,32,256]{2,1,0:T(8,128)}, f32[16,32,256]{2,1,0:T(8,128)}, u32[]{:S(2)}, u32[]{:S(2)}) collective-permute-start(f32[16,32,256]{2,1,0:T(8,128)} %pad_maximum_fusion), channel_id=1, source_target_pairs={{0,1},{1,0},{2,3},{3,2},{4,5},{5,4},{6,7},{7,6},{8,9},{9,8},{10,11... | collective-permute-start | bytes 1572872 | tf_op jit(solution)/shard_map/ppermute | solution.py:19
  90.2 27.9 %collective-permute-start.14 = (f32[8,128,128]{2,1,0:T(8,128)}, f32[8,128,128]{2,1,0:T(8,128)}, u32[]{:S(2)}, u32[]{:S(2)}) collective-permute-start(f32[8,128,128]{2,1,0:T(8,128)} %get-tuple-element.127), channel_id=1, source_target_pairs={{0,6},{2,4},{4,2},{6,0},{1,7},{3,5},{5,3},{7,1},{8,14},{10,12},{12... | collective-permute-start | bytes 1572872 | tf_op jit(solution)/shard_map/ppermute | solution.py:19
  93.4 29.6 %collective-permute-start.8 = (f32[8,128,128]{2,1,0:T(8,128)}, f32[8,128,128]{2,1,0:T(8,128)}, u32[]{:S(2)}, u32[]{:S(2)}) collective-permute-start(f32[8,128,128]{2,1,0:T(8,128)} %get-tuple-element.118), channel_id=1, source_target_pairs={{0,2},{2,0},{4,6},{6,4},{1,3},{3,1},{5,7},{7,5},{8,10},{10,8},{12,... | collective-permute-start | bytes 1572872 | tf_op jit(solution)/shard_map/ppermute | solution.py:19
  100.4 22.6 %collective-permute-start.9 = (f32[8,128,128]{2,1,0:T(8,128)}, f32[8,128,128]{2,1,0:T(8,128)}, u32[]{:S(2)}, u32[]{:S(2)}) collective-permute-start(f32[8,128,128]{2,1,0:T(8,128)} %get-tuple-element.120), channel_id=1, source_target_pairs={{0,4},{2,6},{4,0},{6,2},{1,5},{3,7},{5,1},{7,3},{8,12},{10,14},{12... | collective-permute-start | bytes 1572872 | tf_op jit(solution)/shard_map/ppermute | solution.py:19
  100.4 33.9 %collective-permute-start.12 = (f32[8,128,128]{2,1,0:T(8,128)}, f32[8,128,128]{2,1,0:T(8,128)}, u32[]{:S(2)}, u32[]{:S(2)}) collective-permute-start(f32[8,128,128]{2,1,0:T(8,128)} %get-tuple-element.124), channel_id=1, source_target_pairs={{0,6},{2,4},{4,2},{6,0},{1,7},{3,5},{5,3},{7,1},{8,14},{10,12},{12... | collective-permute-start | bytes 1572872 | tf_op jit(solution)/shard_map/ppermute | solution.py:19
  108.6 4.4 %copy-start.7 = (f32[512,512]{1,0:T(8,128)S(1)}, f32[512,512]{1,0:T(8,128)}, u32[]{:S(2)}) copy-start(f32[512,512]{1,0:T(8,128)} %copy-done.6) | copy-start | bytes 3145732
  110.0 5.8 %copy-start.9 = (f32[16,32,128]{2,1,0:T(8,128)S(1)}, f32[16,32,128]{2,1,0:T(8,128)}, u32[]{:S(2)}) copy-start(f32[16,32,128]{2,1,0:T(8,128)} %copy-done.8) | copy-start | bytes 786436
  110.0 5.8 %copy-start.11 = (f32[16,32,128]{2,1,0:T(8,128)S(1)}, f32[16,32,128]{2,1,0:T(8,128)}, u32[]{:S(2)}) copy-start(f32[16,32,128]{2,1,0:T(8,128)} %copy-done.10) | copy-start | bytes 786436
  115.8 22.6 %collective-permute-start.22 = (f32[64,8,128]{2,1,0:T(8,128)S(1)}, f32[64,8,128]{2,1,0:T(8,128)S(1)}, u32[]{:S(2)}, u32[]{:S(2)}) collective-permute-start(f32[64,8,128]{2,1,0:T(8,128)S(1)} %get-tuple-element.153.refs_0_), channel_id=1, source_target_pairs={{0,1},{1,0},{2,3},{3,2},{4,5},{5,4},{6,7},{7,6},{8,9},{9,8},{10,11... | collective-permute-start | bytes 786440 | tf_op jit(solution)/shard_map/ppermute | solution.py:19
  118.0 27.4 %collective-permute-start.19 = (f32[8,128,128]{2,1,0:T(8,128)S(1)}, f32[8,128,128]{2,1,0:T(8,128)S(1)}, u32[]{:S(2)}, u32[]{:S(2)}) collective-permute-start(f32[8,128,128]{2,1,0:T(8,128)S(1)} %get-tuple-element.148), channel_id=1, source_target_pairs={{0,2},{2,0},{4,6},{6,4},{1,3},{3,1},{5,7},{7,5},{8,10},{10,8},{12,... | collective-permute-start | bytes 1572872 | tf_op jit(solution)/shard_map/ppermute | solution.py:19
  123.0 29.6 %collective-permute-start.21 = (f32[8,128,128]{2,1,0:T(8,128)}, f32[8,128,128]{2,1,0:T(8,128)S(1)}, u32[]{:S(2)}, u32[]{:S(2)}) collective-permute-start(f32[8,128,128]{2,1,0:T(8,128)} %get-tuple-element.152), channel_id=1, source_target_pairs={{0,6},{2,4},{4,2},{6,0},{1,7},{3,5},{5,3},{7,1},{8,14},{10,12},{12... | collective-permute-start | bytes 1572872 | tf_op jit(solution)/shard_map/ppermute | solution.py:19
  123.4 29.1 %collective-permute-start.20 = (f32[8,128,128]{2,1,0:T(8,128)}, f32[8,128,128]{2,1,0:T(8,128)S(1)}, u32[]{:S(2)}, u32[]{:S(2)}) collective-permute-start(f32[8,128,128]{2,1,0:T(8,128)} %get-tuple-element.150), channel_id=1, source_target_pairs={{0,4},{2,6},{4,0},{6,2},{1,5},{3,7},{5,1},{7,3},{8,12},{10,14},{12... | collective-permute-start | bytes 1572872 | tf_op jit(solution)/shard_map/ppermute | solution.py:19
  134.3 4.7 %collective-permute-start.23 = (f32[64,8,128]{2,1,0:T(8,128)S(1)}, f32[64,8,128]{2,1,0:T(8,128)S(1)}, u32[]{:S(2)}, u32[]{:S(2)}) collective-permute-start(f32[64,8,128]{2,1,0:T(8,128)S(1)} %get-tuple-element.154.refs_1_), channel_id=1, source_target_pairs={{0,1},{1,0},{2,3},{3,2},{4,5},{5,4},{6,7},{7,6},{8,9},{9,8},{10,11... | collective-permute-start | bytes 786440 | tf_op jit(solution)/shard_map/ppermute | solution.py:19
  138.4 7.0 %collective-permute-start.24 = (f32[64,8,128]{2,1,0:T(8,128)S(1)}, f32[64,8,128]{2,1,0:T(8,128)S(1)}, u32[]{:S(2)}, u32[]{:S(2)}) collective-permute-start(f32[64,8,128]{2,1,0:T(8,128)S(1)} %get-tuple-element.155.refs_2_), channel_id=1, source_target_pairs={{0,1},{1,0},{2,3},{3,2},{4,5},{5,4},{6,7},{7,6},{8,9},{9,8},{10,11... | collective-permute-start | bytes 786440 | tf_op jit(solution)/shard_map/ppermute | solution.py:19
  155.6 2.4 %collective-permute-start.25 = (f32[4,64,512]{2,1,0:T(8,128)S(1)}, f32[4,64,512]{2,1,0:T(8,128)S(1)}, u32[]{:S(2)}, u32[]{:S(2)}) collective-permute-start(f32[4,64,512]{2,1,0:T(8,128)S(1)} %get-tuple-element.161), channel_id=1, source_target_pairs={{0,1},{1,0},{2,3},{3,2},{4,5},{5,4},{6,7},{7,6},{8,9},{9,8},{10,11... | collective-permute-start | bytes 1572872 | tf_op jit(solution)/shard_map/ppermute | solution.py:19
  155.7 2.3 %collective-permute-start.26 = (f32[64,8,128]{2,1,0:T(8,128)S(1)}, f32[64,8,128]{2,1,0:T(8,128)S(1)}, u32[]{:S(2)}, u32[]{:S(2)}) collective-permute-start(f32[64,8,128]{2,1,0:T(8,128)S(1)} %get-tuple-element.162.refs_3_), channel_id=1, source_target_pairs={{0,1},{1,0},{2,3},{3,2},{4,5},{5,4},{6,7},{7,6},{8,9},{9,8},{10,11... | collective-permute-start | bytes 786440 | tf_op jit(solution)/shard_map/ppermute | solution.py:19
  158.6 7.6 %collective-permute-start.29 = (f32[72,512]{1,0:T(8,128)S(1)}, f32[72,512]{1,0:T(8,128)S(1)}, u32[]{:S(2)}, u32[]{:S(2)}) collective-permute-start(f32[72,512]{1,0:T(8,128)S(1)} %get-tuple-element.169), channel_id=1, source_target_pairs={{0,6},{2,4},{4,2},{6,0},{1,7},{3,5},{5,3},{7,1},{8,14},{10,12},{12... | collective-permute-start | bytes 442376 | tf_op jit(solution)/shard_map/ppermute | solution.py:19
  161.6 7.3 %collective-permute-start.28 = (f32[72,512]{1,0:T(8,128)S(1)}, f32[72,512]{1,0:T(8,128)S(1)}, u32[]{:S(2)}, u32[]{:S(2)}) collective-permute-start(f32[72,512]{1,0:T(8,128)S(1)} %get-tuple-element.167), channel_id=1, source_target_pairs={{0,4},{2,6},{4,0},{6,2},{1,5},{3,7},{5,1},{7,3},{8,12},{10,14},{12... | collective-permute-start | bytes 442376 | tf_op jit(solution)/shard_map/ppermute | solution.py:19
  161.6 7.9 %collective-permute-start.27 = (f32[72,512]{1,0:T(8,128)S(1)}, f32[72,512]{1,0:T(8,128)S(1)}, u32[]{:S(2)}, u32[]{:S(2)}) collective-permute-start(f32[72,512]{1,0:T(8,128)S(1)} %get-tuple-element.165), channel_id=1, source_target_pairs={{0,2},{2,0},{4,6},{6,4},{1,3},{3,1},{5,7},{7,5},{8,10},{10,8},{12,... | collective-permute-start | bytes 442376 | tf_op jit(solution)/shard_map/ppermute | solution.py:19
  162.2 14.0 %collective-permute-start.33 = (f32[16,32,128]{2,1,0:T(8,128)S(1)}, f32[16,32,128]{2,1,0:T(8,128)S(1)}, u32[]{:S(2)}, u32[]{:S(2)}) collective-permute-start(f32[16,32,128]{2,1,0:T(8,128)S(1)} %pad_maximum_fusion.1), channel_id=1, source_target_pairs={{0,2},{2,0},{4,6},{6,4},{1,3},{3,1},{5,7},{7,5},{8,10},{10,8},{12,... | collective-permute-start | bytes 786440 | tf_op jit(solution)/shard_map/ppermute | solution.py:19
  169.5 5.3 %collective-permute-start.30 = (f32[72,512]{1,0:T(8,128)S(1)}, f32[72,512]{1,0:T(8,128)S(1)}, u32[]{:S(2)}, u32[]{:S(2)}) collective-permute-start(f32[72,512]{1,0:T(8,128)S(1)} %add_add_fusion), channel_id=1, source_target_pairs={{0,8},{8,0},{16,24},{24,16},{1,9},{9,1},{17,25},{25,17},{2,10},{10... | collective-permute-start | bytes 442376 | tf_op jit(solution)/shard_map/ppermute | solution.py:19
  170.0 12.9 %collective-permute-start.34 = (f32[16,32,128]{2,1,0:T(8,128)S(1)}, f32[16,32,128]{2,1,0:T(8,128)S(1)}, u32[]{:S(2)}, u32[]{:S(2)}) collective-permute-start(f32[16,32,128]{2,1,0:T(8,128)S(1)} %pad_maximum_fusion.2), channel_id=1, source_target_pairs={{0,4},{2,6},{4,0},{6,2},{1,5},{3,7},{5,1},{7,3},{8,12},{10,14},{12... | collective-permute-start | bytes 786440 | tf_op jit(solution)/shard_map/ppermute | solution.py:19
  170.7 12.2 %collective-permute-start.35 = (f32[16,32,128]{2,1,0:T(8,128)S(1)}, f32[16,32,128]{2,1,0:T(8,128)S(1)}, u32[]{:S(2)}, u32[]{:S(2)}) collective-permute-start(f32[16,32,128]{2,1,0:T(8,128)S(1)} %pad_maximum_fusion.3), channel_id=1, source_target_pairs={{0,6},{2,4},{4,2},{6,0},{1,7},{3,5},{5,3},{7,1},{8,14},{10,12},{12... | collective-permute-start | bytes 786440 | tf_op jit(solution)/shard_map/ppermute | solution.py:19
  174.8 9.5 %collective-permute-start.31 = (f32[72,512]{1,0:T(8,128)S(1)}, f32[72,512]{1,0:T(8,128)S(1)}, u32[]{:S(2)}, u32[]{:S(2)}) collective-permute-start(f32[72,512]{1,0:T(8,128)S(1)} %add.49), channel_id=1, source_target_pairs={{0,16},{8,24},{16,0},{24,8},{1,17},{9,25},{17,1},{25,9},{2,18},{10... | collective-permute-start | bytes 442376 | tf_op jit(solution)/shard_map/ppermute | solution.py:19
  184.3 1.4 collective-permute-start.32
  (1 other events, 0.8 us)
